TPU v7x, 256 devices: a whole 4x4x8 slice. The times are simulated.
256 devices in a mesh: section: 8 (over x_lo, y), expert: 32 (over z, x_hi, core).
Axes of the slice: x: 4 (x_hi: 2, x_lo: 2; x = x_hi * 2 + x_lo), y: 4, z: 8, core: 2. Of those that a mesh axis runs over, the one named last changes fastest.
Arguments:
- queries: bfloat16 [8192, 64, 576], P('expert', 'section'), may hold values from -64 to 64
- group_latent: bfloat16 [8192, 576], P('expert'), may hold values from -6 to 6
- cache_latent: bfloat16 [128, 32, 576], P('expert'), may hold values from -6 to 6
- unit_ids: int32 [16], replicated, may hold values from 0 to 127, as said below
- tokens_b: bfloat16 [1024, 7168], P('expert'), may hold values from -6 to 6
- expert_ids: int32 [1024, 8], P('expert'), may hold values from 0 to 31, all different within a row; in each aligned block of 32 rows (0 to 31, 32 to 63, ...) at most 10 rows name the same one
- affinity: float32 [1024, 8], P('expert'), may hold values from 0.05 to 1
- gate_w: bfloat16 [32, 7168, 1024], P('expert', None, 'section'), may hold values from -0.0625 to 0.0625
- up_w: bfloat16 [32, 7168, 1024], P('expert', None, 'section'), may hold values from -0.0625 to 0.0625
- down_w: bfloat16 [32, 1024, 7168], P('expert', 'section'), may hold values from -0.1875 to 0.1875
Outputs:
- context: bfloat16 [8192, 64, 512], P('expert', 'section')
- moe_out: bfloat16 [1024, 7168], P('expert')
Inputs may be any that keep to these rules, and one draw needn't show every extreme that they name: `expert_ids`: each row names 8 different experts; among the rows of one index of expert no expert is named more than 10 times, a bound that some block reaches. `unit_ids`: distinct unit numbers; unit u is held by index u // 4 of expert. The selected units are spread as evenly as possible over the indices of expert: none holds more than 1 of them, and some index exactly 1.
All inputs are finite; a program needn't handle non-finite values.
Results may differ from a plain program's by a relative error of at most 0.012.
Values may be sent and summed in bfloat16 or wider, within the bound.
No kernel may reach another device: no remote copies, remote signals or barrier semaphores. Data moves between devices by JAX's collectives and lax.ppermute only.
A program may use at most 128 MiB of HBM per device.

v0:
```python
import jax
import jax.numpy as jnp
from jax import lax
from jax.sharding import PartitionSpec as P

LATENT = 512


score_scale = 192.0 ** (-0.5)
route_scale = 2.5


def from_behind(value, axis, steps):
    count = lax.axis_size(axis)
    leading, last = (max(0, -steps), min(count, count - steps))
    return lax.ppermute(value, axis, [(source, source + steps) for source in range(leading, last)])


def attend(queries, group_latent, cache_latent, unit_ids):
    count = queries.shape[0]
    own_index = lax.axis_index("expert")
    previous = from_behind(group_latent, "expert", 1)
    key_rows = jnp.concatenate([previous, group_latent], 0)
    every_unit = lax.all_gather(cache_latent, "expert", axis=0, tiled=True)
    unit_rows = every_unit[unit_ids].reshape(-1, every_unit.shape[2])
    unit_live = jnp.ones((unit_rows.shape[0],), bool)
    query_pos = own_index * count + jnp.arange(count, dtype=jnp.int32)[:, None]
    key_pos = own_index * count - count + jnp.arange(2 * count, dtype=jnp.int32)[None, :]
    allowed = ((key_pos <= query_pos) & (key_pos > query_pos - count) & (key_pos >= 0))[:, None, :]
    win_s = (
        jnp.einsum("thc,kc->thk", queries, key_rows, preferred_element_type=jnp.float32)
        * score_scale
    )
    unit_s = (
        jnp.einsum("thc,kc->thk", queries, unit_rows, preferred_element_type=jnp.float32)
        * score_scale
    )
    unit_mask = unit_live[None, None, :]
    top_s = jnp.maximum(
        jnp.max(jnp.where(allowed, win_s, -1e30), -1),
        jnp.max(jnp.where(unit_mask, unit_s, -1e30), -1),
    )[..., None]
    win_p = jnp.where(allowed, jnp.exp(win_s - top_s), 0.0)
    unit_p = jnp.where(unit_mask, jnp.exp(unit_s - top_s), 0.0)
    denominator = jnp.sum(win_p, -1) + jnp.sum(unit_p, -1)
    numerator = jnp.einsum(
        "thk,kc->thc",
        win_p.astype(jnp.bfloat16),
        key_rows[:, :LATENT],
        preferred_element_type=jnp.float32,
    )
    numerator = numerator + jnp.einsum(
        "thk,kc->thc",
        unit_p.astype(jnp.bfloat16),
        unit_rows[:, :LATENT],
        preferred_element_type=jnp.float32,
    )
    return (numerator / denominator[..., None]).astype(jnp.bfloat16)


def send_back(gate_part, up_part, down_w):
    hidden = (jax.nn.silu(gate_part) * up_part).astype(jnp.bfloat16)
    expert_out = jnp.einsum(
        "scf,fd->scd", hidden, down_w[0], preferred_element_type=jnp.float32
    ).astype(jnp.bfloat16)
    return lax.all_to_all(expert_out, "expert", split_axis=0, concat_axis=0, tiled=True)


def routed(tokens_b, expert_ids, affinity, gate_w, up_w, down_w):
    n_expert = lax.axis_size("expert")
    tok_count, top_count = expert_ids.shape
    feature_width = tokens_b.shape[1]
    capacity = min(tok_count, tok_count * top_count * 5 // (4 * n_expert))
    flat_experts = expert_ids.reshape(-1)
    onehot = (flat_experts[:, None] == jnp.arange(n_expert, dtype=jnp.int32)[None, :]).astype(
        jnp.int32
    )
    slot_rank = jnp.sum((jnp.cumsum(onehot, 0) - 1) * onehot, 1)
    slot_place = flat_experts * capacity + slot_rank
    token_of = jnp.arange(tok_count * top_count, dtype=jnp.int32) // top_count
    slot_table = jnp.full((n_expert * capacity,), tok_count, jnp.int32).at[slot_place].set(token_of)
    padded_rows = jnp.concatenate([tokens_b, jnp.zeros((1, feature_width), jnp.bfloat16)], 0)
    outgoing = padded_rows[slot_table].reshape(n_expert, capacity, feature_width)
    arrived = lax.all_to_all(outgoing, "expert", split_axis=0, concat_axis=0, tiled=True)
    gate_part = jnp.einsum("scd,df->scf", arrived, gate_w[0], preferred_element_type=jnp.float32)
    up_part = jnp.einsum("scd,df->scf", arrived, up_w[0], preferred_element_type=jnp.float32)
    returned_rows = send_back(gate_part, up_part, down_w)
    slab_width = returned_rows.shape[2]
    picked = returned_rows.reshape(n_expert * capacity, slab_width)[slot_place].reshape(
        tok_count, top_count, slab_width
    )
    route_share = route_scale * affinity / jnp.sum(affinity, 1, keepdims=True)
    partial_value = jnp.einsum("tk,tkd->td", route_share, picked.astype(jnp.float32))
    return lax.psum(partial_value, "section").astype(jnp.bfloat16)


def per_device(
    queries,
    group_latent,
    cache_latent,
    unit_ids,
    tokens_b,
    expert_ids,
    affinity,
    gate_w,
    up_w,
    down_w,
):
    context = attend(queries, group_latent, cache_latent, unit_ids)
    moe_out = routed(tokens_b, expert_ids, affinity, gate_w, up_w, down_w)
    return (context, moe_out)


def solution(mesh):
    return jax.shard_map(
        per_device,
        mesh=mesh,
        in_specs=(
            P("expert", "section", None),
            P("expert", None),
            P("expert", None, None),
            P(),
            P("expert", None),
            P("expert", None),
            P("expert", None),
            P("expert", None, "section"),
            P("expert", None, "section"),
            P("expert", "section", None),
        ),
        out_specs=(P("expert", "section", None), P("expert", None)),
        check_vma=False,
    )
```

profile of v0, /device:TPU:64, one launch (start us, length us, event | category | flops | bytes accessed | tf_op | source)
XLA Modules:
  0.0 503.8 jit_solution(11899061452913195919)
XLA Ops:
  7.2 0.0 copy-start
  7.2 0.8 broadcast_multiply_fusion
  8.0 0.8 copy.33
  8.8 0.1 eq.29
  8.9 0.1 eq.25
  9.0 0.1 copy.32
  9.1 0.1 mul.57
  9.2 0.6 reduce-window.6
  9.8 0.2 slice_reduce_fusion
  10.0 0.1 fusion.49
  10.1 1.4 scatter_custom_fusion
  11.5 1.1 concatenate.7
  12.6 6.1 %gather_fusion.1 = bf16[320,7168]{1,0:T(8,128)(2,1)} fusion(bf16[33,7168]{1,0:T(8,128)(2,1)S(1)} %concatenate.7, s32[1024]{0:T(1024)S(1)} %pad_clamp_fusion.1), kind=kCustom, calls=%fused_computation.1 | custom fusion | bytes 9176320 | tf_op jit(solution)/shard_map/gather | solution.py:83
  18.7 7.8 %reshape.152 = bf16[32,10,7168]{2,1,0:T(8,128)(2,1)} reshape(bf16[320,7168]{1,0:T(8,128)(2,1)} %gather_fusion.1) | data formatting | bytes 9175040 | tf_op jit(solution)/shard_map/reshape | solution.py:83
  26.5 10.8 %all-to-all-start = ((bf16[32,10,7168]{2,1,0:T(8,128)(2,1)}), bf16[32,10,7168]{2,1,0:T(8,128)(2,1)}, u32[]{:S(2)}, u32[]{:S(2)}) async-start(bf16[32,10,7168]{2,1,0:T(8,128)(2,1)} %reshape.152), calls=%async_computation | async-start | bytes 14680064 | tf_op jit(solution)/shard_map/all_to_all | solution.py:84
  37.3 0.2 all-gather.2.cloned.1.call-start
  37.6 0.5 all-gather.2.cloned.1.call-update
  38.1 179.6 %all-to-all-done = bf16[32,10,7168]{2,1,0:T(8,128)(2,1)} async-done(((bf16[32,10,7168]{2,1,0:T(8,128)(2,1)}), bf16[32,10,7168]{2,1,0:T(8,128)(2,1)}, u32[]{:S(2)}, u32[]{:S(2)}) %all-to-all-start) | async-done | bytes 4587552 | tf_op jit(solution)/shard_map/all_to_all | solution.py:84
  217.7 6.6 %fusion.12 = f32[32,10,128]{2,0,1:T(8,128)S(1)} fusion(bf16[32,10,7168]{2,1,0:T(8,128)(2,1)} %all-to-all-done, bf16[1,7168,128]{2,1,0:T(8,128)(2,1)} %param.17), kind=kOutput, calls=%fused_computation.22 | convolution fusion | flops 587202560 | bytes 6586368 | tf_op jit(solution)/shard_map/scd,df->scf/dot_general | solution.py:85
  224.3 11.3 %convolution_convert_fusion = bf16[32,10,7168]{2,0,1:T(8,128)(2,1)} fusion(bf16[1,128,7168]{2,1,0:T(8,128)(2,1)} %param.19, bf16[1,7168,128]{2,1,0:T(8,128)(2,1)} %param.18, bf16[32,10,7168]{2,1,0:T(8,128)(2,1)} %all-to-all-done, f32[32,10,128]{2,0,1:T(8,128)S(1)} %fusion.12), kind=kOutput, calls=%fused_computation.4 | convolution fusion | flops 1176944640 | bytes 13008896 | tf_op jit(solution)/shard_map/scf,fd->scd/dot_general | solution.py:63
  235.6 8.2 %copy.38 = bf16[32,10,7168]{2,1,0:T(8,128)(2,1)} copy(bf16[32,10,7168]{2,0,1:T(8,128)(2,1)} %convolution_convert_fusion) | data formatting | bytes 9175040 | tf_op jit(solution)/shard_map/convert_element_type | solution.py:65
  243.8 0.0 copy-start.3
  243.8 0.0 copy-start.6
  243.8 0.0 copy-start.7
  243.8 7.4 %all-to-all-start.1 = ((bf16[32,10,7168]{2,1,0:T(8,128)(2,1)}), bf16[32,10,7168]{2,1,0:T(8,128)(2,1)}, u32[]{:S(2)}, u32[]{:S(2)}) async-start(bf16[32,10,7168]{2,1,0:T(8,128)(2,1)} %copy.38), calls=%async_computation.1 | async-start | bytes 14680064 | tf_op jit(solution)/shard_map/all_to_all | solution.py:66
  251.2 0.0 copy-done.3
  251.2 2.3 collective-permute-start
  253.5 0.0 copy-done.6
  253.5 0.1 copy.44
  253.7 0.0 copy-done.7
  253.7 0.2 and_and_fusion
  253.9 160.9 %collective-permute-done = bf16[256,576]{0,1:T(8,128)(2,1)S(1)} collective-permute-done((bf16[256,576]{0,1:T(8,128)(2,1)S(1)}, bf16[256,576]{0,1:T(8,128)(2,1)S(1)}, u32[]{:S(2)}, u32[]{:S(2)}) %collective-permute-start) | collective-permute-done | bytes 294944 | tf_op jit(solution)/shard_map/ppermute | solution.py:16
  414.9 0.0 copy-start.4
  414.9 0.8 copy-done.4
  415.7 0.0 copy-done
  415.7 4.0 fusion.1
  419.7 0.0 all-gather.2.cloned.1.call-done
  419.7 3.1 gather_fusion
  422.8 0.0 copy-start.2
  422.9 1.8 bitcast_reduce_fusion
  424.7 0.4 copy-done.2
  425.0 1.6 fusion.6
  426.6 0.0 copy-start.5
  426.6 1.3 fusion.15
  427.9 0.0 copy-done.5
  427.9 2.3 divide_convert_fusion
  430.2 2.5 copy.39
  432.7 0.0 all-to-all-done.1
  432.7 8.1 %reshape.153 = bf16[320,7168]{1,0:T(8,128)(2,1)} reshape(bf16[32,10,7168]{2,1,0:T(8,128)(2,1)} %all-to-all-done.1) | data formatting | bytes 9175040 | tf_op jit(solution)/shard_map/reshape | solution.py:89
  440.8 0.0 copy-start.1
  440.8 11.0 %gather_fusion.2 = bf16[256,7168]{1,0:T(8,128)(2,1)} fusion(bf16[320,7168]{1,0:T(8,128)(2,1)} %reshape.153, s32[1024]{0:T(1024)S(1)} %pad_clamp_fusion), kind=kCustom, calls=%fused_computation.2 | custom fusion | bytes 7341056 | tf_op jit(solution)/shard_map/gather | solution.py:89
  451.9 3.1 fusion.4
  455.0 0.2 copy.61
  455.2 41.8 %all-reduce.2 = bf16[32,7168]{1,0:T(8,128)(2,1)} all-reduce(f32[32,7168]{1,0:T(8,128)S(1)} %bitcast.86), channel_id=1, replica_groups=mesh['section'=8,'expert'=32] {'section'}, use_global_device_ids=true, to_apply=%region_9.10 | all-reduce | flops 229376 | bytes 1376256 | tf_op jit(solution)/shard_map/psum | solution.py:94
  496.9 0.0 copy-done.1
  (19 shorter events, 0.2 us)
Async XLA Ops:
  7.2 408.5 %copy-start = (bf16[256,8,576]{0,2,1:T(8,128)(2,1)S(1)}, bf16[256,8,576]{0,2,1:T(8,128)(2,1)}, u32[]{:S(2)}) copy-start(bf16[256,8,576]{0,2,1:T(8,128)(2,1)} %param.10) | copy-start | bytes 7077892
  26.5 191.2 %all-to-all-start = ((bf16[32,10,7168]{2,1,0:T(8,128)(2,1)}), bf16[32,10,7168]{2,1,0:T(8,128)(2,1)}, u32[]{:S(2)}, u32[]{:S(2)}) async-start(bf16[32,10,7168]{2,1,0:T(8,128)(2,1)} %reshape.152), calls=%async_computation | async-start | bytes 14680064 | tf_op jit(solution)/shard_map/all_to_all | solution.py:84
  37.3 382.4 %all-gather.2.cloned.1.call-start = ((), (), s32[]{:S(2)}) async-start(), calls=%async_computation.2 | async-start | bytes 5406720 | tf_op jit(solution)/shard_map/all_gather | solution.py:24
  243.8 7.4 %copy-start.3 = (bf16[256,576]{0,1:T(8,128)(2,1)S(1)}, bf16[256,576]{0,1:T(8,128)(2,1)}, u32[]{:S(2)}) copy-start(bf16[256,576]{0,1:T(8,128)(2,1)} %param.11) | copy-start | bytes 884740
  243.8 9.7 %copy-start.6 = (f32[32,8]{0,1:T(8,128)S(1)}, f32[32,8]{0,1:T(8,128)}, u32[]{:S(2)}) copy-start(f32[32,8]{0,1:T(8,128)} %param.16) | copy-start | bytes 3076
  243.8 9.9 %copy-start.7 = (s32[16]{0:T(128)S(1)}, s32[16]{0:T(128)}, u32[]{:S(2)}) copy-start(s32[16]{0:T(128)} %param.13) | copy-start | bytes 196
  243.8 188.9 %all-to-all-start.1 = ((bf16[32,10,7168]{2,1,0:T(8,128)(2,1)}), bf16[32,10,7168]{2,1,0:T(8,128)(2,1)}, u32[]{:S(2)}, u32[]{:S(2)}) async-start(bf16[32,10,7168]{2,1,0:T(8,128)(2,1)} %copy.38), calls=%async_computation.1 | async-start | bytes 14680064 | tf_op jit(solution)/shard_map/all_to_all | solution.py:66
  251.2 163.6 %collective-permute-start = (bf16[256,576]{0,1:T(8,128)(2,1)S(1)}, bf16[256,576]{0,1:T(8,128)(2,1)S(1)}, u32[]{:S(2)}, u32[]{:S(2)}) collective-permute-start(bf16[256,576]{0,1:T(8,128)(2,1)S(1)} %copy-done.3), channel_id=1, source_target_pairs={{0,1},{1,2},{2,3},{3,4},{4,5},{5,6},{6,7},{7,8},{8,9},{9,10},{10,1... | collective-permute-start | bytes 884744 | tf_op jit(solution)/shard_map/ppermute | solution.py:16
  414.9 0.8 copy-start.4
  422.8 2.2 copy-start.2
  426.6 1.3 copy-start.5
  440.8 56.1 %copy-start.1 = (bf16[256,8,576]{0,2,1:T(8,128)(2,1)S(1)}, bf16[256,8,576]{0,2,1:T(8,128)(2,1)}, u32[]{:S(2)}) copy-start(bf16[256,8,576]{0,2,1:T(8,128)(2,1)} %param.10) | copy-start | bytes 7077892
Sparse Core Ops, SparseCore 0:
  40.9 120.7 all-gather.1
where the time goes:
time: 505 us; the launch traced here: 504 us
  waiting for transfers between devices  341 us (68%)
  local copies, waits for them, and re-layouts  52.1 us (10%)
  blocking collectives  41.8 us (8%)
  matrix products  30.4 us (6%)
  starting transfers between devices  20.7 us (4%)
  between operations  14.3 us (3%)
    all_to_all x1, waiting for transfers between devices, routed(): lax.all_to_all(outgoing, 'expert', split_axis=0, concat_axis=0, tiled=True)  180 us
    ppermute x1, waiting for transfers between devices, from_behind(): lax.ppermute(value, axis, [(source, source + steps) for source in range(l...  161 us
    psum x1, blocking collectives, routed(): return lax.psum(partial_value, 'section').astype(jnp.bfloat16)  41.8 us
    dot_general x1, matrix products, send_back(): jnp.einsum('scf,fd->scd', hidden, down_w[0], preferred_element_type=jnp.f...  11.3 us
    gather x1, local copies, waits for them, and re-layouts, routed(): returned_rows.reshape(n_expert * capacity, slab_width)[slot_place]  11 us
    all_to_all x1, starting transfers between devices, routed(): lax.all_to_all(outgoing, 'expert', split_axis=0, concat_axis=0, tiled=True)  10.8 us
  transfers between devices with their start and end apart: 4, of which 2 were waited for; matrix products, arithmetic and copies ran while one was open for 9% of the time, Pallas kernels for 0%

commit v1 on v0

v1 whole, which is shorter than its diff:
```python
import jax
import jax.numpy as jnp
from jax import lax
from jax.sharding import PartitionSpec as P

LATENT = 512
N_EXPERT = 32
N_SECTION = 8
N_Y = 4
CAP = 10
LANES = 128

score_scale = 192.0 ** (-0.5)
route_scale = 2.5


def along_y(value, step):
    pairs = [
        (a * N_Y + y, a * N_Y + (y + step) % N_Y) for a in range(2) for y in range(N_Y)
    ]
    return lax.ppermute(value, "section", pairs)


def across_x(value):
    pairs = [(s, (s + N_Y) % N_SECTION) for s in range(N_SECTION)]
    return lax.ppermute(value, "section", pairs)


def spread(value):
    copies = jnp.broadcast_to(value[None], (N_SECTION,) + value.shape)
    return lax.all_to_all(copies, "section", split_axis=0, concat_axis=0, tiled=True)


def attend(queries, previous, group_latent, unit_rows):
    count = queries.shape[0]
    own_index = lax.axis_index("expert")
    key_rows = jnp.concatenate([previous, group_latent], 0)
    query_pos = own_index * count + jnp.arange(count, dtype=jnp.int32)[:, None]
    key_pos = own_index * count - count + jnp.arange(2 * count, dtype=jnp.int32)[None, :]
    allowed = ((key_pos <= query_pos) & (key_pos > query_pos - count) & (key_pos >= 0))[:, None, :]
    win_s = (
        jnp.einsum("thc,kc->thk", queries, key_rows, preferred_element_type=jnp.float32)
        * score_scale
    )
    unit_s = (
        jnp.einsum("thc,kc->thk", queries, unit_rows, preferred_element_type=jnp.float32)
        * score_scale
    )
    top_s = jnp.maximum(
        jnp.max(jnp.where(allowed, win_s, -1e30), -1), jnp.max(unit_s, -1)
    )[..., None]
    win_p = jnp.where(allowed, jnp.exp(win_s - top_s), 0.0)
    unit_p = jnp.exp(unit_s - top_s)
    denominator = jnp.sum(win_p, -1) + jnp.sum(unit_p, -1)
    numerator = jnp.einsum(
        "thk,kc->thc",
        win_p.astype(jnp.bfloat16),
        key_rows[:, :LATENT],
        preferred_element_type=jnp.float32,
    )
    numerator = numerator + jnp.einsum(
        "thk,kc->thc",
        unit_p.astype(jnp.bfloat16),
        unit_rows[:, :LATENT],
        preferred_element_type=jnp.float32,
    )
    return (numerator / denominator[..., None]).astype(jnp.bfloat16)


def per_device(
    queries,
    group_latent,
    cache_latent,
    unit_ids,
    tokens_b,
    expert_ids,
    affinity,
    gate_w,
    up_w,
    down_w,
):
    own_s = lax.axis_index("section")
    own_e = lax.axis_index("expert")
    own_x, own_y = own_s // N_Y, own_s % N_Y
    tok_count, width = tokens_b.shape
    part = width // N_SECTION
    chunks = part // LANES
    half = width // 2
    f_dev = gate_w.shape[2]

    gate_all, up_all = gate_w[0], up_w[0]
    gate_up = jnp.concatenate([gate_all, up_all], 1)
    other_half = across_x(lax.dynamic_slice_in_dim(gate_up, (1 - own_x) * half, half, 0))
    own_half = lax.dynamic_slice_in_dim(gate_up, own_x * half, half, 0)
    down_cut = down_w[0].reshape(f_dev, N_SECTION, part).transpose(1, 0, 2)
    down_all = lax.all_to_all(down_cut, "section", split_axis=0, concat_axis=0, tiled=True)
    down_all = down_all.reshape(N_SECTION * f_dev, part)

    previous = lax.ppermute(
        group_latent, "expert", [(i, i + 1) for i in range(N_EXPERT - 1)]
    )

    experts = jnp.arange(N_EXPERT, dtype=jnp.int32)
    named = jnp.any(expert_ids[:, :, None] == experts[None, None, :], 1)
    rank = jnp.cumsum(named.astype(jnp.int32), 0) - 1
    slot = jnp.where(named, rank, -CAP * chunks)
    place = jnp.arange(chunks, dtype=jnp.int32)[:, None] * CAP + slot.T[:, None, :]
    place = jnp.where(slot.T[:, None, :] < 0, -1, place).reshape(N_EXPERT, chunks * tok_count)
    rows = -(-CAP * chunks // 8) * 8
    picks = (place[:, None, :] == jnp.arange(rows, dtype=jnp.int32)[None, :, None])
    tok_part = lax.dynamic_slice_in_dim(tokens_b, own_s * part, part, 1)
    tok_stack = tok_part.reshape(tok_count, chunks, LANES).transpose(1, 0, 2)
    tok_stack = tok_stack.reshape(chunks * tok_count, LANES)
    outgoing = jnp.einsum(
        "eqk,kd->eqd",
        picks.astype(jnp.bfloat16),
        tok_stack,
        preferred_element_type=jnp.float32,
    ).astype(jnp.bfloat16)

    held = cache_latent.shape[0]
    mine = jnp.sum(jnp.where(unit_ids // held == own_e, unit_ids % held, 0))
    unit_len, qk = cache_latent.shape[1:]
    cut = unit_len // N_SECTION
    unit_cut = lax.dynamic_slice(cache_latent, (mine, own_s * cut, 0), (1, cut, qk))
    unit_cut = unit_cut.reshape(1, cut * qk // LANES, LANES)
    unit_cut = jnp.broadcast_to(unit_cut, (N_EXPERT,) + unit_cut.shape[1:])

    sent = jnp.concatenate([outgoing[:, : CAP * chunks], unit_cut], 1)
    got = lax.all_to_all(sent, "expert", split_axis=0, concat_axis=0, tiled=True)

    units = got[:, CAP * chunks :][unit_ids // held]
    units = spread(units.reshape(-1, LANES))
    unit_rows = units.reshape(-1, qk)

    x_own = got[:, : CAP * chunks].reshape(N_EXPERT, chunks, CAP, LANES).transpose(2, 0, 1, 3)
    x_own = x_own.reshape(CAP * N_EXPERT, part)
    n_rows = CAP * N_EXPERT
    first, second = x_own[: n_rows // 2], x_own[n_rows // 2 :]
    before_1 = along_y(first, 1)
    after_2 = along_y(second, -1)
    before_2 = along_y(second, 1)
    after_1 = along_y(first, -1)
    far_1 = along_y(before_1, 1)
    far_2 = along_y(after_2, -1)
    x_half = jnp.stack(
        [
            x_own,
            jnp.concatenate([before_1, before_2], 0),
            jnp.concatenate([after_1, after_2], 0),
            jnp.concatenate([far_1, far_2], 0),
        ],
        0,
    )
    order = (own_y + jnp.array([0, 3, 1, 2], jnp.int32)) % N_Y
    w_half = jnp.concatenate([own_half, other_half], 1).reshape(N_Y, part, 4 * f_dev)[order]
    sums = jnp.einsum("ymk,ykf->mf", x_half, w_half, preferred_element_type=jnp.float32)
    from_x = across_x(sums[:, 2 * f_dev :].astype(jnp.bfloat16))
    both = sums[:, : 2 * f_dev] + from_x.astype(jnp.float32)
    hidden = (jax.nn.silu(both[:, :f_dev]) * both[:, f_dev:]).astype(jnp.bfloat16)
    hidden_all = spread(hidden)

    expert_out = jnp.einsum(
        "smf,sfd->md",
        hidden_all,
        down_all.reshape(N_SECTION, f_dev, part),
        preferred_element_type=jnp.float32,
    ).astype(jnp.bfloat16)
    back = expert_out.reshape(CAP, N_EXPERT, chunks, LANES).transpose(1, 2, 0, 3)
    back = back.reshape(N_EXPERT, CAP * chunks, LANES)
    back = jnp.pad(back, ((0, 0), (0, rows - CAP * chunks), (0, 0)))
    returned = lax.all_to_all(back, "expert", split_axis=0, concat_axis=0, tiled=True)

    route_share = route_scale * affinity / jnp.sum(affinity, 1, keepdims=True)
    share_e = jnp.sum(
        jnp.where(expert_ids[:, :, None] == experts[None, None, :], route_share[:, :, None], 0.0), 1
    )
    high = share_e.astype(jnp.bfloat16)
    low = (share_e - high.astype(jnp.float32)).astype(jnp.bfloat16)
    at = place.reshape(N_EXPERT, chunks, tok_count).transpose(1, 2, 0)
    hit = at[..., None] == jnp.arange(rows, dtype=jnp.int32)
    total = jnp.zeros((chunks, tok_count, LANES), jnp.float32)
    for weight in (high, low):
        mix = jnp.where(hit, weight[None, :, :, None], jnp.bfloat16(0))
        total = total + jnp.einsum(
            "jteq,eqd->jtd", mix, returned, preferred_element_type=jnp.float32
        )
    out_part = total.astype(jnp.bfloat16).transpose(1, 0, 2).reshape(tok_count, part)
    moe_out = spread(out_part).transpose(1, 0, 2).reshape(tok_count, width)

    context = attend(queries, previous, group_latent, unit_rows)
    return (context, moe_out)


def solution(mesh):
    return jax.shard_map(
        per_device,
        mesh=mesh,
        in_specs=(
            P("expert", "section", None),
            P("expert", None),
            P("expert", None, None),
            P(),
            P("expert", None),
            P("expert", None),
            P("expert", None),
            P("expert", None, "section"),
            P("expert", None, "section"),
            P("expert", "section", None),
        ),
        out_specs=(P("expert", "section", None), P("expert", None)),
        check_vma=False,
    )
```

time: 505 us -> 185 us (0.37)
  waiting for transfers between devices: 341 us -> 46 us
  blocking collectives: 41.8 us -> 0 us
  starting transfers between devices: 20.7 us -> 48 us
  other arithmetic: 3.42 us -> 20.3 us
  local copies, waits for them, and re-layouts: 52.1 us -> 37.2 us
  between operations: 14.3 us -> 3.07 us
    all_to_all x2 -> x6, waiting for transfers between devices: 180 us -> 30 us  [the longest x3 13 us: spread(): lax.all_to_all(copies, 'section', split_axis=0, concat_axis=0, tiled=True)]
    ppermute x1 -> x9, waiting for transfers between devices: 161 us -> 16 us  [the longest x6 16 us: along_y(): return lax.ppermute(value, 'section', pairs)]
    psum x1 -> x0, blocking collectives: 41.8 us -> none  [routed(): return lax.psum(partial_value, 'section').astype(jnp.bfloat16)]
    all_to_all x2 -> x6, starting transfers between devices: 18.2 us -> 33.9 us  [the longest x3 11.2 us: spread(): lax.all_to_all(copies, 'section', split_axis=0, concat_axis=0, tiled=True)]
    gather x3 -> x2, local copies, waits for them, and re-layouts: 20.3 us -> 5.26 us  [the longest x1 4.68 us: per_device(): jnp.concatenate([own_half, other_half], 1).reshape(N_Y, part, 4 * f_dev)]
    ppermute x1 -> x9, starting transfers between devices: 2.28 us -> 14.1 us  [the longest x6 9.85 us: along_y(): return lax.ppermute(value, 'section', pairs)]
    reshape x2 -> x5, local copies, waits for them, and re-layouts: 15.9 us -> 4.25 us  [the longest x1 1.75 us: per_device(): expert_out.reshape(CAP, N_EXPERT, chunks, LANES).transpose(1, 2, 0, 3)]
    dot_general x3 -> x5, matrix products: 21 us -> 11.2 us  [the longest x2 3.68 us: per_device(): jnp.einsum('jteq,eqd->jtd', mix, returned, preferred_element_type=jnp.flo...]
  transfers between devices with their start and end apart: 4 -> 15, of which waited for: 2 -> 6; matrix products, arithmetic and copies ran while one was open for 9% -> 35% of each run, Pallas kernels for 0% -> 0%
where the time goes in v1:
time: 185 us; the launch traced here: 182 us
  starting transfers between devices  48 us (26%)
  waiting for transfers between devices  46 us (25%)
  local copies, waits for them, and re-layouts  37.2 us (20%)
  matrix products  27.1 us (15%)
  other arithmetic  20.3 us (11%)
  between operations  3.07 us (2%)
    ppermute x6, waiting for transfers between devices, along_y(): return lax.ppermute(value, 'section', pairs)  16 us
    all_to_all x3, waiting for transfers between devices, spread(): lax.all_to_all(copies, 'section', split_axis=0, concat_axis=0, tiled=True)  13 us
    unnamed x28, local copies, waits for them, and re-layouts  11.3 us
    all_to_all x3, starting transfers between devices, spread(): lax.all_to_all(copies, 'section', split_axis=0, concat_axis=0, tiled=True)  11.2 us
    all_to_all x1, starting transfers between devices, per_device(): lax.all_to_all(sent, 'expert', split_axis=0, concat_axis=0, tiled=True)  10.7 us
    all_to_all x1, waiting for transfers between devices, per_device(): lax.all_to_all(back, 'expert', split_axis=0, concat_axis=0, tiled=True)  10.5 us
    ppermute x6, starting transfers between devices, along_y(): return lax.ppermute(value, 'section', pairs)  9.85 us
    all_to_all x1, starting transfers between devices, per_device(): lax.all_to_all(back, 'expert', split_axis=0, concat_axis=0, tiled=True)  7.47 us
  transfers between devices with their start and end apart: 15, of which 6 were waited for; matrix products, arithmetic and copies ran while one was open for 35% of the time, Pallas kernels for 0%

profile of v1, /device:TPU:64, one launch (start us, length us, event | category | flops | bytes accessed | tf_op | source)
XLA Modules:
  0.0 181.6 jit_solution(14045551824039919421)
XLA Ops:
  0.7 0.8 compare_select_fusion.1
  1.5 1.3 fusion.69
  4.1 0.8 constant_dynamic-slice_fusion.1
  5.0 0.8 copy.88
  7.1 0.7 constant_dynamic-slice_fusion
  8.0 0.5 fusion.10
  8.5 1.0 pad_maximum_fusion.1
  9.5 10.7 %all-to-all-start = ((bf16[32,88,128]{2,1,0:T(8,128)(2,1)}), bf16[32,88,128]{2,1,0:T(8,128)(2,1)S(1)}, u32[]{:S(2)}, u32[]{:S(2)}) async-start(bf16[32,88,128]{2,1,0:T(8,128)(2,1)} %pad_maximum_fusion.1), calls=%async_computation | async-start | bytes 1441792 | tf_op jit(solution)/shard_map/all_to_all | solution.py:130
  20.3 4.3 %fusion.33 = (bf16[3584,256]{1,0:T(8,128)(2,1)}, bf16[3584,256]{1,0:T(8,128)(2,1)}) fusion(s32[]{:T(128)S(6)} %select_n.113, bf16[7168,128]{1,0:T(8,128)(2,1)} %bitcast.119, bf16[7168,128]{1,0:T(8,128)(2,1)} %bitcast.120, s32[]{:T(128)S(6)} %select_n.114), kind=kLoop, calls=%fused_computation.43 | loop fusion | flops 7340032 | bytes 7340040 | tf_op jit(solution)/shard_map/concatenate | solution.py:92
  24.5 0.6 collective-permute-start.7
  25.1 3.9 %copy.103 = bf16[1,128,7168]{1,2,0:T(8,128)(2,1)} copy(bf16[1,128,7168]{2,1,0:T(8,128)(2,1)} %param.20) | data formatting | bytes 3670016 | tf_op args[9]
  29.0 3.8 %copy.104 = bf16[128,8,896]{2,0,1:T(8,128)(2,1)} copy(bf16[128,8,896]{0,2,1:T(8,128)(2,1)} %bitcast.113) | data formatting | bytes 3670016 | tf_op jit(solution)/shard_map/reshape;squeeze | solution.py:95
  33.1 0.7 add_select_fusion
  33.8 0.8 and_and_fusion
  34.6 6.5 %all-to-all-done = bf16[32,88,128]{2,1,0:T(8,128)(2,1)S(1)} async-done(((bf16[32,88,128]{2,1,0:T(8,128)(2,1)}), bf16[32,88,128]{2,1,0:T(8,128)(2,1)S(1)}, u32[]{:S(2)}, u32[]{:S(2)}) %all-to-all-start) | async-done | bytes 720928 | tf_op jit(solution)/shard_map/all_to_all | solution.py:130
  41.1 4.5 %all-to-all-start.3 = ((bf16[8,128,896]{2,1,0:T(8,128)(2,1)}), bf16[8,128,896]{2,1,0:T(8,128)(2,1)}, u32[]{:S(2)}, u32[]{:S(2)}) async-start(bf16[8,128,896]{2,1,0:T(8,128)(2,1)} %bitcast.112), calls=%async_computation.3 | async-start | bytes 3670016 | tf_op jit(solution)/shard_map/all_to_all | solution.py:96
  45.9 0.8 copy.126
  46.7 3.2 %collective-permute-start.4 = (bf16[160,896]{1,0:T(8,128)(2,1)}, bf16[160,896]{1,0:T(8,128)(2,1)}, u32[]{:S(2)}, u32[]{:S(2)}) collective-permute-start(bf16[160,896]{1,0:T(8,128)(2,1)} %bitcast.107), channel_id=1, source_target_pairs={{0,96},{32,0},{64,32},{96,64},{128,224},{160,128},{192,160},{224,1... | collective-permute-start | bytes 860168 | tf_op jit(solution)/shard_map/ppermute | solution.py:21
  50.1 0.8 copy.127
  50.8 0.8 collective-permute-start.1
  51.8 2.5 %collective-permute-start.3 = (bf16[160,896]{1,0:T(8,128)(2,1)}, bf16[160,896]{1,0:T(8,128)(2,1)}, u32[]{:S(2)}, u32[]{:S(2)}) collective-permute-start(bf16[160,896]{1,0:T(8,128)(2,1)} %bitcast.108), channel_id=1, source_target_pairs={{0,96},{32,0},{64,32},{96,64},{128,224},{160,128},{192,160},{224,1... | collective-permute-start | bytes 860168 | tf_op jit(solution)/shard_map/ppermute | solution.py:21
  54.3 1.2 copy.100
  55.5 2.5 %stack_reshape.3 = bf16[1,320,896]{2,1,0:T(8,128)(2,1)} reshape(bf16[10,32,7,128]{3,2,1,0:T(8,128)(2,1)} %copy.100) | data formatting | bytes 1146880 | tf_op jit(solution)/shard_map/stack;reshape | solution.py:146
  58.1 0.6 gather_fusion
  58.6 0.7 broadcast_in_dim.134
  59.3 11.5 %collective-permute-done.1 = bf16[160,896]{1,0:T(8,128)(2,1)} collective-permute-done((bf16[160,896]{1,0:T(8,128)(2,1)}, bf16[160,896]{1,0:T(8,128)(2,1)}, u32[]{:S(2)}, u32[]{:S(2)}) %collective-permute-start.1) | collective-permute-done | bytes 286752 | tf_op jit(solution)/shard_map/ppermute | solution.py:21
  70.8 1.9 %collective-permute-start = (bf16[256,576]{0,1:T(8,128)(2,1)}, bf16[256,576]{0,1:T(8,128)(2,1)}, u32[]{:S(2)}, u32[]{:S(2)}) collective-permute-start(bf16[256,576]{0,1:T(8,128)(2,1)} %param.12), channel_id=1, source_target_pairs={{0,1},{1,2},{2,3},{3,4},{4,5},{5,6},{6,7},{7,8},{8,9},{9,10},{10,1... | collective-permute-start | bytes 884744 | tf_op jit(solution)/shard_map/ppermute | solution.py:99
  72.9 3.2 %collective-permute-start.6 = (bf16[160,896]{1,0:T(8,128)(2,1)}, bf16[160,896]{1,0:T(8,128)(2,1)}, u32[]{:S(2)}, u32[]{:S(2)}) collective-permute-start(bf16[160,896]{1,0:T(8,128)(2,1)} %collective-permute-done.4), channel_id=1, source_target_pairs={{0,96},{32,0},{64,32},{96,64},{128,224},{160,128},{192,160},{224,1... | collective-permute-start | bytes 860168 | tf_op jit(solution)/shard_map/ppermute | solution.py:21
  76.1 1.1 maximum_bitcast_fusion
  77.2 1.9 %maximum_bitcast_fusion.1 = bf16[1,320,896]{2,1,0:T(8,128)(2,1)} fusion(bf16[160,896]{1,0:T(8,128)(2,1)} %collective-permute-done.4, bf16[160,896]{1,0:T(8,128)(2,1)} %collective-permute-done.3), kind=kLoop, calls=%fused_computation.68 | loop fusion | flops 1146880 | bytes 1146880 | tf_op jit(solution)/shard_map/stack | solution.py:146
  79.1 4.2 %pad_maximum_fusion = bf16[3584,512]{1,0:T(8,128)(2,1)} fusion(bf16[3584,256]{1,0:T(8,128)(2,1)} %collective-permute-done.7, bf16[3584,256]{1,0:T(8,128)(2,1)} %get-tuple-element.20), kind=kLoop, calls=%fused_computation.15 | loop fusion | flops 7340032 | bytes 7340032 | tf_op jit(solution)/shard_map/concatenate | solution.py:156
  83.3 4.7 %gather_fusion.1 = bf16[4,896,512]{2,1,0:T(8,128)(2,1)} fusion(bf16[4,896,512]{2,1,0:T(8,128)(2,1)} %bitcast.111, s32[1024]{0:T(1024)S(1)} %pad_clamp_fusion), kind=kCustom, calls=%fused_computation.1 | custom fusion | bytes 7340048 | tf_op jit(solution)/shard_map/gather | solution.py:156
  87.9 4.4 %collective-permute-done.5 = bf16[160,896]{1,0:T(8,128)(2,1)} collective-permute-done((bf16[160,896]{1,0:T(8,128)(2,1)}, bf16[160,896]{1,0:T(8,128)(2,1)}, u32[]{:S(2)}, u32[]{:S(2)}) %collective-permute-start.5) | collective-permute-done | bytes 286752 | tf_op jit(solution)/shard_map/ppermute | solution.py:21
  92.4 1.1 maximum_bitcast_fusion.2
  93.5 3.6 %fusion.37 = f32[320,512]{1,0:T(8,128)S(1)} fusion(bf16[4,896,512]{2,1,0:T(8,128)(2,1)} %gather_fusion.1, bf16[1,320,896]{2,1,0:T(8,128)(2,1)S(1)} %maximum_bitcast_fusion.2, bf16[1,320,896]{2,1,0:T(8,128)(2,1)} %maximum_bitcast_fusion.1, bf16[1,320,896]{2,1,0:T(8,128)(2,1)S(1)} %maximum_bitcast_fusion, bf16[1,320,896]{2,1,0:T(8,128)(2,1)S(1)} %copy-done.3), kind=kOutput, calls=%fused_computation.48 | convolution fusion | flops 1177845760 | bytes 6619136 | tf_op jit(solution)/shard_map/ymk,ykf->mf/dot_general | solution.py:157
  97.1 0.8 copy-done.5
  97.9 0.7 slice.80
  98.6 1.8 collective-permute-start.8
  100.4 1.8 broadcast_in_dim.135
  102.2 3.5 %all-to-all-start.1 = ((bf16[8,288,128]{2,1,0:T(8,128)(2,1)}), bf16[8,288,128]{2,1,0:T(8,128)(2,1)S(1)}, u32[]{:S(2)}, u32[]{:S(2)}) async-start(bf16[8,288,128]{2,1,0:T(8,128)(2,1)} %broadcast_in_dim.135), calls=%async_computation.1 | async-start | bytes 1179648 | tf_op jit(solution)/shard_map/all_to_all | solution.py:31
  105.9 1.1 slice_add_fusion
  107.0 9.5 %all-to-all-done.1 = bf16[8,288,128]{2,1,0:T(8,128)(2,1)S(1)} async-done(((bf16[8,288,128]{2,1,0:T(8,128)(2,1)}), bf16[8,288,128]{2,1,0:T(8,128)(2,1)S(1)}, u32[]{:S(2)}, u32[]{:S(2)}) %all-to-all-start.1) | async-done | bytes 589856 | tf_op jit(solution)/shard_map/all_to_all | solution.py:31
  116.6 0.9 broadcast_in_dim.144
  117.5 4.2 %all-to-all-start.2 = ((bf16[8,320,128]{2,1,0:T(8,128)(2,1)}), bf16[8,320,128]{2,1,0:T(8,128)(2,1)}, u32[]{:S(2)}, u32[]{:S(2)}) async-start(bf16[8,320,128]{2,1,0:T(8,128)(2,1)} %broadcast_in_dim.144), calls=%async_computation.2 | async-start | bytes 1310720 | tf_op jit(solution)/shard_map/all_to_all | solution.py:31
  121.7 1.0 constant_dynamic-update-slice_fusion.1
  122.8 0.8 copy-done.7
  123.6 3.9 %fusion.1 = (f32[256,8]{0,1:T(8,128)S(1)}, f32[512,256,8]{1,0,2:T(8,128)}) fusion(pred[256,512]{0,1:T(8,128)(4,1)S(1)} %copy-done.4, bf16[256,8,576]{0,2,1:T(8,128)(2,1)S(1)} %copy-done, bf16[512,576]{0,1:T(8,128)(2,1)S(1)} %constant_dynamic-update-slice_fusion), kind=kOutput, calls=%fused_computation.7 | convolution fusion | flops 1211103232 | bytes 7282688 | tf_op jit(solution)/shard_map/thc,kc->thk/dot_general | solution.py:42
  127.5 1.4 reshape.170
  128.9 3.4 %all-to-all-done.2 = bf16[8,320,128]{2,1,0:T(8,128)(2,1)} async-done(((bf16[8,320,128]{2,1,0:T(8,128)(2,1)}), bf16[8,320,128]{2,1,0:T(8,128)(2,1)}, u32[]{:S(2)}, u32[]{:S(2)}) %all-to-all-start.2) | async-done | bytes 655392 | tf_op jit(solution)/shard_map/all_to_all | solution.py:31
  132.3 3.4 %fusion.36 = bf16[320,896]{1,0:T(8,128)(2,1)} fusion(bf16[8,320,128]{2,1,0:T(8,128)(2,1)} %all-to-all-done.2, bf16[8,128,896]{2,1,0:T(8,128)(2,1)} %all-to-all-done.3), kind=kOutput, calls=%fused_computation.47 | convolution fusion | flops 587489280 | bytes 3063808 | tf_op jit(solution)/shard_map/smf,sfd->md/dot_general | solution.py:163
  135.7 1.8 reshape.173
  137.8 0.9 pad.4
  138.7 7.5 %all-to-all-start.4 = ((bf16[32,72,128]{2,1,0:T(8,128)(2,1)}), bf16[32,72,128]{2,1,0:T(8,128)(2,1)S(1)}, u32[]{:S(2)}, u32[]{:S(2)}) async-start(bf16[32,72,128]{2,1,0:T(8,128)(2,1)} %pad.4), calls=%async_computation.4 | async-start | bytes 1179648 | tf_op jit(solution)/shard_map/all_to_all | solution.py:172
  146.2 3.0 %bitcast_reduce_fusion = (f32[256,8]{0,1:T(8,128)S(1)}, f32[512,256,8]{1,0,2:T(8,128)S(1)}) fusion(bf16[256,8,576]{0,2,1:T(8,128)(2,1)S(1)} %copy-done, bf16[512,576]{1,0:T(8,128)(2,1)} %reshape.170), kind=kOutput, calls=%fused_computation.3 | convolution fusion | flops 1210054656 | bytes 7151616 | tf_op jit(solution)/shard_map/thc,kc->thk/dot_general | solution.py:46
  149.3 1.6 fusion.6
  150.8 3.3 %fusion.20 = f32[256,8,512]{2,0,1:T(8,128)} fusion(f32[512,256,8]{1,0,2:T(8,128)S(1)} %get-tuple-element.27, f32[256,8]{0,1:T(8,128)S(1)} %max.7, bf16[512,576]{1,0:T(8,128)(2,1)S(1)} %copy-done.2), kind=kOutput, calls=%fused_computation.33 | convolution fusion | flops 1076887552 | bytes 8921088 | tf_op jit(solution)/shard_map/thk,kc->thc/dot_general | solution.py:61
  154.1 10.5 %all-to-all-done.4 = bf16[32,72,128]{2,1,0:T(8,128)(2,1)S(1)} async-done(((bf16[32,72,128]{2,1,0:T(8,128)(2,1)}), bf16[32,72,128]{2,1,0:T(8,128)(2,1)S(1)}, u32[]{:S(2)}, u32[]{:S(2)}) %all-to-all-start.4) | async-done | bytes 589856 | tf_op jit(solution)/shard_map/all_to_all | solution.py:172
  164.6 1.7 fusion.41
  166.3 2.0 %fusion.53 = bf16[7,4,8,128]{3,2,1,0:T(8,128)(2,1)S(1)} fusion(f32[7,32,128]{2,1,0:T(8,128)S(1)} %fusion.41, s32[7,32,32]{1,2,0:T(8,128)S(1)} %copy-done.8, bf16[32,32]{0,1:T(8,128)(2,1)S(1)} %copy.98, bf16[32,72,128]{2,1,0:T(8,128)(2,1)S(1)} %all-to-all-done.4), kind=kOutput, calls=%fused_computation.55 | convolution fusion | flops 133210112 | bytes 792576 | tf_op jit(solution)/shard_map/jteq,eqd->jtd/dot_general | solution.py:185
  168.3 0.8 broadcast_in_dim.147
  169.1 3.5 %all-to-all-start.5 = ((bf16[8,32,896]{2,1,0:T(8,128)(2,1)}), bf16[8,32,896]{2,1,0:T(8,128)(2,1)S(1)}, u32[]{:S(2)}, u32[]{:S(2)}) async-start(bf16[8,32,896]{2,1,0:T(8,128)(2,1)} %broadcast_in_dim.147), calls=%async_computation.5 | async-start | bytes 917504 | tf_op jit(solution)/shard_map/all_to_all | solution.py:31
  172.6 5.7 %divide_convert_fusion = bf16[256,8,512]{2,0,1:T(8,128)(2,1)S(1)} fusion(f32[256,8,512]{2,0,1:T(8,128)} %fusion.20, f32[512,256,8]{1,0,2:T(8,128)} %get-tuple-element.25, f32[256,8]{0,1:T(8,128)S(1)} %add.159, f32[256,8]{0,1:T(8,128)S(1)} %max.7, pred[256,512]{0,1:T(8,128)(4,1)S(1)} %copy-done.4, bf16[512,576]{0,1:T(8,128)(2,1)} %copy-done.7), kind=kOutput, calls=%fused_computation.10 | convolution fusion | flops 1081081856 | bytes 11157504 | tf_op jit(solution)/shard_map/thk,kc->thc/dot_general | solution.py:55
  178.3 2.5 %copy.110 = bf16[256,8,512]{2,1,0:T(8,128)(2,1)} copy(bf16[256,8,512]{2,0,1:T(8,128)(2,1)S(1)} %divide_convert_fusion) | data formatting | bytes 4194304
  180.8 0.8 copy.120
  (76 shorter events, 2.5 us)
Async XLA Ops:
  0.6 122.9 %copy-start = (bf16[256,8,576]{0,2,1:T(8,128)(2,1)S(1)}, bf16[256,8,576]{0,2,1:T(8,128)(2,1)}, u32[]{:S(2)}) copy-start(bf16[256,8,576]{0,2,1:T(8,128)(2,1)} %param.11) | copy-start | bytes 7077892
  9.5 31.6 %all-to-all-start = ((bf16[32,88,128]{2,1,0:T(8,128)(2,1)}), bf16[32,88,128]{2,1,0:T(8,128)(2,1)S(1)}, u32[]{:S(2)}, u32[]{:S(2)}) async-start(bf16[32,88,128]{2,1,0:T(8,128)(2,1)} %pad_maximum_fusion.1), calls=%async_computation | async-start | bytes 1441792 | tf_op jit(solution)/shard_map/all_to_all | solution.py:130
  24.5 54.6 %collective-permute-start.7 = (bf16[3584,256]{1,0:T(8,128)(2,1)}, bf16[3584,256]{1,0:T(8,128)(2,1)}, u32[]{:S(2)}, u32[]{:S(2)}) collective-permute-start(bf16[3584,256]{1,0:T(8,128)(2,1)} %get-tuple-element.21), channel_id=1, source_target_pairs={{0,128},{32,160},{64,192},{96,224},{128,0},{160,32},{192,64},{224,... | collective-permute-start | bytes 5505032 | tf_op jit(solution)/shard_map/ppermute | solution.py:26
  25.1 7.8 %copy-start.9 = (f32[32,8]{0,1:T(8,128)S(1)}, f32[32,8]{0,1:T(8,128)}, u32[]{:S(2)}) copy-start(f32[32,8]{0,1:T(8,128)} %param.17) | copy-start | bytes 3076
  25.1 7.9 %copy-start.10 = (s32[4]{0:T(128)S(1)}, s32[4]{0:T(128)}, u32[]{:S(2)}) copy-start(s32[4]{0:T(128)} %constant.114.clone) | copy-start | bytes 52
  41.1 59.3 %all-to-all-start.3 = ((bf16[8,128,896]{2,1,0:T(8,128)(2,1)}), bf16[8,128,896]{2,1,0:T(8,128)(2,1)}, u32[]{:S(2)}, u32[]{:S(2)}) async-start(bf16[8,128,896]{2,1,0:T(8,128)(2,1)} %bitcast.112), calls=%async_computation.3 | async-start | bytes 3670016 | tf_op jit(solution)/shard_map/all_to_all | solution.py:96
  46.7 26.1 %collective-permute-start.4 = (bf16[160,896]{1,0:T(8,128)(2,1)}, bf16[160,896]{1,0:T(8,128)(2,1)}, u32[]{:S(2)}, u32[]{:S(2)}) collective-permute-start(bf16[160,896]{1,0:T(8,128)(2,1)} %bitcast.107), channel_id=1, source_target_pairs={{0,96},{32,0},{64,32},{96,64},{128,224},{160,128},{192,160},{224,1... | collective-permute-start | bytes 860168 | tf_op jit(solution)/shard_map/ppermute | solution.py:21
  49.9 22.9 %collective-permute-start.2 = (bf16[160,896]{1,0:T(8,128)(2,1)}, bf16[160,896]{1,0:T(8,128)(2,1)}, u32[]{:S(2)}, u32[]{:S(2)}) collective-permute-start(bf16[160,896]{1,0:T(8,128)(2,1)} %bitcast.107), channel_id=1, source_target_pairs={{0,32},{32,64},{64,96},{96,0},{128,160},{160,192},{192,224},{224,1... | collective-permute-start | bytes 860168 | tf_op jit(solution)/shard_map/ppermute | solution.py:21
  50.8 20.0 %collective-permute-start.1 = (bf16[160,896]{1,0:T(8,128)(2,1)}, bf16[160,896]{1,0:T(8,128)(2,1)}, u32[]{:S(2)}, u32[]{:S(2)}) collective-permute-start(bf16[160,896]{1,0:T(8,128)(2,1)} %bitcast.108), channel_id=1, source_target_pairs={{0,32},{32,64},{64,96},{96,0},{128,160},{160,192},{192,224},{224,1... | collective-permute-start | bytes 860168 | tf_op jit(solution)/shard_map/ppermute | solution.py:21
  51.8 25.4 %collective-permute-start.3 = (bf16[160,896]{1,0:T(8,128)(2,1)}, bf16[160,896]{1,0:T(8,128)(2,1)}, u32[]{:S(2)}, u32[]{:S(2)}) collective-permute-start(bf16[160,896]{1,0:T(8,128)(2,1)} %bitcast.108), channel_id=1, source_target_pairs={{0,96},{32,0},{64,32},{96,64},{128,224},{160,128},{192,160},{224,1... | collective-permute-start | bytes 860168 | tf_op jit(solution)/shard_map/ppermute | solution.py:21
  70.8 50.9 %collective-permute-start = (bf16[256,576]{0,1:T(8,128)(2,1)}, bf16[256,576]{0,1:T(8,128)(2,1)}, u32[]{:S(2)}, u32[]{:S(2)}) collective-permute-start(bf16[256,576]{0,1:T(8,128)(2,1)} %param.12), channel_id=1, source_target_pairs={{0,1},{1,2},{2,3},{3,4},{4,5},{5,6},{6,7},{7,8},{8,9},{9,10},{10,1... | collective-permute-start | bytes 884744 | tf_op jit(solution)/shard_map/ppermute | solution.py:99
  72.8 19.6 %collective-permute-start.5 = (bf16[160,896]{1,0:T(8,128)(2,1)}, bf16[160,896]{1,0:T(8,128)(2,1)}, u32[]{:S(2)}, u32[]{:S(2)}) collective-permute-start(bf16[160,896]{1,0:T(8,128)(2,1)} %collective-permute-done.1), channel_id=1, source_target_pairs={{0,32},{32,64},{64,96},{96,0},{128,160},{160,192},{192,224},{224,1... | collective-permute-start | bytes 860168 | tf_op jit(solution)/shard_map/ppermute | solution.py:21
  72.9 19.5 %collective-permute-start.6 = (bf16[160,896]{1,0:T(8,128)(2,1)}, bf16[160,896]{1,0:T(8,128)(2,1)}, u32[]{:S(2)}, u32[]{:S(2)}) collective-permute-start(bf16[160,896]{1,0:T(8,128)(2,1)} %collective-permute-done.4), channel_id=1, source_target_pairs={{0,96},{32,0},{64,32},{96,64},{128,224},{160,128},{192,160},{224,1... | collective-permute-start | bytes 860168 | tf_op jit(solution)/shard_map/ppermute | solution.py:21
  83.3 10.2 %copy-start.3 = (bf16[1,320,896]{2,1,0:T(8,128)(2,1)S(1)}, bf16[1,320,896]{2,1,0:T(8,128)(2,1)}, u32[]{:S(2)}) copy-start(bf16[1,320,896]{2,1,0:T(8,128)(2,1)} %stack_reshape.3) | copy-start | bytes 1720324
  97.1 0.8 copy-start.5
  97.9 24.8 %copy-start.6 = (bf16[256,576]{0,1:T(8,128)(2,1)S(1)}, bf16[256,576]{0,1:T(8,128)(2,1)}, u32[]{:S(2)}) copy-start(bf16[256,576]{0,1:T(8,128)(2,1)} %param.12) | copy-start | bytes 884740
  97.9 25.7 %copy-start.4 = (pred[256,512]{0,1:T(8,128)(4,1)S(1)}, pred[256,512]{0,1:T(8,128)(4,1)}, u32[]{:S(2)}) copy-start(pred[256,512]{0,1:T(8,128)(4,1)} %and_and_fusion) | copy-start | bytes 393220
  98.6 7.3 %collective-permute-start.8 = (bf16[320,256]{1,0:T(8,128)(2,1)}, bf16[320,256]{1,0:T(8,128)(2,1)}, u32[]{:S(2)}, u32[]{:S(2)}) collective-permute-start(bf16[320,256]{1,0:T(8,128)(2,1)} %slice.80), channel_id=1, source_target_pairs={{0,128},{32,160},{64,192},{96,224},{128,0},{160,32},{192,64},{224,... | collective-permute-start | bytes 491528 | tf_op jit(solution)/shard_map/ppermute | solution.py:26
  102.2 14.4 %all-to-all-start.1 = ((bf16[8,288,128]{2,1,0:T(8,128)(2,1)}), bf16[8,288,128]{2,1,0:T(8,128)(2,1)S(1)}, u32[]{:S(2)}, u32[]{:S(2)}) async-start(bf16[8,288,128]{2,1,0:T(8,128)(2,1)} %broadcast_in_dim.135), calls=%async_computation.1 | async-start | bytes 1179648 | tf_op jit(solution)/shard_map/all_to_all | solution.py:31
  117.5 14.8 %all-to-all-start.2 = ((bf16[8,320,128]{2,1,0:T(8,128)(2,1)}), bf16[8,320,128]{2,1,0:T(8,128)(2,1)}, u32[]{:S(2)}, u32[]{:S(2)}) async-start(bf16[8,320,128]{2,1,0:T(8,128)(2,1)} %broadcast_in_dim.144), calls=%async_computation.2 | async-start | bytes 1310720 | tf_op jit(solution)/shard_map/all_to_all | solution.py:31
  122.8 0.8 copy-start.7
  138.7 25.9 %all-to-all-start.4 = ((bf16[32,72,128]{2,1,0:T(8,128)(2,1)}), bf16[32,72,128]{2,1,0:T(8,128)(2,1)S(1)}, u32[]{:S(2)}, u32[]{:S(2)}) async-start(bf16[32,72,128]{2,1,0:T(8,128)(2,1)} %pad.4), calls=%async_computation.4 | async-start | bytes 1179648 | tf_op jit(solution)/shard_map/all_to_all | solution.py:172
  146.2 3.1 %copy-start.1 = (f32[512,256,8]{1,0,2:T(8,128)S(1)}, f32[512,256,8]{1,0,2:T(8,128)}, u32[]{:S(2)}) copy-start(f32[512,256,8]{1,0,2:T(8,128)} %get-tuple-element.25) | copy-start | bytes 12582916
  149.2 1.6 copy-start.2
  150.8 13.8 %copy-start.8 = (s32[7,32,32]{1,2,0:T(8,128)S(1)}, s32[7,32,32]{1,2,0:T(8,128)}, u32[]{:S(2)}) copy-start(s32[7,32,32]{1,2,0:T(8,128)} %add_select_fusion) | copy-start | bytes 86020
  169.1 11.6 %all-to-all-start.5 = ((bf16[8,32,896]{2,1,0:T(8,128)(2,1)}), bf16[8,32,896]{2,1,0:T(8,128)(2,1)S(1)}, u32[]{:S(2)}, u32[]{:S(2)}) async-start(bf16[8,32,896]{2,1,0:T(8,128)(2,1)} %broadcast_in_dim.147), calls=%async_computation.5 | async-start | bytes 917504 | tf_op jit(solution)/shard_map/all_to_all | solution.py:31

commit v2 on v0

v2 whole, which is shorter than its diff:
```python
import functools

import jax
import jax.numpy as jnp
from jax import lax
from jax.experimental import pallas as pl
from jax.experimental.pallas import tpu as pltpu
from jax.sharding import PartitionSpec as P

LATENT = 512
N_EXPERT = 32
N_SECTION = 8
N_Y = 4
N_Z = 8
N_J = 4
CAP = 10
AUX = 128
AUX_AT = 640
Z_ORDER = (0, 1, 7, 2, 6, 3, 5, 4)
BLOCK = 64

score_scale = 192.0 ** (-0.5)
route_scale = 2.5

J_GROUPS = [[z * N_J + j for j in range(N_J)] for z in range(N_Z)]
Z_GROUPS = [[z * N_J + j for z in range(N_Z)] for j in range(N_J)]

VMEM = pl.BlockSpec(memory_space=pltpu.VMEM)
SMEM = pl.BlockSpec(memory_space=pltpu.SMEM)


def along_y(value, step):
    pairs = [
        (a * N_Y + y, a * N_Y + (y + step) % N_Y) for a in range(2) for y in range(N_Y)
    ]
    return lax.ppermute(value, "section", pairs)


def across_x(value):
    pairs = [(s, (s + N_Y) % N_SECTION) for s in range(N_SECTION)]
    return lax.ppermute(value, "section", pairs)


def across_section(value, bits):
    return lax.ppermute(value, "section", [(s, s ^ bits) for s in range(N_SECTION)])


def across_j(value, bit):
    return lax.ppermute(value, "expert", [(e, e ^ bit) for e in range(N_EXPERT)])


def along_z(value, steps):
    return lax.ppermute(
        value, "expert", [(e, (e + steps * N_J) % N_EXPERT) for e in range(N_EXPERT)]
    )


def over_z(value):
    return lax.all_to_all(
        value, "expert", split_axis=0, concat_axis=0, tiled=True, axis_index_groups=Z_GROUPS
    )


def over_j(value):
    return lax.all_to_all(
        value, "expert", split_axis=0, concat_axis=0, tiled=True, axis_index_groups=J_GROUPS
    )


def over_section(value):
    return lax.all_to_all(value, "section", split_axis=0, concat_axis=0, tiled=True)


def after(value, *others):
    return lax.optimization_barrier((value,) + others)[0]


def cost(flops, moved):
    return pl.CostEstimate(flops=flops, bytes_accessed=moved, transcendentals=0)


def params():
    return pltpu.CompilerParams(vmem_limit_bytes=60 * 1024 * 1024)


def prep_kernel(at_ref, unit_ref, tok_ref, ids_ref, aff_ref, cache_ref, out_ref):
    count, part = tok_ref.shape
    held, unit_len, qk = cache_ref.shape
    own_y, own_e = lax.rem(at_ref[0], N_Y), at_ref[1]
    affinity = aff_ref[...]
    high = affinity.astype(jnp.bfloat16).astype(jnp.float32)
    mid = (affinity - high).astype(jnp.bfloat16).astype(jnp.float32)
    low = affinity - high - mid
    names = jnp.concatenate([ids_ref[...].astype(jnp.float32), high, mid, low], 1)
    out_ref[0:count] = tok_ref[...]
    mine = jnp.int32(0)
    for i in range(unit_ref.shape[0]):
        unit = unit_ref[i]
        mine = mine + jnp.where(unit // held == own_e, unit % held, 0)
    extra = out_ref.shape[0] - count
    cut = unit_len // N_Y
    row = lax.broadcasted_iota(jnp.int32, (extra, unit_len), 0)
    column = lax.broadcasted_iota(jnp.int32, (extra, unit_len), 1)
    pick = jnp.where((column == own_y * cut + row) & (row < cut), 1.0, 0.0).astype(jnp.bfloat16)
    rows = jnp.dot(pick, cache_ref[mine], preferred_element_type=jnp.float32)
    names = jnp.concatenate([names, jnp.zeros((extra - 8, AUX), jnp.float32)], 0)
    rows = jnp.concatenate(
        [
            rows,
            jnp.zeros((extra, AUX_AT - qk), jnp.float32),
            names,
            jnp.zeros((extra, part - AUX_AT - AUX), jnp.float32),
        ],
        1,
    )
    out_ref[count:] = rows.astype(jnp.bfloat16)


def prep(at, unit_ids, tokens_b, expert_ids, affinity, cache_latent):
    count, width = tokens_b.shape
    part = width // N_SECTION
    rows = count + 16
    grid_spec = pltpu.PrefetchScalarGridSpec(
        num_scalar_prefetch=2,
        grid=(1,),
        in_specs=[
            pl.BlockSpec((count, part), lambda i, a, u: (0, a[0])),
            pl.BlockSpec((expert_ids.shape[1], count), lambda i, a, u: (0, 0)),
            pl.BlockSpec((expert_ids.shape[1], count), lambda i, a, u: (0, 0)),
            pl.BlockSpec(cache_latent.shape, lambda i, a, u: (0, 0, 0)),
        ],
        out_specs=pl.BlockSpec((rows, part), lambda i, a, u: (0, 0)),
    )
    return pl.pallas_call(
        prep_kernel,
        grid_spec=grid_spec,
        out_shape=jax.ShapeDtypeStruct((rows, part), jnp.bfloat16),
        compiler_params=params(),
        cost_estimate=cost(1000, 400 * 1024),
        name="prep",
    )(at, unit_ids, tokens_b, expert_ids.T, affinity.T, cache_latent)


def pack_kernel(e_ref, m_ref, c_ref, x_ref, xc_ref, slot_ref, share_ref, *out_refs):
    rows = N_Z * out_refs[0].shape[0]
    count = slot_ref.shape[1] // N_J
    refs = (m_ref, c_ref, x_ref, xc_ref)
    toks = jnp.concatenate([r[0:count, :] for r in refs], 0)
    total = toks.shape[0]
    aux = [r[count:, AUX_AT : AUX_AT + AUX].astype(jnp.float32)[0:8] for r in refs]
    ids, high, mid, low = [
        jnp.concatenate([a[:, k * count : (k + 1) * count] for a in aux], 1) for k in range(4)
    ]
    affinity = high + mid + low
    share = route_scale * affinity / jnp.sum(affinity, 0, keepdims=True)
    named, shares = [], []
    for step in range(N_Z):
        expert = lax.rem(e_ref[0] + step * N_J, N_EXPERT)
        hit = ids == expert.astype(jnp.float32)
        named.append(jnp.sum(jnp.where(hit, 1.0, 0.0), 0, keepdims=True))
        shares.append(jnp.sum(jnp.where(hit, share, 0.0), 0, keepdims=True))
    named = jnp.concatenate(named, 0)
    before = lax.broadcasted_iota(jnp.int32, (total, total), 0)
    later = lax.broadcasted_iota(jnp.int32, (total, total), 1)
    earlier = ((before // count) == (later // count)) & (before < later)
    rank = jnp.dot(
        named.astype(jnp.bfloat16),
        jnp.where(earlier, 1.0, 0.0).astype(jnp.bfloat16),
        preferred_element_type=jnp.float32,
    )
    source = lax.broadcasted_iota(jnp.int32, (N_Z, total), 1) // count
    slot = jnp.where(named > 0.5, rank + (source * CAP).astype(jnp.float32), -1.0)
    slot_ref[...] = slot
    share_ref[...] = jnp.concatenate(shares, 0)
    each = rows // N_Z
    place = lax.broadcasted_iota(jnp.int32, (N_Z, each, total), 1).astype(jnp.float32)
    pick = jnp.where(slot[:, None, :] == place, 1.0, 0.0).reshape(rows, total)
    got = jnp.dot(pick.astype(jnp.bfloat16), toks, preferred_element_type=jnp.float32)
    part = toks.shape[1]
    qk = out_refs[0].shape[1] - part
    units = [r[count:, :qk].astype(jnp.float32)[0:8] for r in refs]
    units = units + [jnp.zeros((each - N_J * 8, qk), jnp.float32)]
    units = jnp.concatenate(units, 0)
    for step, out_ref in enumerate(out_refs):
        rows = jnp.concatenate([got[step * each : (step + 1) * each], units], 1)
        out_ref[...] = rows.astype(jnp.bfloat16)


def pack(own_e, messages, part, qk):
    rows = N_J * CAP
    piece = jax.ShapeDtypeStruct((rows, part + qk), jnp.bfloat16)
    table = jax.ShapeDtypeStruct((N_Z, 128), jnp.float32)
    slot, share, *pieces = pl.pallas_call(
        pack_kernel,
        out_shape=(table,) * 2 + (piece,) * N_Z,
        in_specs=[SMEM] + [VMEM] * 4,
        out_specs=(VMEM,) * (2 + N_Z),
        compiler_params=params(),
        cost_estimate=cost(2 * N_Z * rows * 128 * part, 2 * N_Z * rows * part * 2),
        name="pack",
    )(own_e, *messages)
    return pieces, slot, share


def cut_kernel(in_ref, out_ref):
    part = out_ref.shape[2]
    for k in range(out_ref.shape[0]):
        out_ref[k] = in_ref[0, :, k * part : (k + 1) * part]


def cut_down(down_w):
    _, f, width = down_w.shape
    part = width // N_SECTION
    return pl.pallas_call(
        cut_kernel,
        out_shape=jax.ShapeDtypeStruct((N_SECTION, f, part), jnp.bfloat16),
        in_specs=[VMEM],
        out_specs=VMEM,
        compiler_params=params(),
        cost_estimate=cost(0, 2 * f * width * 2),
        name="cut_down",
    )(down_w)


def whole(shape):
    return pl.BlockSpec(shape, lambda i, s: (0,) * len(shape))


def sum_kernel(places, at_ref, *refs):
    xs, (gate, up, out_ref) = refs[:-3], refs[-3:]
    rows, part = xs[0].shape
    own_x, own_y = at_ref[0] // N_Y, lax.rem(at_ref[0], N_Y)
    total = None
    for b, (dx, dy) in enumerate(places):
        block = jnp.bitwise_xor(own_x, dx) * N_Y + lax.rem(own_y + dy, N_Y)
        k = pl.ds(pl.multiple_of(block * part, part), part)
        weights = jnp.concatenate([gate[0, k], up[0, k]], 1)
        x = jnp.concatenate([xs[2 * b][...], xs[2 * b + 1][...]], 0)
        term = jnp.dot(x, weights, preferred_element_type=jnp.float32)
        total = term if total is None else total + term
    f = out_ref.shape[2]
    gate, up = total[:, :f], total[:, f:]
    hidden = (gate / (1.0 + jnp.exp(-gate)) * up).astype(jnp.bfloat16)
    for s in range(out_ref.shape[0]):
        out_ref[s] = hidden


def add_blocks(at, blocks, gate_w, up_w):
    f = gate_w.shape[2]
    half, part = blocks[0][2][0].shape
    xs = [x for _, _, halves in blocks for x in halves]
    places = tuple((dx, dy) for dx, dy, _ in blocks)
    return pl.pallas_call(
        functools.partial(sum_kernel, places),
        out_shape=jax.ShapeDtypeStruct((N_SECTION, 2 * half, f), jnp.bfloat16),
        in_specs=[SMEM] + [VMEM] * (len(xs) + 2),
        out_specs=VMEM,
        compiler_params=params(),
        cost_estimate=cost(8 * half * part * f * len(blocks), 10 * 1024 * 1024),
        name="add_blocks",
    )(at, *xs, gate_w, up_w)


def down_kernel(e_ref, hid, w_ref, out_ref):
    total = None
    for k in range(0, N_SECTION, 2):
        left = jnp.concatenate([hid[k], hid[k + 1]], 1)
        right = jnp.concatenate([w_ref[k], w_ref[k + 1]], 0)
        term = jnp.dot(left, right, preferred_element_type=jnp.float32)
        total = term if total is None else total + term
    each = out_ref.shape[1]
    own_z = e_ref[0] // N_J
    for i, step in enumerate(Z_ORDER):
        rows = total[i * each : (i + 1) * each].astype(jnp.bfloat16)
        out_ref[lax.rem(own_z + N_Z - step, N_Z)] = rows


def down(own_e, hidden, weights):
    _, rows, f = hidden.shape
    part = weights.shape[2]
    return pl.pallas_call(
        down_kernel,
        out_shape=jax.ShapeDtypeStruct((N_Z, rows // N_Z, part), jnp.bfloat16),
        in_specs=[SMEM] + [VMEM] * 2,
        out_specs=VMEM,
        compiler_params=params(),
        cost_estimate=cost(2 * rows * f * N_SECTION * part, 4 * 1024 * 1024),
        name="down",
    )(own_e, hidden, weights)


def mix_kernel(e_ref, slot_ref, share_ref, back_ref, out_ref):
    rows = back_ref.shape[0]
    own_z, own_j = e_ref[0] // N_J, lax.rem(e_ref[0], N_J)

    def by_z(ref):
        at = [lax.rem(z + N_Z - own_z, N_Z) for z in range(N_Z)]
        return jnp.concatenate([ref[pl.ds(k, 1), :] for k in at], 0)

    each = rows // N_Z
    total = slot_ref.shape[1]
    place = lax.broadcasted_iota(jnp.int32, (N_Z, each, total), 1).astype(jnp.float32)
    weight = jnp.where(by_z(slot_ref)[:, None, :] == place, by_z(share_ref)[:, None, :], 0.0)
    weight = weight.reshape(rows, total)
    high = weight.astype(jnp.bfloat16)
    low = (weight - high.astype(jnp.float32)).astype(jnp.bfloat16)
    back = back_ref[...]
    dims = (((0,), (0,)), ((), ()))
    got = lax.dot_general(high, back, dims, preferred_element_type=jnp.float32)
    got = got + lax.dot_general(low, back, dims, preferred_element_type=jnp.float32)
    count = out_ref.shape[1]
    for p in range(N_J):
        rows = got[p * count : (p + 1) * count].astype(jnp.bfloat16)
        out_ref[jnp.bitwise_xor(own_j, p)] = rows


def mix(own_e, slot, share, back):
    rows, part = back.shape
    count = slot.shape[1] // N_J
    return pl.pallas_call(
        mix_kernel,
        out_shape=jax.ShapeDtypeStruct((N_J, count, part), jnp.bfloat16),
        in_specs=[SMEM] + [VMEM] * 3,
        out_specs=VMEM,
        compiler_params=params(),
        cost_estimate=cost(4 * rows * N_J * count * part, rows * part * 4),
        name="mix",
    )(own_e, slot, share, back)


def attend_kernel(first_step, s_ref, q_ref, prev_ref, own_ref, *refs):
    unit_refs, (out_ref, keys_ref, units_ref) = refs[:N_Y], refs[-3:]
    block, heads = BLOCK, q_ref.shape[0] // BLOCK
    count = own_ref.shape[0]
    step = pl.program_id(0) + first_step

    @pl.when(step == first_step)
    def _():
        keys_ref[0:count] = prev_ref[...]
        keys_ref[count:] = own_ref[...]
        for i, unit_ref in enumerate(unit_refs):
            rows = unit_ref.shape[0]
            units_ref[i * rows : (i + 1) * rows] = unit_ref[...]

    span = count + block
    keys = keys_ref[pl.ds(pl.multiple_of(step * block, block), span), :]
    units = units_ref[...]
    q = q_ref[...]
    dims = (((1,), (1,)), ((), ()))
    win = lax.dot_general(q, keys, dims, preferred_element_type=jnp.float32) * score_scale
    far = lax.dot_general(q, units, dims, preferred_element_type=jnp.float32) * score_scale
    token = lax.broadcasted_iota(jnp.int32, win.shape, 0) // heads
    key = lax.broadcasted_iota(jnp.int32, win.shape, 1)
    first = jnp.where(s_ref[0] == 0, count - step * block, 0)
    allowed = (key > token) & (key <= token + count) & (key >= first)
    win = jnp.where(allowed, win, -1e30)
    top = jnp.maximum(jnp.max(win, 1, keepdims=True), jnp.max(far, 1, keepdims=True))
    win = jnp.exp(win - top)
    far = jnp.exp(far - top)
    denominator = jnp.sum(win, 1, keepdims=True) + jnp.sum(far, 1, keepdims=True)
    got = jnp.dot(win.astype(jnp.bfloat16), keys[:, :LATENT], preferred_element_type=jnp.float32)
    got = got + jnp.dot(
        far.astype(jnp.bfloat16), units[:, :LATENT], preferred_element_type=jnp.float32
    )
    out_ref[...] = (got / denominator).astype(jnp.bfloat16)


def attend(own_e, queries, previous, group_latent, unit_rows, first_step, steps, context=None):
    count, qk = group_latent.shape
    heads = queries.shape[0] // count
    rows = BLOCK * heads
    operands = [queries, previous, group_latent, *unit_rows]
    specs = [pl.BlockSpec((rows, qk), lambda i, s: (i + first_step, 0))]
    specs += [whole(x.shape) for x in operands[1:]]
    aliases = {}
    if context is not None:
        aliases = {1 + len(operands): 0}
        operands.append(context)
        specs.append(pl.BlockSpec(memory_space=pl.ANY))
    return pl.pallas_call(
        functools.partial(attend_kernel, first_step),
        grid_spec=pltpu.PrefetchScalarGridSpec(
            num_scalar_prefetch=1,
            grid=(steps,),
            in_specs=specs,
            out_specs=pl.BlockSpec((rows, LATENT), lambda i, s: (i + first_step, 0)),
            scratch_shapes=[
                pltpu.VMEM((2 * count, qk), jnp.bfloat16),
                pltpu.VMEM((N_Y * unit_rows[0].shape[0], qk), jnp.bfloat16),
            ],
        ),
        out_shape=jax.ShapeDtypeStruct((count * heads, LATENT), jnp.bfloat16),
        input_output_aliases=aliases,
        compiler_params=params(),
        cost_estimate=cost(1000 * 1000 * 1000 * steps, 2 * 1024 * 1024 * steps),
        name="attend",
    )(own_e, *operands)


def per_device(
    queries,
    group_latent,
    cache_latent,
    unit_ids,
    tokens_b,
    expert_ids,
    affinity,
    gate_w,
    up_w,
    down_w,
):
    own_s = lax.axis_index("section")
    own_e = lax.axis_index("expert")
    at = jnp.stack([own_s, own_e]).astype(jnp.int32)
    tok_count, width = tokens_b.shape
    part = width // N_SECTION
    held, unit_len, qk = cache_latent.shape
    cut = unit_len // N_Y

    message = prep(at, unit_ids, tokens_b, expert_ids, affinity, cache_latent)
    messages = (message,) + tuple(across_j(message, bit) for bit in (1, 2, 3))
    previous = lax.ppermute(
        group_latent, "expert", [(i, i + 1) for i in range(N_EXPERT - 1)]
    )

    down_cut = cut_down(after(down_w, message))
    down_all = over_section(after(down_cut, *messages))

    own_e = own_e[None].astype(jnp.int32)
    pieces, slot, share = pack(own_e, messages, part, qk)
    pieces = [piece if step == 0 else along_z(piece, step) for step, piece in enumerate(pieces)]
    pieces = [pieces[step] for step in Z_ORDER]
    first, second = (
        jnp.concatenate([piece[:, :part] for piece in pieces[i : i + 4]], 0) for i in (0, 4)
    )
    units = [piece[: N_J * cut, part:] for piece in pieces]
    first, second = lax.optimization_barrier((first, second, down_all))[:2]

    before_1 = along_y(first, 1)
    after_2 = along_y(second, -1)
    x_1 = across_x(first)
    before_2 = along_y(second, 1)
    after_1 = along_y(first, -1)
    x_2 = across_x(second)
    far_1 = along_y(before_1, 1)
    far_2 = along_y(after_2, -1)
    before_x = [along_y(x_1, 1), along_y(x_2, 1)]
    after_x = [along_y(x_1, -1), along_y(x_2, -1)]

    far_x = [across_x(far_1), across_x(far_2)]
    blocks = [
        (0, 0, [first, second]),
        (0, 3, [before_1, before_2]),
        (0, 1, [after_1, after_2]),
        (1, 0, [x_1, x_2]),
        (0, 2, [far_1, far_2]),
        (1, 3, before_x),
        (1, 1, after_x),
        (1, 2, far_x),
    ]
    hidden = over_section(add_blocks(at, blocks, gate_w, up_w))

    owner = unit_ids // held
    steps = (own_e // N_J - owner // N_J) % N_Z
    steps = jnp.array([Z_ORDER.index(step) for step in range(N_Z)], jnp.int32)[steps]
    order = steps * N_J + ((owner ^ own_e) % N_J)
    units = list(lax.optimization_barrier((*units, hidden))[:-1])
    units = jnp.concatenate(units, 0).reshape(N_Z * N_J, cut, qk)[order].reshape(-1, qk)
    unit_rows = (units, along_y(units, 1), along_y(units, -1), along_y(units, 2))
    back = over_z(down(own_e, hidden, down_all)).reshape(-1, part)

    keys = (previous, group_latent, unit_rows)
    half = group_latent.shape[0] // BLOCK // 2
    back, rows_q, *_ = lax.optimization_barrier(
        (back, queries.reshape(-1, qk), unit_rows, previous)
    )
    context = attend(at[1:], after(rows_q, back), *keys, 0, half)
    mixed = over_j(mix(own_e, slot, share, back))
    mixed, context = lax.optimization_barrier((mixed, context))
    out_part = jnp.sum(mixed.astype(jnp.float32), 0).astype(jnp.bfloat16)
    out_part = jnp.broadcast_to(out_part[None], (N_SECTION, tok_count, part))
    context = attend(at[1:], after(rows_q, mixed), *keys, half, half, context)
    context = context.reshape(queries.shape[0], queries.shape[1], LATENT)
    moe_out = over_section(out_part).transpose(1, 0, 2).reshape(tok_count, width)
    return (context, moe_out)


def solution(mesh):
    return jax.shard_map(
        per_device,
        mesh=mesh,
        in_specs=(
            P("expert", "section", None),
            P("expert", None),
            P("expert", None, None),
            P(),
            P("expert", None),
            P("expert", None),
            P("expert", None),
            P("expert", None, "section"),
            P("expert", None, "section"),
            P("expert", "section", None),
        ),
        out_specs=(P("expert", "section", None), P("expert", None)),
        check_vma=False,
    )
```

time: 505 us -> 167 us (0.33)
  waiting for transfers between devices: 341 us -> 36.1 us
  starting transfers between devices: 20.7 us -> 75.7 us
  blocking collectives: 41.8 us -> 0 us
  local copies, waits for them, and re-layouts: 52.1 us -> 20.7 us
  Pallas kernels: 0 us -> 31.2 us
  matrix products: 30.4 us -> 0 us
  between operations: 14.3 us -> 1.01 us
    all_to_all x2 -> x5, waiting for transfers between devices: 180 us -> 6.2 us  [the longest x3 5.03 us: over_section(): lax.all_to_all(value, 'section', split_axis=0, concat_axis=0, tiled=True)]
    ppermute x1 -> x28, waiting for transfers between devices: 161 us -> 29.9 us  [the longest x13 14.6 us: along_y(): return lax.ppermute(value, 'section', pairs)]
    ppermute x1 -> x28, starting transfers between devices: 2.28 us -> 48.3 us  [the longest x13 24.1 us: along_y(): return lax.ppermute(value, 'section', pairs)]
    psum x1 -> x0, blocking collectives: 41.8 us -> none  [routed(): return lax.psum(partial_value, 'section').astype(jnp.bfloat16)]
    pallas_call x0 -> x8, Pallas kernels: none -> 31.2 us  [the longest x2 12.1 us: attend(): pl.pallas_call(functools.partial(attend_kernel, first_step), grid_spec=pl...]
    dot_general x7 -> x0, matrix products: 30.4 us -> none  [the longest x1 11.3 us: send_back(): jnp.einsum('scf,fd->scd', hidden, down_w[0], preferred_element_type=jnp.f...]
    gather x3 -> x2, local copies, waits for them, and re-layouts: 20.3 us -> 2.21 us  [the longest x1 1.55 us: per_device(): jnp.concatenate(units, 0).reshape(N_Z * N_J, cut, qk)[order].reshape(-1, qk)]
    reshape x2 -> x1, local copies, waits for them, and re-layouts: 15.9 us -> 0.81 us  [per_device(): over_section(out_part).transpose(1, 0, 2).reshape(tok_count, width)]
  transfers between devices with their start and end apart: 4 -> 33, of which waited for: 2 -> 18; matrix products, arithmetic and copies ran while one was open for 9% -> 10% of each run, Pallas kernels for 0% -> 16%
where the time goes in v2:
time: 167 us; the launch traced here: 166 us
  starting transfers between devices  75.7 us (45%)
  waiting for transfers between devices  36.1 us (22%)
  Pallas kernels  31.2 us (19%)
  local copies, waits for them, and re-layouts  20.7 us (12%)
    ppermute x13, starting transfers between devices, along_y(): return lax.ppermute(value, 'section', pairs)  24.1 us
    ppermute x7, starting transfers between devices, along_z(): lax.ppermute(value, 'expert', [(e, (e + steps * N_J) % N_EXPERT) for e in...  15.4 us
    ppermute x13, waiting for transfers between devices, along_y(): return lax.ppermute(value, 'section', pairs)  14.6 us
    all_to_all x3, starting transfers between devices, over_section(): lax.all_to_all(value, 'section', split_axis=0, concat_axis=0, tiled=True)  13 us
    pallas_call x2, Pallas kernels, attend(): pl.pallas_call(functools.partial(attend_kernel, first_step), grid_spec=pl...  12.1 us
    ppermute x7, waiting for transfers between devices, along_z(): lax.ppermute(value, 'expert', [(e, (e + steps * N_J) % N_EXPERT) for e in...  11.5 us
    unnamed x63, local copies, waits for them, and re-layouts  8.6 us
    slice x8, local copies, waits for them, and re-layouts, per_device(): units = [piece[:N_J * cut, part:] for piece in pieces]  7.32 us
  transfers between devices with their start and end apart: 33, of which 18 were waited for; matrix products, arithmetic and copies ran while one was open for 10% of the time, Pallas kernels for 16%

profile of v2, /device:TPU:64, one launch (start us, length us, event | category | flops | bytes accessed | tf_op | source)
XLA Modules:
  0.0 165.6 jit_solution(16898579722295713470)
XLA Ops:
  0.6 0.6 pad_add_fusion.at_ref
  1.3 2.4 %prep.1.m_ref = bf16[48,896]{1,0:T(8,128)(2,1)} custom-call(s32[2]{0:T(128)} %pad_add_fusion.at_ref, s32[16]{0:T(128)} %unit_ref.1, bf16[32,7168]{1,0:T(8,128)(2,1)} %tok_ref.1, s32[8,32]{1,0:T(8,128)} %bitcast.25, f32[8,32]{1,0:T(8,128)} %bitcast.26, bf16[4,32,576]{2,1,0:T(8,128)(2,1)} %cache_ref.1), custom_call_target="tpu_custom_call" | custom-call | flops 1000 | bytes 409600 | tf_op jit(solution)/shard_map/prep/pallas_call | solution.py:134
  3.7 2.5 %collective-permute-start.2 = (bf16[48,896]{1,0:T(8,128)(2,1)}, bf16[48,896]{1,0:T(8,128)(2,1)S(1)}, u32[]{:S(2)}, u32[]{:S(2)}) collective-permute-start(bf16[48,896]{1,0:T(8,128)(2,1)} %prep.1.m_ref), channel_id=1, source_target_pairs={{0,3},{1,2},{2,1},{3,0},{4,7},{5,6},{6,5},{7,4},{8,11},{9,10},{10,... | collective-permute-start | bytes 258056 | tf_op jit(solution)/shard_map/ppermute | solution.py:49
  7.1 2.9 %cut_down.1 = bf16[8,128,896]{2,1,0:T(8,128)(2,1)} custom-call(bf16[1,128,7168]{2,1,0:T(8,128)(2,1)} %in_ref), custom_call_target="tpu_custom_call" | custom-call | bytes 3670016 | tf_op jit(solution)/shard_map/cut_down/pallas_call | solution.py:214
  10.2 2.8 %collective-permute-done.1.x_ref = bf16[48,896]{1,0:T(8,128)(2,1)S(1)} collective-permute-done((bf16[48,896]{1,0:T(8,128)(2,1)}, bf16[48,896]{1,0:T(8,128)(2,1)S(1)}, u32[]{:S(2)}, u32[]{:S(2)}) %collective-permute-start.1) | collective-permute-done | bytes 86048 | tf_op jit(solution)/shard_map/ppermute | solution.py:49
  13.0 4.5 %all-to-all-start = ((bf16[8,128,896]{2,1,0:T(8,128)(2,1)}), bf16[8,128,896]{2,1,0:T(8,128)(2,1)S(1)}, u32[]{:S(2)}, u32[]{:S(2)}) async-start(bf16[8,128,896]{2,1,0:T(8,128)(2,1)} %cut_down.1), calls=%async_computation | async-start | bytes 3670016 | tf_op jit(solution)/shard_map/all_to_all | solution.py:71
  17.5 2.4 %pack.1 = (f32[8,128]{1,0:T(8,128)}, f32[8,128]{1,0:T(8,128)}, bf16[40,1472]{1,0:T(8,128)(2,1)}, bf16[40,1472]{1,0:T(8,128)(2,1)}, bf16[40,1472]{1,0:T(8,128)(2,...) custom-call(s32[1]{0:T(128)} %bitcast.e_ref.s_ref, ...), custom_call_target="tpu_custom_call" | custom-call | flops 73400320 | bytes 1146880 | tf_op jit(solution)/shard_map/pack/pallas_call | solution.py:193
  20.0 1.9 %collective-permute-start.3 = (bf16[40,1472]{1,0:T(8,128)(2,1)}, bf16[40,1472]{1,0:T(8,128)(2,1)S(1)}, u32[]{:S(2)}, u32[]{:S(2)}) collective-permute-start(bf16[40,1472]{1,0:T(8,128)(2,1)} %get-tuple-element.31), channel_id=1, source_target_pairs={{0,4},{1,5},{2,6},{3,7},{4,8},{5,9},{6,10},{7,11},{8,12},{9,13},{1... | collective-permute-start | bytes 353288 | tf_op jit(solution)/shard_map/ppermute | solution.py:53
  22.0 5.7 %collective-permute-start.5 = (bf16[40,1472]{1,0:T(8,128)(2,1)}, bf16[40,1472]{1,0:T(8,128)(2,1)S(1)}, u32[]{:S(2)}, u32[]{:S(2)}) collective-permute-start(bf16[40,1472]{1,0:T(8,128)(2,1)} %get-tuple-element.33), channel_id=1, source_target_pairs={{0,8},{1,9},{2,10},{3,11},{4,12},{5,13},{6,14},{7,15},{8,16},{9,17... | collective-permute-start | bytes 353288 | tf_op jit(solution)/shard_map/ppermute | solution.py:53
  27.7 3.4 %collective-permute-start.7 = (bf16[40,1472]{1,0:T(8,128)(2,1)}, bf16[40,1472]{1,0:T(8,128)(2,1)S(1)}, u32[]{:S(2)}, u32[]{:S(2)}) collective-permute-start(bf16[40,1472]{1,0:T(8,128)(2,1)} %get-tuple-element.35), channel_id=1, source_target_pairs={{0,12},{1,13},{2,14},{3,15},{4,16},{5,17},{6,18},{7,19},{8,20},{9,... | collective-permute-start | bytes 353288 | tf_op jit(solution)/shard_map/ppermute | solution.py:53
  31.1 1.7 %collective-permute-start.8 = (bf16[40,1472]{1,0:T(8,128)(2,1)}, bf16[40,1472]{1,0:T(8,128)(2,1)S(1)}, u32[]{:S(2)}, u32[]{:S(2)}) collective-permute-start(bf16[40,1472]{1,0:T(8,128)(2,1)} %get-tuple-element.36), channel_id=1, source_target_pairs={{0,20},{1,21},{2,22},{3,23},{4,24},{5,25},{6,26},{7,27},{8,28},{9,... | collective-permute-start | bytes 353288 | tf_op jit(solution)/shard_map/ppermute | solution.py:53
  32.7 2.6 %collective-permute-start.9 = (bf16[40,1472]{1,0:T(8,128)(2,1)}, bf16[40,1472]{1,0:T(8,128)(2,1)S(1)}, u32[]{:S(2)}, u32[]{:S(2)}) collective-permute-start(bf16[40,1472]{1,0:T(8,128)(2,1)} %get-tuple-element.37), channel_id=1, source_target_pairs={{0,16},{1,17},{2,18},{3,19},{4,20},{5,21},{6,22},{7,23},{8,24},{9,... | collective-permute-start | bytes 353288 | tf_op jit(solution)/shard_map/ppermute | solution.py:53
  35.3 0.9 slice.48
  36.3 1.6 collective-permute-done.5
  37.9 5.4 %collective-permute-done.7 = bf16[40,1472]{1,0:T(8,128)(2,1)S(1)} collective-permute-done((bf16[40,1472]{1,0:T(8,128)(2,1)}, bf16[40,1472]{1,0:T(8,128)(2,1)S(1)}, u32[]{:S(2)}, u32[]{:S(2)}) %collective-permute-start.7) | collective-permute-done | bytes 117792 | tf_op jit(solution)/shard_map/ppermute | solution.py:53
  43.3 3.8 %collective-permute-done.8 = bf16[40,1472]{1,0:T(8,128)(2,1)S(1)} collective-permute-done((bf16[40,1472]{1,0:T(8,128)(2,1)}, bf16[40,1472]{1,0:T(8,128)(2,1)S(1)}, u32[]{:S(2)}, u32[]{:S(2)}) %collective-permute-start.8) | collective-permute-done | bytes 117792 | tf_op jit(solution)/shard_map/ppermute | solution.py:53
  47.1 0.7 collective-permute-done.9
  48.0 2.1 %collective-permute-start.14 = (bf16[160,896]{1,0:T(8,128)(2,1)S(1)}, bf16[160,896]{1,0:T(8,128)(2,1)S(1)}, u32[]{:S(2)}, u32[]{:S(2)}) collective-permute-start(bf16[160,896]{1,0:T(8,128)(2,1)S(1)} %pad_maximum_fusion.refs_0_), channel_id=1, source_target_pairs={{0,128},{32,160},{64,192},{96,224},{128,0},{160,32},{192,64},{224,... | collective-permute-start | bytes 860168 | tf_op jit(solution)/shard_map/ppermute | solution.py:41
  50.1 2.7 %collective-permute-start.12 = (bf16[160,896]{1,0:T(8,128)(2,1)S(1)}, bf16[160,896]{1,0:T(8,128)(2,1)S(1)}, u32[]{:S(2)}, u32[]{:S(2)}) collective-permute-start(bf16[160,896]{1,0:T(8,128)(2,1)S(1)} %pad_maximum_fusion.refs_0_), channel_id=1, source_target_pairs={{0,96},{32,0},{64,32},{96,64},{128,224},{160,128},{192,160},{224,1... | collective-permute-start | bytes 860168 | tf_op jit(solution)/shard_map/ppermute | solution.py:36
  52.8 3.2 %collective-permute-start.13 = (bf16[160,896]{1,0:T(8,128)(2,1)S(1)}, bf16[160,896]{1,0:T(8,128)(2,1)S(1)}, u32[]{:S(2)}, u32[]{:S(2)}) collective-permute-start(bf16[160,896]{1,0:T(8,128)(2,1)S(1)} %pad_maximum_fusion.1.refs_1_), channel_id=1, source_target_pairs={{0,96},{32,0},{64,32},{96,64},{128,224},{160,128},{192,160},{224,1... | collective-permute-start | bytes 860168 | tf_op jit(solution)/shard_map/ppermute | solution.py:36
  56.6 3.3 %collective-permute-start.11 = (bf16[160,896]{1,0:T(8,128)(2,1)S(1)}, bf16[160,896]{1,0:T(8,128)(2,1)S(1)}, u32[]{:S(2)}, u32[]{:S(2)}) collective-permute-start(bf16[160,896]{1,0:T(8,128)(2,1)S(1)} %pad_maximum_fusion.1.refs_1_), channel_id=1, source_target_pairs={{0,32},{32,64},{64,96},{96,0},{128,160},{160,192},{192,224},{224,1... | collective-permute-start | bytes 860168 | tf_op jit(solution)/shard_map/ppermute | solution.py:36
  60.1 3.7 %collective-permute-start.20 = (bf16[160,896]{1,0:T(8,128)(2,1)S(1)}, bf16[160,896]{1,0:T(8,128)(2,1)S(1)}, u32[]{:S(2)}, u32[]{:S(2)}) collective-permute-start(bf16[160,896]{1,0:T(8,128)(2,1)S(1)} %collective-permute-done.14.refs_6_), channel_id=1, source_target_pairs={{0,96},{32,0},{64,32},{96,64},{128,224},{160,128},{192,160},{224,1... | collective-permute-start | bytes 860168 | tf_op jit(solution)/shard_map/ppermute | solution.py:36
  63.8 2.4 %collective-permute-done.13.refs_5_ = bf16[160,896]{1,0:T(8,128)(2,1)S(1)} collective-permute-done((bf16[160,896]{1,0:T(8,128)(2,1)S(1)}, bf16[160,896]{1,0:T(8,128)(2,1)S(1)}, u32[]{:S(2)}, u32[]{:S(2)}) %collective-permute-start.13) | collective-permute-done | bytes 286752 | tf_op jit(solution)/shard_map/ppermute | solution.py:36
  66.2 3.7 %collective-permute-start.17 = (bf16[160,896]{1,0:T(8,128)(2,1)S(1)}, bf16[160,896]{1,0:T(8,128)(2,1)}, u32[]{:S(2)}, u32[]{:S(2)}) collective-permute-start(bf16[160,896]{1,0:T(8,128)(2,1)S(1)} %collective-permute-done.13.refs_5_), channel_id=1, source_target_pairs={{0,96},{32,0},{64,32},{96,64},{128,224},{160,128},{192,160},{224,1... | collective-permute-start | bytes 860168 | tf_op jit(solution)/shard_map/ppermute | solution.py:36
  70.0 3.2 %collective-permute-start.21 = (bf16[160,896]{1,0:T(8,128)(2,1)}, bf16[160,896]{1,0:T(8,128)(2,1)}, u32[]{:S(2)}, u32[]{:S(2)}) collective-permute-start(bf16[160,896]{1,0:T(8,128)(2,1)} %collective-permute-done.15.refs_7_), channel_id=1, source_target_pairs={{0,96},{32,0},{64,32},{96,64},{128,224},{160,128},{192,160},{224,1... | collective-permute-start | bytes 860168 | tf_op jit(solution)/shard_map/ppermute | solution.py:36
  73.7 2.5 %collective-permute-done.16.refs_8_ = bf16[160,896]{1,0:T(8,128)(2,1)} collective-permute-done((bf16[160,896]{1,0:T(8,128)(2,1)S(1)}, bf16[160,896]{1,0:T(8,128)(2,1)}, u32[]{:S(2)}, u32[]{:S(2)}) %collective-permute-start.16) | collective-permute-done | bytes 286752 | tf_op jit(solution)/shard_map/ppermute | solution.py:36
  76.6 1.9 %collective-permute-done.17.refs_9_ = bf16[160,896]{1,0:T(8,128)(2,1)} collective-permute-done((bf16[160,896]{1,0:T(8,128)(2,1)S(1)}, bf16[160,896]{1,0:T(8,128)(2,1)}, u32[]{:S(2)}, u32[]{:S(2)}) %collective-permute-start.17) | collective-permute-done | bytes 286752 | tf_op jit(solution)/shard_map/ppermute | solution.py:36
  79.4 3.0 %collective-permute-done.18.refs_10_ = bf16[160,896]{1,0:T(8,128)(2,1)} collective-permute-done((bf16[160,896]{1,0:T(8,128)(2,1)S(1)}, bf16[160,896]{1,0:T(8,128)(2,1)}, u32[]{:S(2)}, u32[]{:S(2)}) %collective-permute-start.18) | collective-permute-done | bytes 286752 | tf_op jit(solution)/shard_map/ppermute | solution.py:36
  82.3 1.9 %collective-permute-start.27 = (bf16[256,576]{1,0:T(8,128)(2,1)S(1)}, bf16[256,576]{1,0:T(8,128)(2,1)}, u32[]{:S(2)}, u32[]{:S(2)}) collective-permute-start(bf16[256,576]{1,0:T(8,128)(2,1)S(1)} %copy.27.own_ref), channel_id=1, source_target_pairs={{0,1},{1,2},{2,3},{3,4},{4,5},{5,6},{6,7},{7,8},{8,9},{9,10},{10,1... | collective-permute-start | bytes 884744 | tf_op jit(solution)/shard_map/ppermute | solution.py:422
  84.3 1.9 %collective-permute-done.19.refs_11_ = bf16[160,896]{1,0:T(8,128)(2,1)} collective-permute-done((bf16[160,896]{1,0:T(8,128)(2,1)}, bf16[160,896]{1,0:T(8,128)(2,1)}, u32[]{:S(2)}, u32[]{:S(2)}) %collective-permute-start.19) | collective-permute-done | bytes 286752 | tf_op jit(solution)/shard_map/ppermute | solution.py:36
  86.1 0.7 collective-permute-done.23.refs_15_
  86.8 5.8 %add_blocks.1 = bf16[8,320,128]{2,1,0:T(8,128)(2,1)} custom-call(s32[2]{0:T(128)} %pad_add_fusion.at_ref, bf16[160,896]{1,0:T(8,128)(2,1)} %copy-done.6, bf16[160,896]{1,0:T(8,128)(2,1)} %copy-done.7, bf16[160,896]{1,0:T(8,128)(2,1)} %copy-done.12, bf16[160,896]{1,0:T(8,128)(2,1)} %copy-done.14, bf16[160,896]{1,0:T(8,128)(2,1)} %copy-done.11, ...), custom_call_target="tpu_custom_call" | custom-call | flops 1174405120 | bytes 10485760 | tf_op jit(solution)/shard_map/add_blocks/pallas_call | solution.py:253
  92.7 5.0 %all-to-all-start.1 = ((bf16[8,320,128]{2,1,0:T(8,128)(2,1)}), bf16[8,320,128]{2,1,0:T(8,128)(2,1)S(1)}, u32[]{:S(2)}, u32[]{:S(2)}) async-start(bf16[8,320,128]{2,1,0:T(8,128)(2,1)} %add_blocks.1), calls=%async_computation.1 | async-start | bytes 1310720 | tf_op jit(solution)/shard_map/all_to_all | solution.py:71
  97.8 0.7 gather_fusion
  98.5 1.4 slice.56
  100.5 1.4 slice.76
  101.9 0.8 slice.77
  102.7 0.8 slice.78
  103.4 0.8 slice.79
  104.2 0.8 slice.80
  105.0 0.8 slice.81
  105.8 2.1 %all-to-all-done.1.hid = bf16[8,320,128]{2,1,0:T(8,128)(2,1)S(1)} async-done(((bf16[8,320,128]{2,1,0:T(8,128)(2,1)}), bf16[8,320,128]{2,1,0:T(8,128)(2,1)S(1)}, u32[]{:S(2)}, u32[]{:S(2)}) %all-to-all-start.1) | async-done | bytes 655392 | tf_op jit(solution)/shard_map/all_to_all | solution.py:71
  107.8 0.9 copy-done.2
  108.7 3.4 %down.1 = bf16[8,40,896]{2,1,0:T(8,128)(2,1)} custom-call(s32[1]{0:T(128)} %bitcast.e_ref.s_ref, bf16[8,320,128]{2,1,0:T(8,128)(2,1)} %copy-done.2, bf16[8,128,896]{2,1,0:T(8,128)(2,1)} %copy-done.1), custom_call_target="tpu_custom_call" | custom-call | flops 587202560 | bytes 4194304 | tf_op jit(solution)/shard_map/down/pallas_call | solution.py:281
  112.1 7.1 %all-to-all-start.2 = ((bf16[8,40,896]{2,1,0:T(8,128)(2,1)}), bf16[8,40,896]{2,1,0:T(8,128)(2,1)S(1)}, u32[]{:S(2)}, u32[]{:S(2)}) async-start(bf16[8,40,896]{2,1,0:T(8,128)(2,1)} %down.1), calls=%async_computation.2 | async-start | bytes 1146880 | tf_op jit(solution)/shard_map/all_to_all | solution.py:59
  119.2 0.8 constant_dynamic-update-slice_fusion.7
  119.9 0.8 constant_dynamic-update-slice_fusion.6
  120.7 0.8 constant_dynamic-update-slice_fusion.5
  121.6 0.7 copy-done.16
  122.3 1.6 gather_fusion.1
  123.9 1.7 %collective-permute-start.26 = (bf16[128,576]{1,0:T(8,128)(2,1)S(1)}, bf16[128,576]{1,0:T(8,128)(2,1)}, u32[]{:S(2)}, u32[]{:S(2)}) collective-permute-start(bf16[128,576]{1,0:T(8,128)(2,1)S(1)} %bitcast.18), channel_id=1, source_target_pairs={{0,64},{32,96},{64,0},{96,32},{128,192},{160,224},{192,128},{224,1... | collective-permute-start | bytes 442376 | tf_op jit(solution)/shard_map/ppermute | solution.py:36
  125.6 1.6 collective-permute-start.25
  127.7 3.5 %copy.26 = bf16[256,8,576]{2,1,0:T(8,128)(2,1)} copy(bf16[256,8,576]{0,2,1:T(8,128)(2,1)S(1)} %copy-done.3) | data formatting | bytes 4718592 | tf_op args[0]
  131.7 2.1 %collective-permute-done.24.refs_1_ = bf16[128,576]{1,0:T(8,128)(2,1)} collective-permute-done((bf16[128,576]{1,0:T(8,128)(2,1)S(1)}, bf16[128,576]{1,0:T(8,128)(2,1)}, u32[]{:S(2)}, u32[]{:S(2)}) %collective-permute-start.24) | collective-permute-done | bytes 147488 | tf_op jit(solution)/shard_map/ppermute | solution.py:36
  133.8 0.8 copy-done.4
  134.6 2.3 %mix.1 = bf16[4,32,896]{2,1,0:T(8,128)(2,1)} custom-call(s32[1]{0:T(128)} %bitcast.e_ref.s_ref, f32[8,128]{1,0:T(8,128)} %get-tuple-element.51.slot_ref, f32[8,128]{1,0:T(8,128)} %get-tuple-element.52.share_ref, bf16[320,896]{1,0:T(8,128)(2,1)} %bitcast.15), custom_call_target="tpu_custom_call" | custom-call | flops 146800640 | bytes 1146880 | tf_op jit(solution)/shard_map/mix/pallas_call | solution.py:320
  136.9 7.3 %all-to-all-start.3 = ((bf16[4,32,896]{2,1,0:T(8,128)(2,1)}), bf16[4,32,896]{2,1,0:T(8,128)(2,1)S(1)}, u32[]{:S(2)}, u32[]{:S(2)}) async-start(bf16[4,32,896]{2,1,0:T(8,128)(2,1)} %mix.1), calls=%async_computation.3 | async-start | bytes 458752 | tf_op jit(solution)/shard_map/all_to_all | solution.py:65
  144.2 6.0 %attend.2.refs_4_ = bf16[2048,512]{1,0:T(8,128)(2,1)} custom-call(s32[1]{0:T(128)} %bitcast.e_ref.s_ref, bf16[2048,576]{1,0:T(8,128)(2,1)} %bitcast.13, bf16[256,576]{1,0:T(8,128)(2,1)} %collective-permute-done.27.prev_ref, bf16[256,576]{1,0:T(8,128)(2,1)} %copy-done.5, bf16[128,576]{1,0:T(8,128)(2,1)} %bitcast.21, ...), custom_call_target="tpu_custom_call" | custom-call | flops 2000000000 | bytes 4194304 | tf_op jit(solution)/shard_map/attend/pallas_call | solution.py:380
  150.2 1.2 all-to-all-done.3
  151.4 0.8 broadcast_in_dim.15
  152.2 3.5 %all-to-all-start.4 = ((bf16[8,32,896]{2,1,0:T(8,128)(2,1)}), bf16[8,32,896]{2,1,0:T(8,128)(2,1)S(1)}, u32[]{:S(2)}, u32[]{:S(2)}) async-start(bf16[8,32,896]{2,1,0:T(8,128)(2,1)} %broadcast_in_dim.15), calls=%async_computation.4 | async-start | bytes 917504 | tf_op jit(solution)/shard_map/all_to_all | solution.py:71
  155.7 6.0 %attend.3 = bf16[2048,512]{1,0:T(8,128)(2,1)} custom-call(s32[1]{0:T(128)} %bitcast.e_ref.s_ref, bf16[2048,576]{1,0:T(8,128)(2,1)} %bitcast.14, bf16[256,576]{1,0:T(8,128)(2,1)} %collective-permute-done.27.prev_ref, bf16[256,576]{1,0:T(8,128)(2,1)} %copy-done.5, bf16[128,576]{1,0:T(8,128)(2,1)} %bitcast.22, ...), custom_call_target="tpu_custom_call", output_to_operand_aliasing={{}: (8, {})} | custom-call | flops 2000000000 | bytes 4194304 | tf_op jit(solution)/shard_map/attend/pallas_call | solution.py:380
  161.8 3.0 %all-to-all-done.4 = bf16[8,32,896]{2,1,0:T(8,128)(2,1)S(1)} async-done(((bf16[8,32,896]{2,1,0:T(8,128)(2,1)}), bf16[8,32,896]{2,1,0:T(8,128)(2,1)S(1)}, u32[]{:S(2)}, u32[]{:S(2)}) %all-to-all-start.4) | async-done | bytes 458784 | tf_op jit(solution)/shard_map/all_to_all | solution.py:71
  164.7 0.8 copy.31
  (102 shorter events, 5.6 us)
Async XLA Ops:
  3.7 6.5 %collective-permute-start.2 = (bf16[48,896]{1,0:T(8,128)(2,1)}, bf16[48,896]{1,0:T(8,128)(2,1)S(1)}, u32[]{:S(2)}, u32[]{:S(2)}) collective-permute-start(bf16[48,896]{1,0:T(8,128)(2,1)} %prep.1.m_ref), channel_id=1, source_target_pairs={{0,3},{1,2},{2,1},{3,0},{4,7},{5,6},{6,5},{7,4},{8,11},{9,10},{10,... | collective-permute-start | bytes 258056 | tf_op jit(solution)/shard_map/ppermute | solution.py:49
  6.2 6.8 %collective-permute-start.1 = (bf16[48,896]{1,0:T(8,128)(2,1)}, bf16[48,896]{1,0:T(8,128)(2,1)S(1)}, u32[]{:S(2)}, u32[]{:S(2)}) collective-permute-start(bf16[48,896]{1,0:T(8,128)(2,1)} %prep.1.m_ref), channel_id=1, source_target_pairs={{0,2},{1,3},{2,0},{3,1},{4,6},{5,7},{6,4},{7,5},{8,10},{9,11},{10,... | collective-permute-start | bytes 258056 | tf_op jit(solution)/shard_map/ppermute | solution.py:49
  6.8 6.2 %collective-permute-start = (bf16[48,896]{1,0:T(8,128)(2,1)}, bf16[48,896]{1,0:T(8,128)(2,1)S(1)}, u32[]{:S(2)}, u32[]{:S(2)}) collective-permute-start(bf16[48,896]{1,0:T(8,128)(2,1)} %prep.1.m_ref), channel_id=1, source_target_pairs={{0,1},{1,0},{2,3},{3,2},{4,5},{5,4},{6,7},{7,6},{8,9},{9,8},{10,11... | collective-permute-start | bytes 258056 | tf_op jit(solution)/shard_map/ppermute | solution.py:49
  10.2 7.3 %copy-start.23 = (bf16[48,896]{1,0:T(8,128)(2,1)}, bf16[48,896]{1,0:T(8,128)(2,1)S(1)}, u32[]{:S(2)}) copy-start(bf16[48,896]{1,0:T(8,128)(2,1)S(1)} %collective-permute-done.2.xc_ref) | copy-start | bytes 258052
  13.0 4.5 %copy-start.24 = (bf16[48,896]{1,0:T(8,128)(2,1)}, bf16[48,896]{1,0:T(8,128)(2,1)S(1)}, u32[]{:S(2)}) copy-start(bf16[48,896]{1,0:T(8,128)(2,1)S(1)} %collective-permute-done.1.x_ref) | copy-start | bytes 258052
  13.0 4.5 %copy-start.25 = (bf16[48,896]{1,0:T(8,128)(2,1)}, bf16[48,896]{1,0:T(8,128)(2,1)S(1)}, u32[]{:S(2)}) copy-start(bf16[48,896]{1,0:T(8,128)(2,1)S(1)} %collective-permute-done.c_ref) | copy-start | bytes 258052
  13.0 35.0 %all-to-all-start = ((bf16[8,128,896]{2,1,0:T(8,128)(2,1)}), bf16[8,128,896]{2,1,0:T(8,128)(2,1)S(1)}, u32[]{:S(2)}, u32[]{:S(2)}) async-start(bf16[8,128,896]{2,1,0:T(8,128)(2,1)} %cut_down.1), calls=%async_computation | async-start | bytes 3670016 | tf_op jit(solution)/shard_map/all_to_all | solution.py:71
  17.5 61.6 %copy-start.9 = (bf16[256,576]{0,1:T(8,128)(2,1)S(1)}, bf16[256,576]{0,1:T(8,128)(2,1)}, u32[]{:S(2)}) copy-start(bf16[256,576]{0,1:T(8,128)(2,1)} %param.12) | copy-start | bytes 884740
  20.0 11.1 %collective-permute-start.3 = (bf16[40,1472]{1,0:T(8,128)(2,1)}, bf16[40,1472]{1,0:T(8,128)(2,1)S(1)}, u32[]{:S(2)}, u32[]{:S(2)}) collective-permute-start(bf16[40,1472]{1,0:T(8,128)(2,1)} %get-tuple-element.31), channel_id=1, source_target_pairs={{0,4},{1,5},{2,6},{3,7},{4,8},{5,9},{6,10},{7,11},{8,12},{9,13},{1... | collective-permute-start | bytes 353288 | tf_op jit(solution)/shard_map/ppermute | solution.py:53
  21.9 10.8 %collective-permute-start.4 = (bf16[40,1472]{1,0:T(8,128)(2,1)}, bf16[40,1472]{1,0:T(8,128)(2,1)S(1)}, u32[]{:S(2)}, u32[]{:S(2)}) collective-permute-start(bf16[40,1472]{1,0:T(8,128)(2,1)} %get-tuple-element.32), channel_id=1, source_target_pairs={{0,28},{1,29},{2,30},{3,31},{4,0},{5,1},{6,2},{7,3},{8,4},{9,5},{1... | collective-permute-start | bytes 353288 | tf_op jit(solution)/shard_map/ppermute | solution.py:53
  22.0 15.9 %collective-permute-start.5 = (bf16[40,1472]{1,0:T(8,128)(2,1)}, bf16[40,1472]{1,0:T(8,128)(2,1)S(1)}, u32[]{:S(2)}, u32[]{:S(2)}) collective-permute-start(bf16[40,1472]{1,0:T(8,128)(2,1)} %get-tuple-element.33), channel_id=1, source_target_pairs={{0,8},{1,9},{2,10},{3,11},{4,12},{5,13},{6,14},{7,15},{8,16},{9,17... | collective-permute-start | bytes 353288 | tf_op jit(solution)/shard_map/ppermute | solution.py:53
  27.7 10.2 %collective-permute-start.6 = (bf16[40,1472]{1,0:T(8,128)(2,1)}, bf16[40,1472]{1,0:T(8,128)(2,1)S(1)}, u32[]{:S(2)}, u32[]{:S(2)}) collective-permute-start(bf16[40,1472]{1,0:T(8,128)(2,1)} %get-tuple-element.34), channel_id=1, source_target_pairs={{0,24},{1,25},{2,26},{3,27},{4,28},{5,29},{6,30},{7,31},{8,0},{9,1... | collective-permute-start | bytes 353288 | tf_op jit(solution)/shard_map/ppermute | solution.py:53
  27.7 15.6 %collective-permute-start.7 = (bf16[40,1472]{1,0:T(8,128)(2,1)}, bf16[40,1472]{1,0:T(8,128)(2,1)S(1)}, u32[]{:S(2)}, u32[]{:S(2)}) collective-permute-start(bf16[40,1472]{1,0:T(8,128)(2,1)} %get-tuple-element.35), channel_id=1, source_target_pairs={{0,12},{1,13},{2,14},{3,15},{4,16},{5,17},{6,18},{7,19},{8,20},{9,... | collective-permute-start | bytes 353288 | tf_op jit(solution)/shard_map/ppermute | solution.py:53
  31.1 16.1 %collective-permute-start.8 = (bf16[40,1472]{1,0:T(8,128)(2,1)}, bf16[40,1472]{1,0:T(8,128)(2,1)S(1)}, u32[]{:S(2)}, u32[]{:S(2)}) collective-permute-start(bf16[40,1472]{1,0:T(8,128)(2,1)} %get-tuple-element.36), channel_id=1, source_target_pairs={{0,20},{1,21},{2,22},{3,23},{4,24},{5,25},{6,26},{7,27},{8,28},{9,... | collective-permute-start | bytes 353288 | tf_op jit(solution)/shard_map/ppermute | solution.py:53
  32.7 15.1 %copy-start.17 = (bf16[40,1472]{1,0:T(8,128)(2,1)}, bf16[40,1472]{1,0:T(8,128)(2,1)S(1)}, u32[]{:S(2)}) copy-start(bf16[40,1472]{1,0:T(8,128)(2,1)S(1)} %collective-permute-done.4) | copy-start | bytes 353284
  32.7 15.1 %collective-permute-start.9 = (bf16[40,1472]{1,0:T(8,128)(2,1)}, bf16[40,1472]{1,0:T(8,128)(2,1)S(1)}, u32[]{:S(2)}, u32[]{:S(2)}) collective-permute-start(bf16[40,1472]{1,0:T(8,128)(2,1)} %get-tuple-element.37), channel_id=1, source_target_pairs={{0,16},{1,17},{2,18},{3,19},{4,20},{5,21},{6,22},{7,23},{8,24},{9,... | collective-permute-start | bytes 353288 | tf_op jit(solution)/shard_map/ppermute | solution.py:53
  37.9 10.0 %copy-start.18 = (bf16[40,1472]{1,0:T(8,128)(2,1)}, bf16[40,1472]{1,0:T(8,128)(2,1)S(1)}, u32[]{:S(2)}) copy-start(bf16[40,1472]{1,0:T(8,128)(2,1)S(1)} %collective-permute-done.5) | copy-start | bytes 353284
  37.9 10.1 %copy-start.19 = (bf16[40,1472]{1,0:T(8,128)(2,1)}, bf16[40,1472]{1,0:T(8,128)(2,1)S(1)}, u32[]{:S(2)}) copy-start(bf16[40,1472]{1,0:T(8,128)(2,1)S(1)} %collective-permute-done.6) | copy-start | bytes 353284
  43.3 4.7 %copy-start.20 = (bf16[40,1472]{1,0:T(8,128)(2,1)}, bf16[40,1472]{1,0:T(8,128)(2,1)S(1)}, u32[]{:S(2)}) copy-start(bf16[40,1472]{1,0:T(8,128)(2,1)S(1)} %collective-permute-done.7) | copy-start | bytes 353284
  47.1 0.9 copy-start.21
  47.9 31.2 %copy-start.22 = (bf16[40,1472]{1,0:T(8,128)(2,1)}, bf16[40,1472]{1,0:T(8,128)(2,1)S(1)}, u32[]{:S(2)}) copy-start(bf16[40,1472]{1,0:T(8,128)(2,1)S(1)} %collective-permute-done.9) | copy-start | bytes 353284
  47.9 38.9 %copy-start.6 = (bf16[160,896]{1,0:T(8,128)(2,1)}, bf16[160,896]{1,0:T(8,128)(2,1)S(1)}, u32[]{:S(2)}) copy-start(bf16[160,896]{1,0:T(8,128)(2,1)S(1)} %pad_maximum_fusion.refs_0_) | copy-start | bytes 860164
  48.0 38.8 %copy-start.7 = (bf16[160,896]{1,0:T(8,128)(2,1)}, bf16[160,896]{1,0:T(8,128)(2,1)S(1)}, u32[]{:S(2)}) copy-start(bf16[160,896]{1,0:T(8,128)(2,1)S(1)} %pad_maximum_fusion.1.refs_1_) | copy-start | bytes 860164
  48.0 44.7 %copy-start.1 = (bf16[8,128,896]{2,1,0:T(8,128)(2,1)}, bf16[8,128,896]{2,1,0:T(8,128)(2,1)S(1)}, u32[]{:S(2)}) copy-start(bf16[8,128,896]{2,1,0:T(8,128)(2,1)S(1)} %all-to-all-done.w_ref) | copy-start | bytes 5505028
  48.0 8.6 %collective-permute-start.14 = (bf16[160,896]{1,0:T(8,128)(2,1)S(1)}, bf16[160,896]{1,0:T(8,128)(2,1)S(1)}, u32[]{:S(2)}, u32[]{:S(2)}) collective-permute-start(bf16[160,896]{1,0:T(8,128)(2,1)S(1)} %pad_maximum_fusion.refs_0_), channel_id=1, source_target_pairs={{0,128},{32,160},{64,192},{96,224},{128,0},{160,32},{192,64},{224,... | collective-permute-start | bytes 860168 | tf_op jit(solution)/shard_map/ppermute | solution.py:41
  50.1 10.0 %collective-permute-start.12 = (bf16[160,896]{1,0:T(8,128)(2,1)S(1)}, bf16[160,896]{1,0:T(8,128)(2,1)S(1)}, u32[]{:S(2)}, u32[]{:S(2)}) collective-permute-start(bf16[160,896]{1,0:T(8,128)(2,1)S(1)} %pad_maximum_fusion.refs_0_), channel_id=1, source_target_pairs={{0,96},{32,0},{64,32},{96,64},{128,224},{160,128},{192,160},{224,1... | collective-permute-start | bytes 860168 | tf_op jit(solution)/shard_map/ppermute | solution.py:36
  52.8 11.0 %collective-permute-start.10 = (bf16[160,896]{1,0:T(8,128)(2,1)S(1)}, bf16[160,896]{1,0:T(8,128)(2,1)S(1)}, u32[]{:S(2)}, u32[]{:S(2)}) collective-permute-start(bf16[160,896]{1,0:T(8,128)(2,1)S(1)} %pad_maximum_fusion.refs_0_), channel_id=1, source_target_pairs={{0,32},{32,64},{64,96},{96,0},{128,160},{160,192},{192,224},{224,1... | collective-permute-start | bytes 860168 | tf_op jit(solution)/shard_map/ppermute | solution.py:36
  52.8 13.4 %collective-permute-start.13 = (bf16[160,896]{1,0:T(8,128)(2,1)S(1)}, bf16[160,896]{1,0:T(8,128)(2,1)S(1)}, u32[]{:S(2)}, u32[]{:S(2)}) collective-permute-start(bf16[160,896]{1,0:T(8,128)(2,1)S(1)} %pad_maximum_fusion.1.refs_1_), channel_id=1, source_target_pairs={{0,96},{32,0},{64,32},{96,64},{128,224},{160,128},{192,160},{224,1... | collective-permute-start | bytes 860168 | tf_op jit(solution)/shard_map/ppermute | solution.py:36
  56.0 13.9 %collective-permute-start.15 = (bf16[160,896]{1,0:T(8,128)(2,1)S(1)}, bf16[160,896]{1,0:T(8,128)(2,1)}, u32[]{:S(2)}, u32[]{:S(2)}) collective-permute-start(bf16[160,896]{1,0:T(8,128)(2,1)S(1)} %pad_maximum_fusion.1.refs_1_), channel_id=1, source_target_pairs={{0,128},{32,160},{64,192},{96,224},{128,0},{160,32},{192,64},{224,... | collective-permute-start | bytes 860168 | tf_op jit(solution)/shard_map/ppermute | solution.py:41
  56.6 30.2 %copy-start.10 = (bf16[160,896]{1,0:T(8,128)(2,1)}, bf16[160,896]{1,0:T(8,128)(2,1)S(1)}, u32[]{:S(2)}) copy-start(bf16[160,896]{1,0:T(8,128)(2,1)S(1)} %collective-permute-done.14.refs_6_) | copy-start | bytes 860164
  56.6 13.3 %collective-permute-start.11 = (bf16[160,896]{1,0:T(8,128)(2,1)S(1)}, bf16[160,896]{1,0:T(8,128)(2,1)S(1)}, u32[]{:S(2)}, u32[]{:S(2)}) collective-permute-start(bf16[160,896]{1,0:T(8,128)(2,1)S(1)} %pad_maximum_fusion.1.refs_1_), channel_id=1, source_target_pairs={{0,32},{32,64},{64,96},{96,0},{128,160},{160,192},{192,224},{224,1... | collective-permute-start | bytes 860168 | tf_op jit(solution)/shard_map/ppermute | solution.py:36
  60.1 13.1 %copy-start.11 = (bf16[160,896]{1,0:T(8,128)(2,1)}, bf16[160,896]{1,0:T(8,128)(2,1)S(1)}, u32[]{:S(2)}) copy-start(bf16[160,896]{1,0:T(8,128)(2,1)S(1)} %collective-permute-done.12.refs_4_) | copy-start | bytes 860164
  60.1 13.1 %collective-permute-start.20 = (bf16[160,896]{1,0:T(8,128)(2,1)S(1)}, bf16[160,896]{1,0:T(8,128)(2,1)S(1)}, u32[]{:S(2)}, u32[]{:S(2)}) collective-permute-start(bf16[160,896]{1,0:T(8,128)(2,1)S(1)} %collective-permute-done.14.refs_6_), channel_id=1, source_target_pairs={{0,96},{32,0},{64,32},{96,64},{128,224},{160,128},{192,160},{224,1... | collective-permute-start | bytes 860168 | tf_op jit(solution)/shard_map/ppermute | solution.py:36
  63.8 9.9 %copy-start.12 = (bf16[160,896]{1,0:T(8,128)(2,1)}, bf16[160,896]{1,0:T(8,128)(2,1)S(1)}, u32[]{:S(2)}) copy-start(bf16[160,896]{1,0:T(8,128)(2,1)S(1)} %collective-permute-done.10.refs_2_) | copy-start | bytes 860164
  63.8 12.4 %collective-permute-start.16 = (bf16[160,896]{1,0:T(8,128)(2,1)S(1)}, bf16[160,896]{1,0:T(8,128)(2,1)}, u32[]{:S(2)}, u32[]{:S(2)}) collective-permute-start(bf16[160,896]{1,0:T(8,128)(2,1)S(1)} %collective-permute-done.10.refs_2_), channel_id=1, source_target_pairs={{0,32},{32,64},{64,96},{96,0},{128,160},{160,192},{192,224},{224,1... | collective-permute-start | bytes 860168 | tf_op jit(solution)/shard_map/ppermute | solution.py:36
  66.2 9.9 %copy-start.13 = (bf16[160,896]{1,0:T(8,128)(2,1)}, bf16[160,896]{1,0:T(8,128)(2,1)S(1)}, u32[]{:S(2)}) copy-start(bf16[160,896]{1,0:T(8,128)(2,1)S(1)} %collective-permute-done.13.refs_5_) | copy-start | bytes 860164
  66.2 12.3 %collective-permute-start.17 = (bf16[160,896]{1,0:T(8,128)(2,1)S(1)}, bf16[160,896]{1,0:T(8,128)(2,1)}, u32[]{:S(2)}, u32[]{:S(2)}) collective-permute-start(bf16[160,896]{1,0:T(8,128)(2,1)S(1)} %collective-permute-done.13.refs_5_), channel_id=1, source_target_pairs={{0,96},{32,0},{64,32},{96,64},{128,224},{160,128},{192,160},{224,1... | collective-permute-start | bytes 860168 | tf_op jit(solution)/shard_map/ppermute | solution.py:36
  69.9 12.4 %collective-permute-start.18 = (bf16[160,896]{1,0:T(8,128)(2,1)S(1)}, bf16[160,896]{1,0:T(8,128)(2,1)}, u32[]{:S(2)}, u32[]{:S(2)}) collective-permute-start(bf16[160,896]{1,0:T(8,128)(2,1)S(1)} %collective-permute-done.14.refs_6_), channel_id=1, source_target_pairs={{0,32},{32,64},{64,96},{96,0},{128,160},{160,192},{192,224},{224,1... | collective-permute-start | bytes 860168 | tf_op jit(solution)/shard_map/ppermute | solution.py:36
  69.9 8.6 %copy-start.14 = (bf16[160,896]{1,0:T(8,128)(2,1)}, bf16[160,896]{1,0:T(8,128)(2,1)S(1)}, u32[]{:S(2)}) copy-start(bf16[160,896]{1,0:T(8,128)(2,1)S(1)} %collective-permute-done.11.refs_3_) | copy-start | bytes 860164
  70.0 14.3 %collective-permute-start.21 = (bf16[160,896]{1,0:T(8,128)(2,1)}, bf16[160,896]{1,0:T(8,128)(2,1)}, u32[]{:S(2)}, u32[]{:S(2)}) collective-permute-start(bf16[160,896]{1,0:T(8,128)(2,1)} %collective-permute-done.15.refs_7_), channel_id=1, source_target_pairs={{0,96},{32,0},{64,32},{96,64},{128,224},{160,128},{192,160},{224,1... | collective-permute-start | bytes 860168 | tf_op jit(solution)/shard_map/ppermute | solution.py:36
  73.2 5.3 %copy-start.15 = (bf16[160,896]{1,0:T(8,128)(2,1)}, bf16[160,896]{1,0:T(8,128)(2,1)S(1)}, u32[]{:S(2)}) copy-start(bf16[160,896]{1,0:T(8,128)(2,1)S(1)} %collective-permute-done.20.refs_12_) | copy-start | bytes 860164
  73.2 12.9 %collective-permute-start.19 = (bf16[160,896]{1,0:T(8,128)(2,1)}, bf16[160,896]{1,0:T(8,128)(2,1)}, u32[]{:S(2)}, u32[]{:S(2)}) collective-permute-start(bf16[160,896]{1,0:T(8,128)(2,1)} %collective-permute-done.15.refs_7_), channel_id=1, source_target_pairs={{0,32},{32,64},{64,96},{96,0},{128,160},{160,192},{192,224},{224,1... | collective-permute-start | bytes 860168 | tf_op jit(solution)/shard_map/ppermute | solution.py:36
  76.2 10.0 %collective-permute-start.22 = (bf16[160,896]{1,0:T(8,128)(2,1)}, bf16[160,896]{1,0:T(8,128)(2,1)}, u32[]{:S(2)}, u32[]{:S(2)}) collective-permute-start(bf16[160,896]{1,0:T(8,128)(2,1)} %collective-permute-done.16.refs_8_), channel_id=1, source_target_pairs={{0,128},{32,160},{64,192},{96,224},{128,0},{160,32},{192,64},{224,... | collective-permute-start | bytes 860168 | tf_op jit(solution)/shard_map/ppermute | solution.py:41
  78.5 8.3 %collective-permute-start.23 = (bf16[160,896]{1,0:T(8,128)(2,1)}, bf16[160,896]{1,0:T(8,128)(2,1)}, u32[]{:S(2)}, u32[]{:S(2)}) collective-permute-start(bf16[160,896]{1,0:T(8,128)(2,1)} %collective-permute-done.17.refs_9_), channel_id=1, source_target_pairs={{0,128},{32,160},{64,192},{96,224},{128,0},{160,32},{192,64},{224,... | collective-permute-start | bytes 860168 | tf_op jit(solution)/shard_map/ppermute | solution.py:41
  79.3 13.4 %copy-start.5 = (bf16[256,576]{1,0:T(8,128)(2,1)}, bf16[256,576]{1,0:T(8,128)(2,1)S(1)}, u32[]{:S(2)}) copy-start(bf16[256,576]{1,0:T(8,128)(2,1)S(1)} %copy.27.own_ref) | copy-start | bytes 884740
  79.3 18.4 %copy-start.26 = (s32[16]{0:T(128)S(1)}, s32[16]{0:T(128)}, u32[]{:S(2)}) copy-start(s32[16]{0:T(128)} %unit_ref.1) | copy-start | bytes 196
  79.3 18.4 %copy-start = (s32[8]{0:T(128)S(1)}, s32[8]{0:T(128)}, u32[]{:S(2)}) copy-start(s32[8]{0:T(128)} %constant.85.clone) | copy-start | bytes 100
  82.3 48.8 %collective-permute-start.27 = (bf16[256,576]{1,0:T(8,128)(2,1)S(1)}, bf16[256,576]{1,0:T(8,128)(2,1)}, u32[]{:S(2)}, u32[]{:S(2)}) collective-permute-start(bf16[256,576]{1,0:T(8,128)(2,1)S(1)} %copy.27.own_ref), channel_id=1, source_target_pairs={{0,1},{1,2},{2,3},{3,4},{4,5},{5,6},{6,7},{7,8},{8,9},{9,10},{10,1... | collective-permute-start | bytes 884744 | tf_op jit(solution)/shard_map/ppermute | solution.py:422
  92.7 15.1 %all-to-all-start.1 = ((bf16[8,320,128]{2,1,0:T(8,128)(2,1)}), bf16[8,320,128]{2,1,0:T(8,128)(2,1)S(1)}, u32[]{:S(2)}, u32[]{:S(2)}) async-start(bf16[8,320,128]{2,1,0:T(8,128)(2,1)} %add_blocks.1), calls=%async_computation.1 | async-start | bytes 1310720 | tf_op jit(solution)/shard_map/all_to_all | solution.py:71
  105.8 21.9 %copy-start.3 = (bf16[256,8,576]{0,2,1:T(8,128)(2,1)S(1)}, bf16[256,8,576]{0,2,1:T(8,128)(2,1)}, u32[]{:S(2)}) copy-start(bf16[256,8,576]{0,2,1:T(8,128)(2,1)} %param.11) | copy-start | bytes 7077892
  107.8 0.9 copy-start.2
  112.1 21.7 %all-to-all-start.2 = ((bf16[8,40,896]{2,1,0:T(8,128)(2,1)}), bf16[8,40,896]{2,1,0:T(8,128)(2,1)S(1)}, u32[]{:S(2)}, u32[]{:S(2)}) async-start(bf16[8,40,896]{2,1,0:T(8,128)(2,1)} %down.1), calls=%async_computation.2 | async-start | bytes 1146880 | tf_op jit(solution)/shard_map/all_to_all | solution.py:59
  121.6 0.7 copy-start.16
  123.9 7.3 %copy-start.8 = (bf16[16,8,576]{2,1,0:T(8,128)(2,1)}, bf16[16,8,576]{2,1,0:T(8,128)(2,1)S(1)}, u32[]{:S(2)}) copy-start(bf16[16,8,576]{2,1,0:T(8,128)(2,1)S(1)} %gather_fusion.1) | copy-start | bytes 442372
  123.9 7.3 %collective-permute-start.26 = (bf16[128,576]{1,0:T(8,128)(2,1)S(1)}, bf16[128,576]{1,0:T(8,128)(2,1)}, u32[]{:S(2)}, u32[]{:S(2)}) collective-permute-start(bf16[128,576]{1,0:T(8,128)(2,1)S(1)} %bitcast.18), channel_id=1, source_target_pairs={{0,64},{32,96},{64,0},{96,32},{128,192},{160,224},{192,128},{224,1... | collective-permute-start | bytes 442376 | tf_op jit(solution)/shard_map/ppermute | solution.py:36
  125.6 6.0 %collective-permute-start.25 = (bf16[128,576]{1,0:T(8,128)(2,1)S(1)}, bf16[128,576]{1,0:T(8,128)(2,1)}, u32[]{:S(2)}, u32[]{:S(2)}) collective-permute-start(bf16[128,576]{1,0:T(8,128)(2,1)S(1)} %bitcast.19), channel_id=1, source_target_pairs={{0,96},{32,0},{64,32},{96,64},{128,224},{160,128},{192,160},{224,1... | collective-permute-start | bytes 442376 | tf_op jit(solution)/shard_map/ppermute | solution.py:36
  127.2 6.6 %collective-permute-start.24 = (bf16[128,576]{1,0:T(8,128)(2,1)S(1)}, bf16[128,576]{1,0:T(8,128)(2,1)}, u32[]{:S(2)}, u32[]{:S(2)}) collective-permute-start(bf16[128,576]{1,0:T(8,128)(2,1)S(1)} %bitcast.20), channel_id=1, source_target_pairs={{0,32},{32,64},{64,96},{96,0},{128,160},{160,192},{192,224},{224,1... | collective-permute-start | bytes 442376 | tf_op jit(solution)/shard_map/ppermute | solution.py:36
  133.8 0.8 copy-start.4
  136.9 14.5 %all-to-all-start.3 = ((bf16[4,32,896]{2,1,0:T(8,128)(2,1)}), bf16[4,32,896]{2,1,0:T(8,128)(2,1)S(1)}, u32[]{:S(2)}, u32[]{:S(2)}) async-start(bf16[4,32,896]{2,1,0:T(8,128)(2,1)} %mix.1), calls=%async_computation.3 | async-start | bytes 458752 | tf_op jit(solution)/shard_map/all_to_all | solution.py:65
  152.2 12.5 %all-to-all-start.4 = ((bf16[8,32,896]{2,1,0:T(8,128)(2,1)}), bf16[8,32,896]{2,1,0:T(8,128)(2,1)S(1)}, u32[]{:S(2)}, u32[]{:S(2)}) async-start(bf16[8,32,896]{2,1,0:T(8,128)(2,1)} %broadcast_in_dim.15), calls=%async_computation.4 | async-start | bytes 917504 | tf_op jit(solution)/shard_map/all_to_all | solution.py:71

commit v3 on v2

--- a/solution.py
+++ b/solution.py
@@ -16,16 +16,18 @@
 CAP = 10
 AUX = 128
 AUX_AT = 640
+U_HELD = 4
+REST = 64
 Z_ORDER = (0, 1, 7, 2, 6, 3, 5, 4)
 BLOCK = 64
 
 score_scale = 192.0 ** (-0.5)
 route_scale = 2.5
 
-J_GROUPS = [[z * N_J + j for j in range(N_J)] for z in range(N_Z)]
 Z_GROUPS = [[z * N_J + j for z in range(N_Z)] for j in range(N_J)]
 
 VMEM = pl.BlockSpec(memory_space=pltpu.VMEM)
+ANY = pl.BlockSpec(memory_space=pl.ANY)
 SMEM = pl.BlockSpec(memory_space=pltpu.SMEM)
 
 
@@ -58,12 +60,6 @@
 def over_z(value):
     return lax.all_to_all(
         value, "expert", split_axis=0, concat_axis=0, tiled=True, axis_index_groups=Z_GROUPS
-    )
-
-
-def over_j(value):
-    return lax.all_to_all(
-        value, "expert", split_axis=0, concat_axis=0, tiled=True, axis_index_groups=J_GROUPS
     )
 
 
@@ -177,18 +173,19 @@
     pick = jnp.where(slot[:, None, :] == place, 1.0, 0.0).reshape(rows, total)
     got = jnp.dot(pick.astype(jnp.bfloat16), toks, preferred_element_type=jnp.float32)
     part = toks.shape[1]
-    qk = out_refs[0].shape[1] - part
-    units = [r[count:, :qk].astype(jnp.float32)[0:8] for r in refs]
-    units = units + [jnp.zeros((each - N_J * 8, qk), jnp.float32)]
+    units = [r[count:, :AUX_AT].astype(jnp.float32)[0:8] for r in refs]
+    rests = [u[:, LATENT : LATENT + REST] for u in units]
+    rests = rests + [jnp.zeros((8, LATENT - N_J * REST), jnp.float32)]
+    units = [u[:, :LATENT] for u in units] + [jnp.concatenate(rests, 1)]
     units = jnp.concatenate(units, 0)
     for step, out_ref in enumerate(out_refs):
         rows = jnp.concatenate([got[step * each : (step + 1) * each], units], 1)
         out_ref[...] = rows.astype(jnp.bfloat16)
 
 
-def pack(own_e, messages, part, qk):
+def pack(own_e, messages, part):
     rows = N_J * CAP
-    piece = jax.ShapeDtypeStruct((rows, part + qk), jnp.bfloat16)
+    piece = jax.ShapeDtypeStruct((rows, part + LATENT), jnp.bfloat16)
     table = jax.ShapeDtypeStruct((N_Z, 128), jnp.float32)
     slot, share, *pieces = pl.pallas_call(
         pack_kernel,
@@ -227,18 +224,36 @@
 
 
 def sum_kernel(places, at_ref, *refs):
-    xs, (gate, up, out_ref) = refs[:-3], refs[-3:]
-    rows, part = xs[0].shape
+    count = 2 * len(places)
+    xs, (gate, up, out_ref, x_buf, w_buf, x_sem, w_sem) = refs[:count], refs[count:]
+    half, part = xs[0].shape
+    f = out_ref.shape[2]
     own_x, own_y = at_ref[0] // N_Y, lax.rem(at_ref[0], N_Y)
-    total = None
+    copies = []
     for b, (dx, dy) in enumerate(places):
         block = jnp.bitwise_xor(own_x, dx) * N_Y + lax.rem(own_y + dy, N_Y)
         k = pl.ds(pl.multiple_of(block * part, part), part)
-        weights = jnp.concatenate([gate[0, k], up[0, k]], 1)
-        x = jnp.concatenate([xs[2 * b][...], xs[2 * b + 1][...]], 0)
-        term = jnp.dot(x, weights, preferred_element_type=jnp.float32)
+        mine = [
+            pltpu.make_async_copy(
+                xs[2 * b + h], x_buf.at[b, pl.ds(h * half, half)], x_sem.at[2 * b + h]
+            )
+            for h in range(2)
+        ]
+        mine += [
+            pltpu.make_async_copy(
+                ref.at[0, k], w_buf.at[b, :, pl.ds(i * f, f)], w_sem.at[2 * b + i]
+            )
+            for i, ref in enumerate((gate, up))
+        ]
+        for copy in mine:
+            copy.start()
+        copies.append(mine)
+    total = None
+    for b, mine in enumerate(copies):
+        for copy in mine:
+            copy.wait()
+        term = jnp.dot(x_buf[b], w_buf[b], preferred_element_type=jnp.float32)
         total = term if total is None else total + term
-    f = out_ref.shape[2]
     gate, up = total[:, :f], total[:, f:]
     hidden = (gate / (1.0 + jnp.exp(-gate)) * up).astype(jnp.bfloat16)
     for s in range(out_ref.shape[0]):
@@ -250,24 +265,39 @@
     half, part = blocks[0][2][0].shape
     xs = [x for _, _, halves in blocks for x in halves]
     places = tuple((dx, dy) for dx, dy, _ in blocks)
+    count = len(blocks)
     return pl.pallas_call(
         functools.partial(sum_kernel, places),
         out_shape=jax.ShapeDtypeStruct((N_SECTION, 2 * half, f), jnp.bfloat16),
-        in_specs=[SMEM] + [VMEM] * (len(xs) + 2),
+        in_specs=[SMEM] + [ANY] * (len(xs) + 2),
         out_specs=VMEM,
-        compiler_params=params(),
-        cost_estimate=cost(8 * half * part * f * len(blocks), 10 * 1024 * 1024),
+        scratch_shapes=[
+            pltpu.VMEM((count, 2 * half, part), jnp.bfloat16),
+            pltpu.VMEM((count, part, 2 * f), jnp.bfloat16),
+            pltpu.SemaphoreType.DMA((2 * count,)),
+            pltpu.SemaphoreType.DMA((2 * count,)),
+        ],
+        compiler_params=params(),
+        cost_estimate=cost(8 * half * part * f * count, 10 * 1024 * 1024),
         name="add_blocks",
     )(at, *xs, gate_w, up_w)
 
 
-def down_kernel(e_ref, hid, w_ref, out_ref):
-    total = None
-    for k in range(0, N_SECTION, 2):
-        left = jnp.concatenate([hid[k], hid[k + 1]], 1)
-        right = jnp.concatenate([w_ref[k], w_ref[k + 1]], 0)
-        term = jnp.dot(left, right, preferred_element_type=jnp.float32)
-        total = term if total is None else total + term
+def down_kernel(e_ref, hid, w_ref, out_ref, h_buf, w_buf, h_sem, w_sem):
+    count, _, f = hid.shape
+    copies = []
+    for k in range(count):
+        at = pl.ds(k * f, f)
+        mine = (
+            pltpu.make_async_copy(hid.at[k], h_buf.at[:, at], h_sem.at[k]),
+            pltpu.make_async_copy(w_ref.at[k], w_buf.at[at], w_sem.at[k]),
+        )
+        for copy in mine:
+            copy.start()
+        copies += mine
+    for copy in copies:
+        copy.wait()
+    total = jnp.dot(h_buf[...], w_buf[...], preferred_element_type=jnp.float32)
     each = out_ref.shape[1]
     own_z = e_ref[0] // N_J
     for i, step in enumerate(Z_ORDER):
@@ -276,22 +306,69 @@
 
 
 def down(own_e, hidden, weights):
-    _, rows, f = hidden.shape
+    count, rows, f = hidden.shape
     part = weights.shape[2]
     return pl.pallas_call(
         down_kernel,
         out_shape=jax.ShapeDtypeStruct((N_Z, rows // N_Z, part), jnp.bfloat16),
-        in_specs=[SMEM] + [VMEM] * 2,
+        in_specs=[SMEM] + [ANY] * 2,
         out_specs=VMEM,
+        scratch_shapes=[
+            pltpu.VMEM((rows, count * f), jnp.bfloat16),
+            pltpu.VMEM((count * f, part), jnp.bfloat16),
+            pltpu.SemaphoreType.DMA((count,)),
+            pltpu.SemaphoreType.DMA((count,)),
+        ],
         compiler_params=params(),
         cost_estimate=cost(2 * rows * f * N_SECTION * part, 4 * 1024 * 1024),
         name="down",
     )(own_e, hidden, weights)
 
 
-def mix_kernel(e_ref, slot_ref, share_ref, back_ref, out_ref):
+def units_kernel(e_ref, ids_ref, *refs):
+    pieces, out_ref = refs[:-1], refs[-1]
+    qk = out_ref.shape[1]
+    rows = out_ref.shape[0] // ids_ref.shape[0]
+    held = N_J * rows
+    first = pieces[0].shape[1] - LATENT
+    rest = qk - LATENT
+    units = []
+    for piece in pieces:
+        rows_of = piece[:, first:].astype(jnp.float32)
+        rests = [rows_of[held:, j * rest : (j + 1) * rest] for j in range(N_J)]
+        units.append(jnp.concatenate([rows_of[:held], jnp.concatenate(rests, 0)], 1))
+    units = jnp.concatenate(units, 0).astype(jnp.bfloat16)
+    own_e = e_ref[0]
+    row = lax.broadcasted_iota(jnp.int32, (rows, units.shape[0]), 0)
+    column = lax.broadcasted_iota(jnp.int32, (rows, units.shape[0]), 1)
+    picks = []
+    for i in range(ids_ref.shape[0]):
+        owner = ids_ref[i] // U_HELD
+        step = lax.rem(own_e // N_J + N_Z - owner // N_J, N_Z)
+        place = jnp.int32(0)
+        for k, z_step in enumerate(Z_ORDER):
+            place = place + jnp.where(step == z_step, k, 0)
+        start = (place * N_J + lax.rem(jnp.bitwise_xor(owner, own_e), N_J)) * rows
+        picks.append(jnp.where(column == row + start, 1.0, 0.0))
+    picks = jnp.concatenate(picks, 0).astype(jnp.bfloat16)
+    out_ref[...] = jnp.dot(picks, units, preferred_element_type=jnp.float32).astype(jnp.bfloat16)
+
+
+def select_units(own_e, unit_ids, pieces, qk):
+    return pl.pallas_call(
+        units_kernel,
+        out_shape=jax.ShapeDtypeStruct((unit_ids.shape[0] * 8, qk), jnp.bfloat16),
+        in_specs=[SMEM, SMEM] + [VMEM] * len(pieces),
+        out_specs=VMEM,
+        compiler_params=params(),
+        cost_estimate=cost(1000, 2 * 1024 * 1024),
+        name="select_units",
+    )(own_e, unit_ids, *pieces)
+
+
+def mix_kernel(e_ref, slot_ref, share_ref, back_ref, own_ref, *out_refs):
     rows = back_ref.shape[0]
-    own_z, own_j = e_ref[0] // N_J, lax.rem(e_ref[0], N_J)
+    own_z = e_ref[0] // N_J
 
     def by_z(ref):
         at = [lax.rem(z + N_Z - own_z, N_Z) for z in range(N_Z)]
@@ -308,10 +385,10 @@
     dims = (((0,), (0,)), ((), ()))
     got = lax.dot_general(high, back, dims, preferred_element_type=jnp.float32)
     got = got + lax.dot_general(low, back, dims, preferred_element_type=jnp.float32)
-    count = out_ref.shape[1]
-    for p in range(N_J):
-        rows = got[p * count : (p + 1) * count].astype(jnp.bfloat16)
-        out_ref[jnp.bitwise_xor(own_j, p)] = rows
+    count = own_ref.shape[0]
+    own_ref[...] = got[:count]
+    for p, out_ref in enumerate(out_refs, 1):
+        out_ref[...] = got[p * count : (p + 1) * count].astype(jnp.bfloat16)
 
 
 def mix(own_e, slot, share, back):
@@ -319,9 +396,10 @@
     count = slot.shape[1] // N_J
     return pl.pallas_call(
         mix_kernel,
-        out_shape=jax.ShapeDtypeStruct((N_J, count, part), jnp.bfloat16),
+        out_shape=(jax.ShapeDtypeStruct((count, part), jnp.float32),)
+        + (jax.ShapeDtypeStruct((count, part), jnp.bfloat16),) * (N_J - 1),
         in_specs=[SMEM] + [VMEM] * 3,
-        out_specs=VMEM,
+        out_specs=(VMEM,) * N_J,
         compiler_params=params(),
         cost_estimate=cost(4 * rows * N_J * count * part, rows * part * 4),
         name="mix",
@@ -414,8 +492,7 @@
     at = jnp.stack([own_s, own_e]).astype(jnp.int32)
     tok_count, width = tokens_b.shape
     part = width // N_SECTION
-    held, unit_len, qk = cache_latent.shape
-    cut = unit_len // N_Y
+    qk = cache_latent.shape[2]
 
     message = prep(at, unit_ids, tokens_b, expert_ids, affinity, cache_latent)
     messages = (message,) + tuple(across_j(message, bit) for bit in (1, 2, 3))
@@ -427,14 +504,12 @@
     down_all = over_section(after(down_cut, *messages))
 
     own_e = own_e[None].astype(jnp.int32)
-    pieces, slot, share = pack(own_e, messages, part, qk)
-    pieces = [piece if step == 0 else along_z(piece, step) for step, piece in enumerate(pieces)]
-    pieces = [pieces[step] for step in Z_ORDER]
+    pieces, slot, share = pack(own_e, messages, part)
+    pieces = [along_z(pieces[step], step) if step else pieces[step] for step in Z_ORDER]
     first, second = (
         jnp.concatenate([piece[:, :part] for piece in pieces[i : i + 4]], 0) for i in (0, 4)
     )
-    units = [piece[: N_J * cut, part:] for piece in pieces]
-    first, second = lax.optimization_barrier((first, second, down_all))[:2]
+    second = after(second, down_all)
 
     before_1 = along_y(first, 1)
     after_2 = along_y(second, -1)
@@ -460,26 +535,24 @@
     ]
     hidden = over_section(add_blocks(at, blocks, gate_w, up_w))
 
-    owner = unit_ids // held
-    steps = (own_e // N_J - owner // N_J) % N_Z
-    steps = jnp.array([Z_ORDER.index(step) for step in range(N_Z)], jnp.int32)[steps]
-    order = steps * N_J + ((owner ^ own_e) % N_J)
-    units = list(lax.optimization_barrier((*units, hidden))[:-1])
-    units = jnp.concatenate(units, 0).reshape(N_Z * N_J, cut, qk)[order].reshape(-1, qk)
+    units = select_units(own_e, unit_ids, pieces, qk)
+    hidden, rows_q, units = lax.optimization_barrier(
+        (hidden, queries.reshape(-1, qk), units)
+    )
     unit_rows = (units, along_y(units, 1), along_y(units, -1), along_y(units, 2))
     back = over_z(down(own_e, hidden, down_all)).reshape(-1, part)
 
     keys = (previous, group_latent, unit_rows)
     half = group_latent.shape[0] // BLOCK // 2
-    back, rows_q, *_ = lax.optimization_barrier(
-        (back, queries.reshape(-1, qk), unit_rows, previous)
-    )
+    back, *_ = lax.optimization_barrier((back, unit_rows, previous))
     context = attend(at[1:], after(rows_q, back), *keys, 0, half)
-    mixed = over_j(mix(own_e, slot, share, back))
-    mixed, context = lax.optimization_barrier((mixed, context))
-    out_part = jnp.sum(mixed.astype(jnp.float32), 0).astype(jnp.bfloat16)
+    kept, *passed = mix(own_e, slot, share, back)
+    passed = [across_j(value, bit) for bit, value in enumerate(passed, 1)]
+    passed, context = lax.optimization_barrier((passed, context))
+    out_part = kept + sum(value.astype(jnp.float32) for value in passed)
+    out_part = out_part.astype(jnp.bfloat16)
     out_part = jnp.broadcast_to(out_part[None], (N_SECTION, tok_count, part))
-    context = attend(at[1:], after(rows_q, mixed), *keys, half, half, context)
+    context = attend(at[1:], after(rows_q, *passed), *keys, half, half, context)
     context = context.reshape(queries.shape[0], queries.shape[1], LATENT)
     moe_out = over_section(out_part).transpose(1, 0, 2).reshape(tok_count, width)
     return (context, moe_out)

time: 167 us -> 156 us (0.934)
  local copies, waits for them, and re-layouts: 20.7 us -> 10.8 us
  starting transfers between devices: 75.7 us -> 72.2 us
  Pallas kernels: 31.2 us -> 34.3 us
  waiting for transfers between devices: 36.1 us -> 34.2 us
    slice x8 -> x0, local copies, waits for them, and re-layouts: 7.32 us -> none  [per_device(): units = [piece[:N_J * cut, part:] for piece in pieces]]
    all_to_all x1 -> x0, starting transfers between devices: 7.32 us -> none  [over_j(): lax.all_to_all(value, 'expert', split_axis=0, concat_axis=0, tiled=True,...]
    ppermute x7, waiting for transfers between devices: 11.5 us -> 4.87 us  [along_z(): lax.ppermute(value, 'expert', [(e, (e + steps * N_J) % N_EXPERT) for e in...]
    ppermute x1, waiting for transfers between devices: 0.01 us -> 6.33 us  [per_device(): lax.ppermute(group_latent, 'expert', [(i, i + 1) for i in range(N_EXPERT...]
    ppermute x13, starting transfers between devices: 24.1 us -> 20.3 us  [along_y(): return lax.ppermute(value, 'section', pairs)]
    ppermute x3 -> x6, starting transfers between devices: 3.37 us -> 6.74 us  [across_j(): lax.ppermute(value, 'expert', [(e, e ^ bit) for e in range(N_EXPERT)])]
    ppermute x4, starting transfers between devices: 3.6 us -> 6.58 us  [across_x(): return lax.ppermute(value, 'section', pairs)]
    pallas_call x1 -> x2, Pallas kernels: 2.25 us -> 4.65 us  [the longest x1 2.4 us: select_units(): pl.pallas_call(units_kernel, out_shape=jax.ShapeDtypeStruct((unit_ids.sha...]
  transfers between devices with their start and end apart: 33 -> 35, of which waited for: 18 -> 15; matrix products, arithmetic and copies ran while one was open for 10% -> 4% of each run, Pallas kernels for 16% -> 13%
where the time goes in v3:
time: 156 us; the launch traced here: 153 us
  starting transfers between devices  72.2 us (46%)
  Pallas kernels  34.3 us (22%)
  waiting for transfers between devices  34.2 us (22%)
  local copies, waits for them, and re-layouts  10.8 us (7%)
    ppermute x13, starting transfers between devices, along_y(): return lax.ppermute(value, 'section', pairs)  20.3 us
    ppermute x7, starting transfers between devices, along_z(): lax.ppermute(value, 'expert', [(e, (e + steps * N_J) % N_EXPERT) for e in...  15.5 us
    ppermute x13, waiting for transfers between devices, along_y(): return lax.ppermute(value, 'section', pairs)  15.1 us
    pallas_call x2, Pallas kernels, attend(): pl.pallas_call(functools.partial(attend_kernel, first_step), grid_spec=pl...  12.1 us
    all_to_all x3, starting transfers between devices, over_section(): lax.all_to_all(value, 'section', split_axis=0, concat_axis=0, tiled=True)  11.7 us
    all_to_all x1, starting transfers between devices, over_z(): lax.all_to_all(value, 'expert', split_axis=0, concat_axis=0, tiled=True,...  9.45 us
    unnamed x70, local copies, waits for them, and re-layouts  8.29 us
    ppermute x6, starting transfers between devices, across_j(): lax.ppermute(value, 'expert', [(e, e ^ bit) for e in range(N_EXPERT)])  6.74 us
  transfers between devices with their start and end apart: 35, of which 15 were waited for; matrix products, arithmetic and copies ran while one was open for 4% of the time, Pallas kernels for 13%

profile of v3, /device:TPU:64, one launch (start us, length us, event | category | flops | bytes accessed | tf_op | source)
XLA Modules:
  0.0 153.4 jit_solution(13663958097957130084)
XLA Ops:
  0.6 0.6 pad_add_fusion.at_ref
  1.3 2.4 %prep.1.m_ref = bf16[48,896]{1,0:T(8,128)(2,1)} custom-call(s32[2]{0:T(128)} %pad_add_fusion.at_ref, s32[16]{0:T(128)} %ids_ref.1, bf16[32,7168]{1,0:T(8,128)(2,1)} %tok_ref.1, s32[8,32]{1,0:T(8,128)} %bitcast.16, f32[8,32]{1,0:T(8,128)} %bitcast.17, bf16[4,32,576]{2,1,0:T(8,128)(2,1)} %cache_ref.1), custom_call_target="tpu_custom_call" | custom-call | flops 1000 | bytes 409600 | tf_op jit(solution)/shard_map/prep/pallas_call | solution.py:130
  3.7 2.5 %collective-permute-start.2 = (bf16[48,896]{1,0:T(8,128)(2,1)}, bf16[48,896]{1,0:T(8,128)(2,1)S(1)}, u32[]{:S(2)}, u32[]{:S(2)}) collective-permute-start(bf16[48,896]{1,0:T(8,128)(2,1)} %prep.1.m_ref), channel_id=1, source_target_pairs={{0,3},{1,2},{2,1},{3,0},{4,7},{5,6},{6,5},{7,4},{8,11},{9,10},{10,... | collective-permute-start | bytes 258056 | tf_op jit(solution)/shard_map/ppermute | solution.py:51
  6.2 0.6 collective-permute-start.1
  6.8 0.3 collective-permute-start
  7.1 2.9 %cut_down.1 = bf16[8,128,896]{2,1,0:T(8,128)(2,1)} custom-call(bf16[1,128,7168]{2,1,0:T(8,128)(2,1)} %in_ref), custom_call_target="tpu_custom_call" | custom-call | bytes 3670016 | tf_op jit(solution)/shard_map/cut_down/pallas_call | solution.py:211
  9.9 0.2 collective-permute-done.2.xc_ref
  10.2 2.8 %collective-permute-done.1.x_ref = bf16[48,896]{1,0:T(8,128)(2,1)S(1)} collective-permute-done((bf16[48,896]{1,0:T(8,128)(2,1)}, bf16[48,896]{1,0:T(8,128)(2,1)S(1)}, u32[]{:S(2)}, u32[]{:S(2)}) %collective-permute-start.1) | collective-permute-done | bytes 86048 | tf_op jit(solution)/shard_map/ppermute | solution.py:51
  13.0 0.6 copy-done.32
  13.7 4.5 %all-to-all-start = ((bf16[8,128,896]{2,1,0:T(8,128)(2,1)}), bf16[8,128,896]{2,1,0:T(8,128)(2,1)S(1)}, u32[]{:S(2)}, u32[]{:S(2)}) async-start(bf16[8,128,896]{2,1,0:T(8,128)(2,1)} %cut_down.1), calls=%async_computation | async-start | bytes 3670016 | tf_op jit(solution)/shard_map/all_to_all | solution.py:67
  18.2 2.3 %pack.1 = (f32[8,128]{1,0:T(8,128)}, f32[8,128]{1,0:T(8,128)}, bf16[40,1408]{1,0:T(8,128)(2,1)}, bf16[40,1408]{1,0:T(8,128)(2,1)}, bf16[40,1408]{1,0:T(8,128)(2,...) custom-call(s32[1]{0:T(128)} %bitcast.e_ref.s_ref, ...), custom_call_target="tpu_custom_call" | custom-call | flops 73400320 | bytes 1146880 | tf_op jit(solution)/shard_map/pack/pallas_call | solution.py:190
  20.5 1.9 %collective-permute-start.3 = (bf16[40,1408]{1,0:T(8,128)(2,1)}, bf16[40,1408]{1,0:T(8,128)(2,1)S(1)}, u32[]{:S(2)}, u32[]{:S(2)}) collective-permute-start(bf16[40,1408]{1,0:T(8,128)(2,1)} %get-tuple-element.30), channel_id=1, source_target_pairs={{0,4},{1,5},{2,6},{3,7},{4,8},{5,9},{6,10},{7,11},{8,12},{9,13},{1... | collective-permute-start | bytes 337928 | tf_op jit(solution)/shard_map/ppermute | solution.py:55
  22.4 0.1 collective-permute-start.4
  22.5 5.7 %collective-permute-start.5 = (bf16[40,1408]{1,0:T(8,128)(2,1)}, bf16[40,1408]{1,0:T(8,128)(2,1)S(1)}, u32[]{:S(2)}, u32[]{:S(2)}) collective-permute-start(bf16[40,1408]{1,0:T(8,128)(2,1)} %get-tuple-element.32), channel_id=1, source_target_pairs={{0,8},{1,9},{2,10},{3,11},{4,12},{5,13},{6,14},{7,15},{8,16},{9,17... | collective-permute-start | bytes 337928 | tf_op jit(solution)/shard_map/ppermute | solution.py:55
  28.2 0.9 slice.24
  29.1 3.4 %collective-permute-start.7 = (bf16[40,1408]{1,0:T(8,128)(2,1)}, bf16[40,1408]{1,0:T(8,128)(2,1)S(1)}, u32[]{:S(2)}, u32[]{:S(2)}) collective-permute-start(bf16[40,1408]{1,0:T(8,128)(2,1)} %get-tuple-element.34), channel_id=1, source_target_pairs={{0,12},{1,13},{2,14},{3,15},{4,16},{5,17},{6,18},{7,19},{8,20},{9,... | collective-permute-start | bytes 337928 | tf_op jit(solution)/shard_map/ppermute | solution.py:55
  32.5 1.7 %collective-permute-start.8 = (bf16[40,1408]{1,0:T(8,128)(2,1)}, bf16[40,1408]{1,0:T(8,128)(2,1)S(1)}, u32[]{:S(2)}, u32[]{:S(2)}) collective-permute-start(bf16[40,1408]{1,0:T(8,128)(2,1)} %get-tuple-element.35), channel_id=1, source_target_pairs={{0,20},{1,21},{2,22},{3,23},{4,24},{5,25},{6,26},{7,27},{8,28},{9,... | collective-permute-start | bytes 337928 | tf_op jit(solution)/shard_map/ppermute | solution.py:55
  34.3 2.6 %collective-permute-start.9 = (bf16[40,1408]{1,0:T(8,128)(2,1)}, bf16[40,1408]{1,0:T(8,128)(2,1)S(1)}, u32[]{:S(2)}, u32[]{:S(2)}) collective-permute-start(bf16[40,1408]{1,0:T(8,128)(2,1)} %get-tuple-element.36), channel_id=1, source_target_pairs={{0,16},{1,17},{2,18},{3,19},{4,20},{5,21},{6,22},{7,23},{8,24},{9,... | collective-permute-start | bytes 337928 | tf_op jit(solution)/shard_map/ppermute | solution.py:55
  37.0 2.1 %collective-permute-start.14 = (bf16[160,896]{1,0:T(8,128)(2,1)S(1)}, bf16[160,896]{1,0:T(8,128)(2,1)S(1)}, u32[]{:S(2)}, u32[]{:S(2)}) collective-permute-start(bf16[160,896]{1,0:T(8,128)(2,1)S(1)} %pad_maximum_fusion.refs_0_), channel_id=1, source_target_pairs={{0,128},{32,160},{64,192},{96,224},{128,0},{160,32},{192,64},{224,... | collective-permute-start | bytes 860168 | tf_op jit(solution)/shard_map/ppermute | solution.py:43
  39.1 1.9 %collective-permute-done.6.refs_4_ = bf16[40,1408]{1,0:T(8,128)(2,1)S(1)} collective-permute-done((bf16[40,1408]{1,0:T(8,128)(2,1)}, bf16[40,1408]{1,0:T(8,128)(2,1)S(1)}, u32[]{:S(2)}, u32[]{:S(2)}) %collective-permute-start.6) | collective-permute-done | bytes 112672 | tf_op jit(solution)/shard_map/ppermute | solution.py:55
  41.0 2.7 %collective-permute-start.12 = (bf16[160,896]{1,0:T(8,128)(2,1)S(1)}, bf16[160,896]{1,0:T(8,128)(2,1)}, u32[]{:S(2)}, u32[]{:S(2)}) collective-permute-start(bf16[160,896]{1,0:T(8,128)(2,1)S(1)} %pad_maximum_fusion.refs_0_), channel_id=1, source_target_pairs={{0,96},{32,0},{64,32},{96,64},{128,224},{160,128},{192,160},{224,1... | collective-permute-start | bytes 860168 | tf_op jit(solution)/shard_map/ppermute | solution.py:38
  43.8 0.1 collective-permute-start.10
  43.9 2.9 %collective-permute-done.8.refs_6_ = bf16[40,1408]{1,0:T(8,128)(2,1)S(1)} collective-permute-done((bf16[40,1408]{1,0:T(8,128)(2,1)}, bf16[40,1408]{1,0:T(8,128)(2,1)S(1)}, u32[]{:S(2)}, u32[]{:S(2)}) %collective-permute-start.8) | collective-permute-done | bytes 112672 | tf_op jit(solution)/shard_map/ppermute | solution.py:55
  46.9 3.3 %collective-permute-start.13 = (bf16[160,896]{1,0:T(8,128)(2,1)S(1)}, bf16[160,896]{1,0:T(8,128)(2,1)S(1)}, u32[]{:S(2)}, u32[]{:S(2)}) collective-permute-start(bf16[160,896]{1,0:T(8,128)(2,1)S(1)} %pad_maximum_fusion.1.refs_1_), channel_id=1, source_target_pairs={{0,96},{32,0},{64,32},{96,64},{128,224},{160,128},{192,160},{224,1... | collective-permute-start | bytes 860168 | tf_op jit(solution)/shard_map/ppermute | solution.py:38
  50.2 1.6 %collective-permute-done.10.refs_2_ = bf16[160,896]{1,0:T(8,128)(2,1)} collective-permute-done((bf16[160,896]{1,0:T(8,128)(2,1)S(1)}, bf16[160,896]{1,0:T(8,128)(2,1)}, u32[]{:S(2)}, u32[]{:S(2)}) %collective-permute-start.10) | collective-permute-done | bytes 286752 | tf_op jit(solution)/shard_map/ppermute | solution.py:38
  51.8 3.2 %collective-permute-start.20 = (bf16[160,896]{1,0:T(8,128)(2,1)S(1)}, bf16[160,896]{1,0:T(8,128)(2,1)S(1)}, u32[]{:S(2)}, u32[]{:S(2)}) collective-permute-start(bf16[160,896]{1,0:T(8,128)(2,1)S(1)} %collective-permute-done.14.refs_6_), channel_id=1, source_target_pairs={{0,96},{32,0},{64,32},{96,64},{128,224},{160,128},{192,160},{224,1... | collective-permute-start | bytes 860168 | tf_op jit(solution)/shard_map/ppermute | solution.py:38
  55.0 1.5 collective-permute-start.15
  56.5 0.9 collective-permute-done.13.refs_5_
  57.4 3.7 %collective-permute-start.17 = (bf16[160,896]{1,0:T(8,128)(2,1)S(1)}, bf16[160,896]{1,0:T(8,128)(2,1)S(1)}, u32[]{:S(2)}, u32[]{:S(2)}) collective-permute-start(bf16[160,896]{1,0:T(8,128)(2,1)S(1)} %collective-permute-done.13.refs_5_), channel_id=1, source_target_pairs={{0,96},{32,0},{64,32},{96,64},{128,224},{160,128},{192,160},{224,1... | collective-permute-start | bytes 860168 | tf_op jit(solution)/shard_map/ppermute | solution.py:38
  61.1 1.4 collective-permute-done.16.refs_8_
  62.6 1.6 %collective-permute-start.22 = (bf16[160,896]{1,0:T(8,128)(2,1)S(1)}, bf16[160,896]{1,0:T(8,128)(2,1)S(1)}, u32[]{:S(2)}, u32[]{:S(2)}) collective-permute-start(bf16[160,896]{1,0:T(8,128)(2,1)S(1)} %collective-permute-done.16.refs_8_), channel_id=1, source_target_pairs={{0,128},{32,160},{64,192},{96,224},{128,0},{160,32},{192,64},{224,... | collective-permute-start | bytes 860168 | tf_op jit(solution)/shard_map/ppermute | solution.py:43
  64.1 0.7 collective-permute-start.11
  64.9 2.5 %collective-permute-start.21 = (bf16[160,896]{1,0:T(8,128)(2,1)S(1)}, bf16[160,896]{1,0:T(8,128)(2,1)S(1)}, u32[]{:S(2)}, u32[]{:S(2)}) collective-permute-start(bf16[160,896]{1,0:T(8,128)(2,1)S(1)} %collective-permute-done.15.refs_7_), channel_id=1, source_target_pairs={{0,96},{32,0},{64,32},{96,64},{128,224},{160,128},{192,160},{224,1... | collective-permute-start | bytes 860168 | tf_op jit(solution)/shard_map/ppermute | solution.py:38
  67.4 2.3 %collective-permute-done.17.refs_9_ = bf16[160,896]{1,0:T(8,128)(2,1)S(1)} collective-permute-done((bf16[160,896]{1,0:T(8,128)(2,1)S(1)}, bf16[160,896]{1,0:T(8,128)(2,1)S(1)}, u32[]{:S(2)}, u32[]{:S(2)}) %collective-permute-start.17) | collective-permute-done | bytes 286752 | tf_op jit(solution)/shard_map/ppermute | solution.py:38
  69.7 1.5 collective-permute-start.23
  71.2 3.9 %collective-permute-done.11.refs_3_ = bf16[160,896]{1,0:T(8,128)(2,1)S(1)} collective-permute-done((bf16[160,896]{1,0:T(8,128)(2,1)S(1)}, bf16[160,896]{1,0:T(8,128)(2,1)S(1)}, u32[]{:S(2)}, u32[]{:S(2)}) %collective-permute-start.11) | collective-permute-done | bytes 286752 | tf_op jit(solution)/shard_map/ppermute | solution.py:38
  75.1 3.1 %collective-permute-done.19.refs_11_ = bf16[160,896]{1,0:T(8,128)(2,1)S(1)} collective-permute-done((bf16[160,896]{1,0:T(8,128)(2,1)S(1)}, bf16[160,896]{1,0:T(8,128)(2,1)S(1)}, u32[]{:S(2)}, u32[]{:S(2)}) %collective-permute-start.19) | collective-permute-done | bytes 286752 | tf_op jit(solution)/shard_map/ppermute | solution.py:38
  78.3 0.7 copy-done.26
  79.1 6.4 %add_blocks.1 = bf16[8,320,128]{2,1,0:T(8,128)(2,1)} custom-call(s32[2]{0:T(128)} %pad_add_fusion.at_ref, bf16[160,896]{1,0:T(8,128)(2,1)} %copy-done.4, bf16[160,896]{1,0:T(8,128)(2,1)} %copy-done.5, bf16[160,896]{1,0:T(8,128)(2,1)} %collective-permute-done.10.refs_2_, bf16[160,896]{1,0:T(8,128)(2,1)} %copy-done.24, ...), custom_call_target="tpu_custom_call" | custom-call | flops 1174405120 | bytes 10485760 | tf_op jit(solution)/shard_map/add_blocks/pallas_call | solution.py:269
  85.5 3.6 %all-to-all-start.1 = ((bf16[8,320,128]{2,1,0:T(8,128)(2,1)}), bf16[8,320,128]{2,1,0:T(8,128)(2,1)S(1)}, u32[]{:S(2)}, u32[]{:S(2)}) async-start(bf16[8,320,128]{2,1,0:T(8,128)(2,1)} %add_blocks.1), calls=%async_computation.1 | async-start | bytes 1310720 | tf_op jit(solution)/shard_map/all_to_all | solution.py:67
  89.1 4.9 %copy.21 = bf16[256,8,576]{2,1,0:T(8,128)(2,1)} copy(bf16[256,8,576]{0,2,1:T(8,128)(2,1)} %param.10) | data formatting | bytes 4718592 | tf_op args[0]
  94.0 2.4 %select_units.1.refs_0_ = bf16[128,576]{1,0:T(8,128)(2,1)} custom-call(s32[1]{0:T(128)} %bitcast.e_ref.s_ref, s32[16]{0:T(128)} %ids_ref.1, bf16[40,1408]{1,0:T(8,128)(2,1)} %get-tuple-element.29.refs_0_, bf16[40,1408]{1,0:T(8,128)(2,1)} %copy-done.8, bf16[40,1408]{1,0:T(8,128)(2,1)} %copy-done.9, bf16[40,1408]{1,0:T(8,128)(2,1)} %copy-done.10, ...), custom_call_target="tpu_custom_call" | custom-call | flops 1000 | bytes 2097152 | tf_op jit(solution)/shard_map/select_units/pallas_call | solution.py:358
  96.4 1.5 all-to-all-done.1.hid
  97.9 0.9 copy-done.1
  98.8 3.6 %down.1 = bf16[8,40,896]{2,1,0:T(8,128)(2,1)} custom-call(s32[1]{0:T(128)} %bitcast.e_ref.s_ref, bf16[8,320,128]{2,1,0:T(8,128)(2,1)} %copy-done.1, bf16[8,128,896]{2,1,0:T(8,128)(2,1)} %copy-done), custom_call_target="tpu_custom_call" | custom-call | flops 587202560 | bytes 4194304 | tf_op jit(solution)/shard_map/down/pallas_call | solution.py:311
  102.4 9.4 %all-to-all-start.2 = ((bf16[8,40,896]{2,1,0:T(8,128)(2,1)}), bf16[8,40,896]{2,1,0:T(8,128)(2,1)S(1)}, u32[]{:S(2)}, u32[]{:S(2)}) async-start(bf16[8,40,896]{2,1,0:T(8,128)(2,1)} %down.1), calls=%async_computation.2 | async-start | bytes 1146880 | tf_op jit(solution)/shard_map/all_to_all | solution.py:61
  111.8 0.2 copy.22.own_ref
  112.1 1.9 %collective-permute-start.27 = (bf16[256,576]{1,0:T(8,128)(2,1)S(1)}, bf16[256,576]{1,0:T(8,128)(2,1)S(1)}, u32[]{:S(2)}, u32[]{:S(2)}) collective-permute-start(bf16[256,576]{1,0:T(8,128)(2,1)S(1)} %copy.22.own_ref), channel_id=1, source_target_pairs={{0,1},{1,2},{2,3},{3,4},{4,5},{5,6},{6,7},{7,8},{8,9},{9,10},{10,1... | collective-permute-start | bytes 884744 | tf_op jit(solution)/shard_map/ppermute | solution.py:499
  114.0 2.1 %collective-permute-start.26 = (bf16[128,576]{1,0:T(8,128)(2,1)S(1)}, bf16[128,576]{1,0:T(8,128)(2,1)S(1)}, u32[]{:S(2)}, u32[]{:S(2)}) collective-permute-start(bf16[128,576]{1,0:T(8,128)(2,1)S(1)} %copy-done.6), channel_id=1, source_target_pairs={{0,64},{32,96},{64,0},{96,32},{128,192},{160,224},{192,128},{224,1... | collective-permute-start | bytes 442376 | tf_op jit(solution)/shard_map/ppermute | solution.py:38
  116.1 1.2 collective-permute-start.25
  117.3 0.8 collective-permute-start.24
  118.1 6.3 %collective-permute-done.27.prev_ref = bf16[256,576]{1,0:T(8,128)(2,1)S(1)} collective-permute-done((bf16[256,576]{1,0:T(8,128)(2,1)S(1)}, bf16[256,576]{1,0:T(8,128)(2,1)S(1)}, u32[]{:S(2)}, u32[]{:S(2)}) %collective-permute-start.27) | collective-permute-done | bytes 294944 | tf_op jit(solution)/shard_map/ppermute | solution.py:499
  124.5 0.7 collective-permute-done.25.refs_2_
  125.2 1.0 collective-permute-done.24.refs_1_
  126.2 0.8 copy-done.2
  127.0 2.2 %mix.1 = (f32[32,896]{1,0:T(8,128)}, bf16[32,896]{1,0:T(8,128)(2,1)}, bf16[32,896]{1,0:T(8,128)(2,1)}, bf16[32,896]{1,0:T(8,128)(2,1)}) custom-call(s32[1]{0:T(128)} %bitcast.e_ref.s_ref, f32[8,128]{1,0:T(8,128)} %get-tuple-element.41.slot_ref, f32[8,128]{1,0:T(8,128)} %get-tuple-element.42.share_ref, bf16[320,896]{1,0:T(8,128)(2,1)} %bitcast.12), custom_call_target="tpu_custom_call" | custom-call | flops 146800640 | bytes 1146880 | tf_op jit(solution)/shard_map/mix/pallas_call | solution.py:397
  129.4 1.7 %collective-permute-start.29 = (bf16[32,896]{1,0:T(8,128)(2,1)}, bf16[32,896]{1,0:T(8,128)(2,1)S(1)}, u32[]{:S(2)}, u32[]{:S(2)}) collective-permute-start(bf16[32,896]{1,0:T(8,128)(2,1)} %get-tuple-element.47), channel_id=1, source_target_pairs={{0,2},{1,3},{2,0},{3,1},{4,6},{5,7},{6,4},{7,5},{8,10},{9,11},{10,... | collective-permute-start | bytes 172040 | tf_op jit(solution)/shard_map/ppermute | solution.py:51
  131.1 1.6 %collective-permute-start.30 = (bf16[32,896]{1,0:T(8,128)(2,1)}, bf16[32,896]{1,0:T(8,128)(2,1)S(1)}, u32[]{:S(2)}, u32[]{:S(2)}) collective-permute-start(bf16[32,896]{1,0:T(8,128)(2,1)} %get-tuple-element.48), channel_id=1, source_target_pairs={{0,3},{1,2},{2,1},{3,0},{4,7},{5,6},{6,5},{7,4},{8,11},{9,10},{10,... | collective-permute-start | bytes 172040 | tf_op jit(solution)/shard_map/ppermute | solution.py:51
  132.7 6.0 %attend.2.refs_4_ = bf16[2048,512]{1,0:T(8,128)(2,1)} custom-call(s32[1]{0:T(128)} %bitcast.e_ref.s_ref, bf16[2048,576]{1,0:T(8,128)(2,1)} %bitcast.10, bf16[256,576]{1,0:T(8,128)(2,1)} %copy-done.7, bf16[256,576]{1,0:T(8,128)(2,1)} %copy-done.3, bf16[128,576]{1,0:T(8,128)(2,1)} %select_units.1.refs_0_, bf16[128,576]{1,0:T(8,128)(2,1)} %copy-done.29, ...), custom_call_target="tpu_custom_call" | custom-call | flops 2000000000 | bytes 4194304 | tf_op jit(solution)/shard_map/attend/pallas_call | solution.py:458
  138.8 0.8 broadcast_in_dim.2
  139.6 3.7 %all-to-all-start.3 = ((bf16[8,32,896]{2,1,0:T(8,128)(2,1)}), bf16[8,32,896]{2,1,0:T(8,128)(2,1)S(1)}, u32[]{:S(2)}, u32[]{:S(2)}) async-start(bf16[8,32,896]{2,1,0:T(8,128)(2,1)} %broadcast_in_dim.2), calls=%async_computation.3 | async-start | bytes 917504 | tf_op jit(solution)/shard_map/all_to_all | solution.py:67
  143.3 6.0 %attend.3 = bf16[2048,512]{1,0:T(8,128)(2,1)} custom-call(s32[1]{0:T(128)} %bitcast.e_ref.s_ref, bf16[2048,576]{1,0:T(8,128)(2,1)} %bitcast.11, bf16[256,576]{1,0:T(8,128)(2,1)} %copy-done.7, bf16[256,576]{1,0:T(8,128)(2,1)} %copy-done.3, bf16[128,576]{1,0:T(8,128)(2,1)} %select_units.1.refs_0_, ...), custom_call_target="tpu_custom_call", output_to_operand_aliasing={{}: (8, {})} | custom-call | flops 2000000000 | bytes 4194304 | tf_op jit(solution)/shard_map/attend/pallas_call | solution.py:458
  149.3 3.3 %all-to-all-done.3 = bf16[8,32,896]{2,1,0:T(8,128)(2,1)S(1)} async-done(((bf16[8,32,896]{2,1,0:T(8,128)(2,1)}), bf16[8,32,896]{2,1,0:T(8,128)(2,1)S(1)}, u32[]{:S(2)}, u32[]{:S(2)}) %all-to-all-start.3) | async-done | bytes 458784 | tf_op jit(solution)/shard_map/all_to_all | solution.py:67
  152.6 0.8 copy.26
  (99 shorter events, 0.4 us)
Async XLA Ops:
  3.7 6.5 %collective-permute-start.2 = (bf16[48,896]{1,0:T(8,128)(2,1)}, bf16[48,896]{1,0:T(8,128)(2,1)S(1)}, u32[]{:S(2)}, u32[]{:S(2)}) collective-permute-start(bf16[48,896]{1,0:T(8,128)(2,1)} %prep.1.m_ref), channel_id=1, source_target_pairs={{0,3},{1,2},{2,1},{3,0},{4,7},{5,6},{6,5},{7,4},{8,11},{9,10},{10,... | collective-permute-start | bytes 258056 | tf_op jit(solution)/shard_map/ppermute | solution.py:51
  6.2 6.8 %collective-permute-start.1 = (bf16[48,896]{1,0:T(8,128)(2,1)}, bf16[48,896]{1,0:T(8,128)(2,1)S(1)}, u32[]{:S(2)}, u32[]{:S(2)}) collective-permute-start(bf16[48,896]{1,0:T(8,128)(2,1)} %prep.1.m_ref), channel_id=1, source_target_pairs={{0,2},{1,3},{2,0},{3,1},{4,6},{5,7},{6,4},{7,5},{8,10},{9,11},{10,... | collective-permute-start | bytes 258056 | tf_op jit(solution)/shard_map/ppermute | solution.py:51
  6.8 6.2 %collective-permute-start = (bf16[48,896]{1,0:T(8,128)(2,1)}, bf16[48,896]{1,0:T(8,128)(2,1)S(1)}, u32[]{:S(2)}, u32[]{:S(2)}) collective-permute-start(bf16[48,896]{1,0:T(8,128)(2,1)} %prep.1.m_ref), channel_id=1, source_target_pairs={{0,1},{1,0},{2,3},{3,2},{4,5},{5,4},{6,7},{7,6},{8,9},{9,8},{10,11... | collective-permute-start | bytes 258056 | tf_op jit(solution)/shard_map/ppermute | solution.py:51
  10.2 2.8 %copy-start.31 = (bf16[48,896]{1,0:T(8,128)(2,1)}, bf16[48,896]{1,0:T(8,128)(2,1)S(1)}, u32[]{:S(2)}) copy-start(bf16[48,896]{1,0:T(8,128)(2,1)S(1)} %collective-permute-done.2.xc_ref) | copy-start | bytes 258052
  13.7 33.2 %all-to-all-start = ((bf16[8,128,896]{2,1,0:T(8,128)(2,1)}), bf16[8,128,896]{2,1,0:T(8,128)(2,1)S(1)}, u32[]{:S(2)}, u32[]{:S(2)}) async-start(bf16[8,128,896]{2,1,0:T(8,128)(2,1)} %cut_down.1), calls=%async_computation | async-start | bytes 3670016 | tf_op jit(solution)/shard_map/all_to_all | solution.py:67
  20.5 12.0 %collective-permute-start.3 = (bf16[40,1408]{1,0:T(8,128)(2,1)}, bf16[40,1408]{1,0:T(8,128)(2,1)S(1)}, u32[]{:S(2)}, u32[]{:S(2)}) collective-permute-start(bf16[40,1408]{1,0:T(8,128)(2,1)} %get-tuple-element.30), channel_id=1, source_target_pairs={{0,4},{1,5},{2,6},{3,7},{4,8},{5,9},{6,10},{7,11},{8,12},{9,13},{1... | collective-permute-start | bytes 337928 | tf_op jit(solution)/shard_map/ppermute | solution.py:55
  22.4 11.8 %collective-permute-start.4 = (bf16[40,1408]{1,0:T(8,128)(2,1)}, bf16[40,1408]{1,0:T(8,128)(2,1)S(1)}, u32[]{:S(2)}, u32[]{:S(2)}) collective-permute-start(bf16[40,1408]{1,0:T(8,128)(2,1)} %get-tuple-element.31), channel_id=1, source_target_pairs={{0,28},{1,29},{2,30},{3,31},{4,0},{5,1},{6,2},{7,3},{8,4},{9,5},{1... | collective-permute-start | bytes 337928 | tf_op jit(solution)/shard_map/ppermute | solution.py:55
  22.5 14.4 %collective-permute-start.5 = (bf16[40,1408]{1,0:T(8,128)(2,1)}, bf16[40,1408]{1,0:T(8,128)(2,1)S(1)}, u32[]{:S(2)}, u32[]{:S(2)}) collective-permute-start(bf16[40,1408]{1,0:T(8,128)(2,1)} %get-tuple-element.32), channel_id=1, source_target_pairs={{0,8},{1,9},{2,10},{3,11},{4,12},{5,13},{6,14},{7,15},{8,16},{9,17... | collective-permute-start | bytes 337928 | tf_op jit(solution)/shard_map/ppermute | solution.py:55
  29.1 11.9 %collective-permute-start.6 = (bf16[40,1408]{1,0:T(8,128)(2,1)}, bf16[40,1408]{1,0:T(8,128)(2,1)S(1)}, u32[]{:S(2)}, u32[]{:S(2)}) collective-permute-start(bf16[40,1408]{1,0:T(8,128)(2,1)} %get-tuple-element.33), channel_id=1, source_target_pairs={{0,24},{1,25},{2,26},{3,27},{4,28},{5,29},{6,30},{7,31},{8,0},{9,1... | collective-permute-start | bytes 337928 | tf_op jit(solution)/shard_map/ppermute | solution.py:55
  29.1 14.6 %collective-permute-start.7 = (bf16[40,1408]{1,0:T(8,128)(2,1)}, bf16[40,1408]{1,0:T(8,128)(2,1)S(1)}, u32[]{:S(2)}, u32[]{:S(2)}) collective-permute-start(bf16[40,1408]{1,0:T(8,128)(2,1)} %get-tuple-element.34), channel_id=1, source_target_pairs={{0,12},{1,13},{2,14},{3,15},{4,16},{5,17},{6,18},{7,19},{8,20},{9,... | collective-permute-start | bytes 337928 | tf_op jit(solution)/shard_map/ppermute | solution.py:55
  32.5 53.0 %copy-start.8 = (bf16[40,1408]{1,0:T(8,128)(2,1)}, bf16[40,1408]{1,0:T(8,128)(2,1)S(1)}, u32[]{:S(2)}) copy-start(bf16[40,1408]{1,0:T(8,128)(2,1)S(1)} %collective-permute-done.3.refs_1_) | copy-start | bytes 337924
  32.5 14.3 %collective-permute-start.8 = (bf16[40,1408]{1,0:T(8,128)(2,1)}, bf16[40,1408]{1,0:T(8,128)(2,1)S(1)}, u32[]{:S(2)}, u32[]{:S(2)}) collective-permute-start(bf16[40,1408]{1,0:T(8,128)(2,1)} %get-tuple-element.35), channel_id=1, source_target_pairs={{0,20},{1,21},{2,22},{3,23},{4,24},{5,25},{6,26},{7,27},{8,28},{9,... | collective-permute-start | bytes 337928 | tf_op jit(solution)/shard_map/ppermute | solution.py:55
  34.3 51.2 %copy-start.9 = (bf16[40,1408]{1,0:T(8,128)(2,1)}, bf16[40,1408]{1,0:T(8,128)(2,1)S(1)}, u32[]{:S(2)}) copy-start(bf16[40,1408]{1,0:T(8,128)(2,1)S(1)} %collective-permute-done.4.refs_2_) | copy-start | bytes 337924
  34.3 12.5 %collective-permute-start.9 = (bf16[40,1408]{1,0:T(8,128)(2,1)}, bf16[40,1408]{1,0:T(8,128)(2,1)S(1)}, u32[]{:S(2)}, u32[]{:S(2)}) collective-permute-start(bf16[40,1408]{1,0:T(8,128)(2,1)} %get-tuple-element.36), channel_id=1, source_target_pairs={{0,16},{1,17},{2,18},{3,19},{4,20},{5,21},{6,22},{7,23},{8,24},{9,... | collective-permute-start | bytes 337928 | tf_op jit(solution)/shard_map/ppermute | solution.py:55
  36.9 48.6 %copy-start.10 = (bf16[40,1408]{1,0:T(8,128)(2,1)}, bf16[40,1408]{1,0:T(8,128)(2,1)S(1)}, u32[]{:S(2)}) copy-start(bf16[40,1408]{1,0:T(8,128)(2,1)S(1)} %collective-permute-done.5.refs_3_) | copy-start | bytes 337924
  37.0 42.1 %copy-start.4 = (bf16[160,896]{1,0:T(8,128)(2,1)}, bf16[160,896]{1,0:T(8,128)(2,1)S(1)}, u32[]{:S(2)}) copy-start(bf16[160,896]{1,0:T(8,128)(2,1)S(1)} %pad_maximum_fusion.refs_0_) | copy-start | bytes 860164
  37.0 14.8 %collective-permute-start.14 = (bf16[160,896]{1,0:T(8,128)(2,1)S(1)}, bf16[160,896]{1,0:T(8,128)(2,1)S(1)}, u32[]{:S(2)}, u32[]{:S(2)}) collective-permute-start(bf16[160,896]{1,0:T(8,128)(2,1)S(1)} %pad_maximum_fusion.refs_0_), channel_id=1, source_target_pairs={{0,128},{32,160},{64,192},{96,224},{128,0},{160,32},{192,64},{224,... | collective-permute-start | bytes 860168 | tf_op jit(solution)/shard_map/ppermute | solution.py:43
  41.0 44.5 %copy-start.11 = (bf16[40,1408]{1,0:T(8,128)(2,1)}, bf16[40,1408]{1,0:T(8,128)(2,1)S(1)}, u32[]{:S(2)}) copy-start(bf16[40,1408]{1,0:T(8,128)(2,1)S(1)} %collective-permute-done.6.refs_4_) | copy-start | bytes 337924
  41.0 15.5 %collective-permute-start.12 = (bf16[160,896]{1,0:T(8,128)(2,1)S(1)}, bf16[160,896]{1,0:T(8,128)(2,1)}, u32[]{:S(2)}, u32[]{:S(2)}) collective-permute-start(bf16[160,896]{1,0:T(8,128)(2,1)S(1)} %pad_maximum_fusion.refs_0_), channel_id=1, source_target_pairs={{0,96},{32,0},{64,32},{96,64},{128,224},{160,128},{192,160},{224,1... | collective-permute-start | bytes 860168 | tf_op jit(solution)/shard_map/ppermute | solution.py:38
  43.7 41.8 %copy-start.12 = (bf16[40,1408]{1,0:T(8,128)(2,1)}, bf16[40,1408]{1,0:T(8,128)(2,1)S(1)}, u32[]{:S(2)}) copy-start(bf16[40,1408]{1,0:T(8,128)(2,1)S(1)} %collective-permute-done.7.refs_5_) | copy-start | bytes 337924
  43.8 8.0 %collective-permute-start.10 = (bf16[160,896]{1,0:T(8,128)(2,1)S(1)}, bf16[160,896]{1,0:T(8,128)(2,1)}, u32[]{:S(2)}, u32[]{:S(2)}) collective-permute-start(bf16[160,896]{1,0:T(8,128)(2,1)S(1)} %pad_maximum_fusion.refs_0_), channel_id=1, source_target_pairs={{0,32},{32,64},{64,96},{96,0},{128,160},{160,192},{192,224},{224,1... | collective-permute-start | bytes 860168 | tf_op jit(solution)/shard_map/ppermute | solution.py:38
  46.8 38.7 %copy-start.13 = (bf16[40,1408]{1,0:T(8,128)(2,1)}, bf16[40,1408]{1,0:T(8,128)(2,1)S(1)}, u32[]{:S(2)}) copy-start(bf16[40,1408]{1,0:T(8,128)(2,1)S(1)} %collective-permute-done.8.refs_6_) | copy-start | bytes 337924
  46.8 38.7 %copy-start.14 = (bf16[40,1408]{1,0:T(8,128)(2,1)}, bf16[40,1408]{1,0:T(8,128)(2,1)S(1)}, u32[]{:S(2)}) copy-start(bf16[40,1408]{1,0:T(8,128)(2,1)S(1)} %collective-permute-done.9.refs_7_) | copy-start | bytes 337924
  46.9 32.2 %copy-start.5 = (bf16[160,896]{1,0:T(8,128)(2,1)}, bf16[160,896]{1,0:T(8,128)(2,1)S(1)}, u32[]{:S(2)}) copy-start(bf16[160,896]{1,0:T(8,128)(2,1)S(1)} %pad_maximum_fusion.1.refs_1_) | copy-start | bytes 860164
  46.9 38.6 %copy-start = (bf16[8,128,896]{2,1,0:T(8,128)(2,1)}, bf16[8,128,896]{2,1,0:T(8,128)(2,1)S(1)}, u32[]{:S(2)}) copy-start(bf16[8,128,896]{2,1,0:T(8,128)(2,1)S(1)} %all-to-all-done.w_ref) | copy-start | bytes 5505028
  46.9 10.5 %collective-permute-start.13 = (bf16[160,896]{1,0:T(8,128)(2,1)S(1)}, bf16[160,896]{1,0:T(8,128)(2,1)S(1)}, u32[]{:S(2)}, u32[]{:S(2)}) collective-permute-start(bf16[160,896]{1,0:T(8,128)(2,1)S(1)} %pad_maximum_fusion.1.refs_1_), channel_id=1, source_target_pairs={{0,96},{32,0},{64,32},{96,64},{128,224},{160,128},{192,160},{224,1... | collective-permute-start | bytes 860168 | tf_op jit(solution)/shard_map/ppermute | solution.py:38
  51.8 10.8 %collective-permute-start.16 = (bf16[160,896]{1,0:T(8,128)(2,1)}, bf16[160,896]{1,0:T(8,128)(2,1)S(1)}, u32[]{:S(2)}, u32[]{:S(2)}) collective-permute-start(bf16[160,896]{1,0:T(8,128)(2,1)} %collective-permute-done.10.refs_2_), channel_id=1, source_target_pairs={{0,32},{32,64},{64,96},{96,0},{128,160},{160,192},{192,224},{224,1... | collective-permute-start | bytes 860168 | tf_op jit(solution)/shard_map/ppermute | solution.py:38
  51.8 27.2 %copy-start.16 = (bf16[160,896]{1,0:T(8,128)(2,1)}, bf16[160,896]{1,0:T(8,128)(2,1)S(1)}, u32[]{:S(2)}) copy-start(bf16[160,896]{1,0:T(8,128)(2,1)S(1)} %collective-permute-done.14.refs_6_) | copy-start | bytes 860164
  51.8 12.3 %collective-permute-start.20 = (bf16[160,896]{1,0:T(8,128)(2,1)S(1)}, bf16[160,896]{1,0:T(8,128)(2,1)S(1)}, u32[]{:S(2)}, u32[]{:S(2)}) collective-permute-start(bf16[160,896]{1,0:T(8,128)(2,1)S(1)} %collective-permute-done.14.refs_6_), channel_id=1, source_target_pairs={{0,96},{32,0},{64,32},{96,64},{128,224},{160,128},{192,160},{224,1... | collective-permute-start | bytes 860168 | tf_op jit(solution)/shard_map/ppermute | solution.py:38
  55.0 9.8 %collective-permute-start.15 = (bf16[160,896]{1,0:T(8,128)(2,1)S(1)}, bf16[160,896]{1,0:T(8,128)(2,1)S(1)}, u32[]{:S(2)}, u32[]{:S(2)}) collective-permute-start(bf16[160,896]{1,0:T(8,128)(2,1)S(1)} %pad_maximum_fusion.1.refs_1_), channel_id=1, source_target_pairs={{0,128},{32,160},{64,192},{96,224},{128,0},{160,32},{192,64},{224,... | collective-permute-start | bytes 860168 | tf_op jit(solution)/shard_map/ppermute | solution.py:43
  56.5 10.9 %collective-permute-start.18 = (bf16[160,896]{1,0:T(8,128)(2,1)S(1)}, bf16[160,896]{1,0:T(8,128)(2,1)S(1)}, u32[]{:S(2)}, u32[]{:S(2)}) collective-permute-start(bf16[160,896]{1,0:T(8,128)(2,1)S(1)} %collective-permute-done.14.refs_6_), channel_id=1, source_target_pairs={{0,32},{32,64},{64,96},{96,0},{128,160},{160,192},{192,224},{224,1... | collective-permute-start | bytes 860168 | tf_op jit(solution)/shard_map/ppermute | solution.py:38
  57.4 21.6 %copy-start.17 = (bf16[160,896]{1,0:T(8,128)(2,1)}, bf16[160,896]{1,0:T(8,128)(2,1)S(1)}, u32[]{:S(2)}) copy-start(bf16[160,896]{1,0:T(8,128)(2,1)S(1)} %collective-permute-done.13.refs_5_) | copy-start | bytes 860164
  57.4 12.3 %collective-permute-start.17 = (bf16[160,896]{1,0:T(8,128)(2,1)S(1)}, bf16[160,896]{1,0:T(8,128)(2,1)S(1)}, u32[]{:S(2)}, u32[]{:S(2)}) collective-permute-start(bf16[160,896]{1,0:T(8,128)(2,1)S(1)} %collective-permute-done.13.refs_5_), channel_id=1, source_target_pairs={{0,96},{32,0},{64,32},{96,64},{128,224},{160,128},{192,160},{224,1... | collective-permute-start | bytes 860168 | tf_op jit(solution)/shard_map/ppermute | solution.py:38
  62.6 16.5 %copy-start.18 = (bf16[160,896]{1,0:T(8,128)(2,1)}, bf16[160,896]{1,0:T(8,128)(2,1)S(1)}, u32[]{:S(2)}) copy-start(bf16[160,896]{1,0:T(8,128)(2,1)S(1)} %collective-permute-done.16.refs_8_) | copy-start | bytes 860164
  62.6 8.6 %collective-permute-start.22 = (bf16[160,896]{1,0:T(8,128)(2,1)S(1)}, bf16[160,896]{1,0:T(8,128)(2,1)S(1)}, u32[]{:S(2)}, u32[]{:S(2)}) collective-permute-start(bf16[160,896]{1,0:T(8,128)(2,1)S(1)} %collective-permute-done.16.refs_8_), channel_id=1, source_target_pairs={{0,128},{32,160},{64,192},{96,224},{128,0},{160,32},{192,64},{224,... | collective-permute-start | bytes 860168 | tf_op jit(solution)/shard_map/ppermute | solution.py:43
  64.1 11.0 %copy-start.19 = (bf16[160,896]{1,0:T(8,128)(2,1)}, bf16[160,896]{1,0:T(8,128)(2,1)S(1)}, u32[]{:S(2)}) copy-start(bf16[160,896]{1,0:T(8,128)(2,1)S(1)} %collective-permute-done.20.refs_12_) | copy-start | bytes 860164
  64.1 11.0 %collective-permute-start.11 = (bf16[160,896]{1,0:T(8,128)(2,1)S(1)}, bf16[160,896]{1,0:T(8,128)(2,1)S(1)}, u32[]{:S(2)}, u32[]{:S(2)}) collective-permute-start(bf16[160,896]{1,0:T(8,128)(2,1)S(1)} %pad_maximum_fusion.1.refs_1_), channel_id=1, source_target_pairs={{0,32},{32,64},{64,96},{96,0},{128,160},{160,192},{192,224},{224,1... | collective-permute-start | bytes 860168 | tf_op jit(solution)/shard_map/ppermute | solution.py:38
  64.9 10.3 %copy-start.20 = (bf16[160,896]{1,0:T(8,128)(2,1)}, bf16[160,896]{1,0:T(8,128)(2,1)S(1)}, u32[]{:S(2)}) copy-start(bf16[160,896]{1,0:T(8,128)(2,1)S(1)} %collective-permute-done.15.refs_7_) | copy-start | bytes 860164
  64.9 10.3 %collective-permute-start.21 = (bf16[160,896]{1,0:T(8,128)(2,1)S(1)}, bf16[160,896]{1,0:T(8,128)(2,1)S(1)}, u32[]{:S(2)}, u32[]{:S(2)}) collective-permute-start(bf16[160,896]{1,0:T(8,128)(2,1)S(1)} %collective-permute-done.15.refs_7_), channel_id=1, source_target_pairs={{0,96},{32,0},{64,32},{96,64},{128,224},{160,128},{192,160},{224,1... | collective-permute-start | bytes 860168 | tf_op jit(solution)/shard_map/ppermute | solution.py:38
  67.4 10.9 %copy-start.21 = (bf16[160,896]{1,0:T(8,128)(2,1)}, bf16[160,896]{1,0:T(8,128)(2,1)S(1)}, u32[]{:S(2)}) copy-start(bf16[160,896]{1,0:T(8,128)(2,1)S(1)} %collective-permute-done.18.refs_10_) | copy-start | bytes 860164
  67.4 10.9 %collective-permute-start.19 = (bf16[160,896]{1,0:T(8,128)(2,1)S(1)}, bf16[160,896]{1,0:T(8,128)(2,1)S(1)}, u32[]{:S(2)}, u32[]{:S(2)}) collective-permute-start(bf16[160,896]{1,0:T(8,128)(2,1)S(1)} %collective-permute-done.15.refs_7_), channel_id=1, source_target_pairs={{0,32},{32,64},{64,96},{96,0},{128,160},{160,192},{192,224},{224,1... | collective-permute-start | bytes 860168 | tf_op jit(solution)/shard_map/ppermute | solution.py:38
  69.7 8.6 %copy-start.22 = (bf16[160,896]{1,0:T(8,128)(2,1)}, bf16[160,896]{1,0:T(8,128)(2,1)S(1)}, u32[]{:S(2)}) copy-start(bf16[160,896]{1,0:T(8,128)(2,1)S(1)} %collective-permute-done.17.refs_9_) | copy-start | bytes 860164
  69.7 9.3 %collective-permute-start.23 = (bf16[160,896]{1,0:T(8,128)(2,1)S(1)}, bf16[160,896]{1,0:T(8,128)(2,1)}, u32[]{:S(2)}, u32[]{:S(2)}) collective-permute-start(bf16[160,896]{1,0:T(8,128)(2,1)S(1)} %collective-permute-done.17.refs_9_), channel_id=1, source_target_pairs={{0,128},{32,160},{64,192},{96,224},{128,0},{160,32},{192,64},{224,... | collective-permute-start | bytes 860168 | tf_op jit(solution)/shard_map/ppermute | solution.py:43
  71.2 7.1 %copy-start.23 = (bf16[160,896]{1,0:T(8,128)(2,1)}, bf16[160,896]{1,0:T(8,128)(2,1)S(1)}, u32[]{:S(2)}) copy-start(bf16[160,896]{1,0:T(8,128)(2,1)S(1)} %collective-permute-done.22.refs_14_) | copy-start | bytes 860164
  75.1 3.2 %copy-start.24 = (bf16[160,896]{1,0:T(8,128)(2,1)}, bf16[160,896]{1,0:T(8,128)(2,1)S(1)}, u32[]{:S(2)}) copy-start(bf16[160,896]{1,0:T(8,128)(2,1)S(1)} %collective-permute-done.11.refs_3_) | copy-start | bytes 860164
  75.1 3.2 %copy-start.25 = (bf16[160,896]{1,0:T(8,128)(2,1)}, bf16[160,896]{1,0:T(8,128)(2,1)S(1)}, u32[]{:S(2)}) copy-start(bf16[160,896]{1,0:T(8,128)(2,1)S(1)} %collective-permute-done.21.refs_13_) | copy-start | bytes 860164
  85.5 12.4 %all-to-all-start.1 = ((bf16[8,320,128]{2,1,0:T(8,128)(2,1)}), bf16[8,320,128]{2,1,0:T(8,128)(2,1)S(1)}, u32[]{:S(2)}, u32[]{:S(2)}) async-start(bf16[8,320,128]{2,1,0:T(8,128)(2,1)} %add_blocks.1), calls=%async_computation.1 | async-start | bytes 1310720 | tf_op jit(solution)/shard_map/all_to_all | solution.py:67
  98.8 13.1 %copy-start.15 = (bf16[256,576]{0,1:T(8,128)(2,1)S(1)}, bf16[256,576]{0,1:T(8,128)(2,1)}, u32[]{:S(2)}) copy-start(bf16[256,576]{0,1:T(8,128)(2,1)} %param.11) | copy-start | bytes 884740
  98.8 15.2 %copy-start.6 = (bf16[128,576]{1,0:T(8,128)(2,1)S(1)}, bf16[128,576]{1,0:T(8,128)(2,1)}, u32[]{:S(2)}) copy-start(bf16[128,576]{1,0:T(8,128)(2,1)} %select_units.1.refs_0_) | copy-start | bytes 442372
  102.4 23.8 %all-to-all-start.2 = ((bf16[8,40,896]{2,1,0:T(8,128)(2,1)}), bf16[8,40,896]{2,1,0:T(8,128)(2,1)S(1)}, u32[]{:S(2)}, u32[]{:S(2)}) async-start(bf16[8,40,896]{2,1,0:T(8,128)(2,1)} %down.1), calls=%async_computation.2 | async-start | bytes 1146880 | tf_op jit(solution)/shard_map/all_to_all | solution.py:61
  112.1 20.6 %copy-start.3 = (bf16[256,576]{1,0:T(8,128)(2,1)}, bf16[256,576]{1,0:T(8,128)(2,1)S(1)}, u32[]{:S(2)}) copy-start(bf16[256,576]{1,0:T(8,128)(2,1)S(1)} %copy.22.own_ref) | copy-start | bytes 884740
  112.1 12.4 %collective-permute-start.27 = (bf16[256,576]{1,0:T(8,128)(2,1)S(1)}, bf16[256,576]{1,0:T(8,128)(2,1)S(1)}, u32[]{:S(2)}, u32[]{:S(2)}) collective-permute-start(bf16[256,576]{1,0:T(8,128)(2,1)S(1)} %copy.22.own_ref), channel_id=1, source_target_pairs={{0,1},{1,2},{2,3},{3,4},{4,5},{5,6},{6,7},{7,8},{8,9},{9,10},{10,1... | collective-permute-start | bytes 884744 | tf_op jit(solution)/shard_map/ppermute | solution.py:499
  114.0 10.5 %collective-permute-start.26 = (bf16[128,576]{1,0:T(8,128)(2,1)S(1)}, bf16[128,576]{1,0:T(8,128)(2,1)S(1)}, u32[]{:S(2)}, u32[]{:S(2)}) collective-permute-start(bf16[128,576]{1,0:T(8,128)(2,1)S(1)} %copy-done.6), channel_id=1, source_target_pairs={{0,64},{32,96},{64,0},{96,32},{128,192},{160,224},{192,128},{224,1... | collective-permute-start | bytes 442376 | tf_op jit(solution)/shard_map/ppermute | solution.py:38
  116.1 9.1 %collective-permute-start.25 = (bf16[128,576]{1,0:T(8,128)(2,1)S(1)}, bf16[128,576]{1,0:T(8,128)(2,1)S(1)}, u32[]{:S(2)}, u32[]{:S(2)}) collective-permute-start(bf16[128,576]{1,0:T(8,128)(2,1)S(1)} %copy-done.6), channel_id=1, source_target_pairs={{0,96},{32,0},{64,32},{96,64},{128,224},{160,128},{192,160},{224,1... | collective-permute-start | bytes 442376 | tf_op jit(solution)/shard_map/ppermute | solution.py:38
  117.3 8.9 %collective-permute-start.24 = (bf16[128,576]{1,0:T(8,128)(2,1)S(1)}, bf16[128,576]{1,0:T(8,128)(2,1)S(1)}, u32[]{:S(2)}, u32[]{:S(2)}) collective-permute-start(bf16[128,576]{1,0:T(8,128)(2,1)S(1)} %copy-done.6), channel_id=1, source_target_pairs={{0,32},{32,64},{64,96},{96,0},{128,160},{160,192},{192,224},{224,1... | collective-permute-start | bytes 442376 | tf_op jit(solution)/shard_map/ppermute | solution.py:38
  124.5 8.2 %copy-start.7 = (bf16[256,576]{1,0:T(8,128)(2,1)}, bf16[256,576]{1,0:T(8,128)(2,1)S(1)}, u32[]{:S(2)}) copy-start(bf16[256,576]{1,0:T(8,128)(2,1)S(1)} %collective-permute-done.27.prev_ref) | copy-start | bytes 884740
  124.5 8.2 %copy-start.27 = (bf16[128,576]{1,0:T(8,128)(2,1)}, bf16[128,576]{1,0:T(8,128)(2,1)S(1)}, u32[]{:S(2)}) copy-start(bf16[128,576]{1,0:T(8,128)(2,1)S(1)} %collective-permute-done.26.refs_3_) | copy-start | bytes 442372
  125.2 7.5 %copy-start.28 = (bf16[128,576]{1,0:T(8,128)(2,1)}, bf16[128,576]{1,0:T(8,128)(2,1)S(1)}, u32[]{:S(2)}) copy-start(bf16[128,576]{1,0:T(8,128)(2,1)S(1)} %collective-permute-done.25.refs_2_) | copy-start | bytes 442372
  126.2 6.5 %copy-start.29 = (bf16[128,576]{1,0:T(8,128)(2,1)}, bf16[128,576]{1,0:T(8,128)(2,1)S(1)}, u32[]{:S(2)}) copy-start(bf16[128,576]{1,0:T(8,128)(2,1)S(1)} %collective-permute-done.24.refs_1_) | copy-start | bytes 442372
  129.3 9.5 %collective-permute-start.28 = (bf16[32,896]{1,0:T(8,128)(2,1)}, bf16[32,896]{1,0:T(8,128)(2,1)S(1)}, u32[]{:S(2)}, u32[]{:S(2)}) collective-permute-start(bf16[32,896]{1,0:T(8,128)(2,1)} %get-tuple-element.46), channel_id=1, source_target_pairs={{0,1},{1,0},{2,3},{3,2},{4,5},{5,4},{6,7},{7,6},{8,9},{9,8},{10,11... | collective-permute-start | bytes 172040 | tf_op jit(solution)/shard_map/ppermute | solution.py:51
  129.4 9.4 %collective-permute-start.29 = (bf16[32,896]{1,0:T(8,128)(2,1)}, bf16[32,896]{1,0:T(8,128)(2,1)S(1)}, u32[]{:S(2)}, u32[]{:S(2)}) collective-permute-start(bf16[32,896]{1,0:T(8,128)(2,1)} %get-tuple-element.47), channel_id=1, source_target_pairs={{0,2},{1,3},{2,0},{3,1},{4,6},{5,7},{6,4},{7,5},{8,10},{9,11},{10,... | collective-permute-start | bytes 172040 | tf_op jit(solution)/shard_map/ppermute | solution.py:51
  131.1 7.7 %copy-start.30 = (f32[32,896]{1,0:T(8,128)S(1)}, f32[32,896]{1,0:T(8,128)}, u32[]{:S(2)}) copy-start(f32[32,896]{1,0:T(8,128)} %get-tuple-element.55) | copy-start | bytes 344068
  131.1 7.7 %collective-permute-start.30 = (bf16[32,896]{1,0:T(8,128)(2,1)}, bf16[32,896]{1,0:T(8,128)(2,1)S(1)}, u32[]{:S(2)}, u32[]{:S(2)}) collective-permute-start(bf16[32,896]{1,0:T(8,128)(2,1)} %get-tuple-element.48), channel_id=1, source_target_pairs={{0,3},{1,2},{2,1},{3,0},{4,7},{5,6},{6,5},{7,4},{8,11},{9,10},{10,... | collective-permute-start | bytes 172040 | tf_op jit(solution)/shard_map/ppermute | solution.py:51
  139.6 13.0 %all-to-all-start.3 = ((bf16[8,32,896]{2,1,0:T(8,128)(2,1)}), bf16[8,32,896]{2,1,0:T(8,128)(2,1)S(1)}, u32[]{:S(2)}, u32[]{:S(2)}) async-start(bf16[8,32,896]{2,1,0:T(8,128)(2,1)} %broadcast_in_dim.2), calls=%async_computation.3 | async-start | bytes 917504 | tf_op jit(solution)/shard_map/all_to_all | solution.py:67
  (5 other events, 3.7 us)

commit v4 on v3

--- a/solution.py
+++ b/solution.py
@@ -224,36 +224,18 @@
 
 
 def sum_kernel(places, at_ref, *refs):
-    count = 2 * len(places)
-    xs, (gate, up, out_ref, x_buf, w_buf, x_sem, w_sem) = refs[:count], refs[count:]
-    half, part = xs[0].shape
-    f = out_ref.shape[2]
+    xs, (gate, up, out_ref) = refs[:-3], refs[-3:]
+    rows, part = xs[0].shape
     own_x, own_y = at_ref[0] // N_Y, lax.rem(at_ref[0], N_Y)
-    copies = []
+    total = None
     for b, (dx, dy) in enumerate(places):
         block = jnp.bitwise_xor(own_x, dx) * N_Y + lax.rem(own_y + dy, N_Y)
         k = pl.ds(pl.multiple_of(block * part, part), part)
-        mine = [
-            pltpu.make_async_copy(
-                xs[2 * b + h], x_buf.at[b, pl.ds(h * half, half)], x_sem.at[2 * b + h]
-            )
-            for h in range(2)
-        ]
-        mine += [
-            pltpu.make_async_copy(
-                ref.at[0, k], w_buf.at[b, :, pl.ds(i * f, f)], w_sem.at[2 * b + i]
-            )
-            for i, ref in enumerate((gate, up))
-        ]
-        for copy in mine:
-            copy.start()
-        copies.append(mine)
-    total = None
-    for b, mine in enumerate(copies):
-        for copy in mine:
-            copy.wait()
-        term = jnp.dot(x_buf[b], w_buf[b], preferred_element_type=jnp.float32)
+        weights = jnp.concatenate([gate[0, k], up[0, k]], 1)
+        x = jnp.concatenate([xs[2 * b][...], xs[2 * b + 1][...]], 0)
+        term = jnp.dot(x, weights, preferred_element_type=jnp.float32)
         total = term if total is None else total + term
+    f = out_ref.shape[2]
     gate, up = total[:, :f], total[:, f:]
     hidden = (gate / (1.0 + jnp.exp(-gate)) * up).astype(jnp.bfloat16)
     for s in range(out_ref.shape[0]):
@@ -265,20 +247,13 @@
     half, part = blocks[0][2][0].shape
     xs = [x for _, _, halves in blocks for x in halves]
     places = tuple((dx, dy) for dx, dy, _ in blocks)
-    count = len(blocks)
     return pl.pallas_call(
         functools.partial(sum_kernel, places),
         out_shape=jax.ShapeDtypeStruct((N_SECTION, 2 * half, f), jnp.bfloat16),
-        in_specs=[SMEM] + [ANY] * (len(xs) + 2),
+        in_specs=[SMEM] + [VMEM] * (len(xs) + 2),
         out_specs=VMEM,
-        scratch_shapes=[
-            pltpu.VMEM((count, 2 * half, part), jnp.bfloat16),
-            pltpu.VMEM((count, part, 2 * f), jnp.bfloat16),
-            pltpu.SemaphoreType.DMA((2 * count,)),
-            pltpu.SemaphoreType.DMA((2 * count,)),
-        ],
-        compiler_params=params(),
-        cost_estimate=cost(8 * half * part * f * count, 10 * 1024 * 1024),
+        compiler_params=params(),
+        cost_estimate=cost(8 * half * part * f * len(blocks), 10 * 1024 * 1024),
         name="add_blocks",
     )(at, *xs, gate_w, up_w)
 
@@ -543,16 +518,16 @@
     back = over_z(down(own_e, hidden, down_all)).reshape(-1, part)
 
     keys = (previous, group_latent, unit_rows)
-    half = group_latent.shape[0] // BLOCK // 2
+    steps = group_latent.shape[0] // BLOCK
     back, *_ = lax.optimization_barrier((back, unit_rows, previous))
-    context = attend(at[1:], after(rows_q, back), *keys, 0, half)
+    context = attend(at[1:], after(rows_q, back), *keys, 0, 1)
     kept, *passed = mix(own_e, slot, share, back)
     passed = [across_j(value, bit) for bit, value in enumerate(passed, 1)]
     passed, context = lax.optimization_barrier((passed, context))
     out_part = kept + sum(value.astype(jnp.float32) for value in passed)
     out_part = out_part.astype(jnp.bfloat16)
     out_part = jnp.broadcast_to(out_part[None], (N_SECTION, tok_count, part))
-    context = attend(at[1:], after(rows_q, *passed), *keys, half, half, context)
+    context = attend(at[1:], after(rows_q, *passed), *keys, 1, steps - 1, context)
     context = context.reshape(queries.shape[0], queries.shape[1], LATENT)
     moe_out = over_section(out_part).transpose(1, 0, 2).reshape(tok_count, width)
     return (context, moe_out)

time: 156 us -> 154 us (0.987)
  waiting for transfers between devices: 34.2 us -> 32.6 us
    all_to_all x3, waiting for transfers between devices: 4.85 us -> 3.06 us  [over_section(): lax.all_to_all(value, 'section', split_axis=0, concat_axis=0, tiled=True)]
  transfers between devices with their start and end apart: 35 -> 35, of which waited for: 15 -> 16; matrix products, arithmetic and copies ran while one was open for 4% -> 4% of each run, Pallas kernels for 13% -> 13%
where the time goes in v4:
time: 154 us; the launch traced here: 151 us
  starting transfers between devices  72.1 us (47%)
  Pallas kernels  33.8 us (22%)
  waiting for transfers between devices  32.6 us (21%)
  local copies, waits for them, and re-layouts  10.8 us (7%)
    ppermute x13, starting transfers between devices, along_y(): return lax.ppermute(value, 'section', pairs)  20.3 us
    ppermute x7, starting transfers between devices, along_z(): lax.ppermute(value, 'expert', [(e, (e + steps * N_J) % N_EXPERT) for e in...  15.5 us
    ppermute x13, waiting for transfers between devices, along_y(): return lax.ppermute(value, 'section', pairs)  15.1 us
    pallas_call x2, Pallas kernels, attend(): pl.pallas_call(functools.partial(attend_kernel, first_step), grid_spec=pl...  12 us
    all_to_all x3, starting transfers between devices, over_section(): lax.all_to_all(value, 'section', split_axis=0, concat_axis=0, tiled=True)  11.6 us
    all_to_all x1, starting transfers between devices, over_z(): lax.all_to_all(value, 'expert', split_axis=0, concat_axis=0, tiled=True,...  9.45 us
    unnamed x70, local copies, waits for them, and re-layouts  8.29 us
    ppermute x6, starting transfers between devices, across_j(): lax.ppermute(value, 'expert', [(e, e ^ bit) for e in range(N_EXPERT)])  6.73 us
  transfers between devices with their start and end apart: 35, of which 16 were waited for; matrix products, arithmetic and copies ran while one was open for 4% of the time, Pallas kernels for 13%

profile of v4, /device:TPU:64, one launch (start us, length us, event | category | flops | bytes accessed | tf_op | source)
XLA Modules:
  0.0 151.0 jit_solution(10518292278923429667)
XLA Ops:
  0.6 0.6 pad_add_fusion.at_ref
  1.3 2.4 %prep.1.m_ref = bf16[48,896]{1,0:T(8,128)(2,1)} custom-call(s32[2]{0:T(128)} %pad_add_fusion.at_ref, s32[16]{0:T(128)} %ids_ref.1, bf16[32,7168]{1,0:T(8,128)(2,1)} %tok_ref.1, s32[8,32]{1,0:T(8,128)} %bitcast.16, f32[8,32]{1,0:T(8,128)} %bitcast.17, bf16[4,32,576]{2,1,0:T(8,128)(2,1)} %cache_ref.1), custom_call_target="tpu_custom_call" | custom-call | flops 1000 | bytes 409600 | tf_op jit(solution)/shard_map/prep/pallas_call | solution.py:130
  3.7 2.5 %collective-permute-start.2 = (bf16[48,896]{1,0:T(8,128)(2,1)}, bf16[48,896]{1,0:T(8,128)(2,1)S(1)}, u32[]{:S(2)}, u32[]{:S(2)}) collective-permute-start(bf16[48,896]{1,0:T(8,128)(2,1)} %prep.1.m_ref), channel_id=1, source_target_pairs={{0,3},{1,2},{2,1},{3,0},{4,7},{5,6},{6,5},{7,4},{8,11},{9,10},{10,... | collective-permute-start | bytes 258056 | tf_op jit(solution)/shard_map/ppermute | solution.py:51
  6.2 0.6 collective-permute-start.1
  6.8 0.3 collective-permute-start
  7.1 2.9 %cut_down.1 = bf16[8,128,896]{2,1,0:T(8,128)(2,1)} custom-call(bf16[1,128,7168]{2,1,0:T(8,128)(2,1)} %in_ref), custom_call_target="tpu_custom_call" | custom-call | bytes 3670016 | tf_op jit(solution)/shard_map/cut_down/pallas_call | solution.py:211
  9.9 0.2 collective-permute-done.2.xc_ref
  10.2 2.8 %collective-permute-done.1.x_ref = bf16[48,896]{1,0:T(8,128)(2,1)S(1)} collective-permute-done((bf16[48,896]{1,0:T(8,128)(2,1)}, bf16[48,896]{1,0:T(8,128)(2,1)S(1)}, u32[]{:S(2)}, u32[]{:S(2)}) %collective-permute-start.1) | collective-permute-done | bytes 86048 | tf_op jit(solution)/shard_map/ppermute | solution.py:51
  13.0 0.6 copy-done.32
  13.7 4.5 %all-to-all-start = ((bf16[8,128,896]{2,1,0:T(8,128)(2,1)}), bf16[8,128,896]{2,1,0:T(8,128)(2,1)S(1)}, u32[]{:S(2)}, u32[]{:S(2)}) async-start(bf16[8,128,896]{2,1,0:T(8,128)(2,1)} %cut_down.1), calls=%async_computation | async-start | bytes 3670016 | tf_op jit(solution)/shard_map/all_to_all | solution.py:67
  18.2 2.3 %pack.1 = (f32[8,128]{1,0:T(8,128)}, f32[8,128]{1,0:T(8,128)}, bf16[40,1408]{1,0:T(8,128)(2,1)}, bf16[40,1408]{1,0:T(8,128)(2,1)}, bf16[40,1408]{1,0:T(8,128)(2,...) custom-call(s32[1]{0:T(128)} %bitcast.e_ref.s_ref, ...), custom_call_target="tpu_custom_call" | custom-call | flops 73400320 | bytes 1146880 | tf_op jit(solution)/shard_map/pack/pallas_call | solution.py:190
  20.5 1.9 %collective-permute-start.3 = (bf16[40,1408]{1,0:T(8,128)(2,1)}, bf16[40,1408]{1,0:T(8,128)(2,1)S(1)}, u32[]{:S(2)}, u32[]{:S(2)}) collective-permute-start(bf16[40,1408]{1,0:T(8,128)(2,1)} %get-tuple-element.30), channel_id=1, source_target_pairs={{0,4},{1,5},{2,6},{3,7},{4,8},{5,9},{6,10},{7,11},{8,12},{9,13},{1... | collective-permute-start | bytes 337928 | tf_op jit(solution)/shard_map/ppermute | solution.py:55
  22.4 0.1 collective-permute-start.4
  22.5 5.7 %collective-permute-start.5 = (bf16[40,1408]{1,0:T(8,128)(2,1)}, bf16[40,1408]{1,0:T(8,128)(2,1)S(1)}, u32[]{:S(2)}, u32[]{:S(2)}) collective-permute-start(bf16[40,1408]{1,0:T(8,128)(2,1)} %get-tuple-element.32), channel_id=1, source_target_pairs={{0,8},{1,9},{2,10},{3,11},{4,12},{5,13},{6,14},{7,15},{8,16},{9,17... | collective-permute-start | bytes 337928 | tf_op jit(solution)/shard_map/ppermute | solution.py:55
  28.2 0.9 slice.24
  29.1 3.4 %collective-permute-start.7 = (bf16[40,1408]{1,0:T(8,128)(2,1)}, bf16[40,1408]{1,0:T(8,128)(2,1)S(1)}, u32[]{:S(2)}, u32[]{:S(2)}) collective-permute-start(bf16[40,1408]{1,0:T(8,128)(2,1)} %get-tuple-element.34), channel_id=1, source_target_pairs={{0,12},{1,13},{2,14},{3,15},{4,16},{5,17},{6,18},{7,19},{8,20},{9,... | collective-permute-start | bytes 337928 | tf_op jit(solution)/shard_map/ppermute | solution.py:55
  32.5 1.7 %collective-permute-start.8 = (bf16[40,1408]{1,0:T(8,128)(2,1)}, bf16[40,1408]{1,0:T(8,128)(2,1)S(1)}, u32[]{:S(2)}, u32[]{:S(2)}) collective-permute-start(bf16[40,1408]{1,0:T(8,128)(2,1)} %get-tuple-element.35), channel_id=1, source_target_pairs={{0,20},{1,21},{2,22},{3,23},{4,24},{5,25},{6,26},{7,27},{8,28},{9,... | collective-permute-start | bytes 337928 | tf_op jit(solution)/shard_map/ppermute | solution.py:55
  34.3 2.6 %collective-permute-start.9 = (bf16[40,1408]{1,0:T(8,128)(2,1)}, bf16[40,1408]{1,0:T(8,128)(2,1)S(1)}, u32[]{:S(2)}, u32[]{:S(2)}) collective-permute-start(bf16[40,1408]{1,0:T(8,128)(2,1)} %get-tuple-element.36), channel_id=1, source_target_pairs={{0,16},{1,17},{2,18},{3,19},{4,20},{5,21},{6,22},{7,23},{8,24},{9,... | collective-permute-start | bytes 337928 | tf_op jit(solution)/shard_map/ppermute | solution.py:55
  37.0 2.1 %collective-permute-start.14 = (bf16[160,896]{1,0:T(8,128)(2,1)S(1)}, bf16[160,896]{1,0:T(8,128)(2,1)S(1)}, u32[]{:S(2)}, u32[]{:S(2)}) collective-permute-start(bf16[160,896]{1,0:T(8,128)(2,1)S(1)} %pad_maximum_fusion.refs_0_), channel_id=1, source_target_pairs={{0,128},{32,160},{64,192},{96,224},{128,0},{160,32},{192,64},{224,... | collective-permute-start | bytes 860168 | tf_op jit(solution)/shard_map/ppermute | solution.py:43
  39.1 1.9 %collective-permute-done.6.refs_4_ = bf16[40,1408]{1,0:T(8,128)(2,1)S(1)} collective-permute-done((bf16[40,1408]{1,0:T(8,128)(2,1)}, bf16[40,1408]{1,0:T(8,128)(2,1)S(1)}, u32[]{:S(2)}, u32[]{:S(2)}) %collective-permute-start.6) | collective-permute-done | bytes 112672 | tf_op jit(solution)/shard_map/ppermute | solution.py:55
  41.0 2.7 %collective-permute-start.12 = (bf16[160,896]{1,0:T(8,128)(2,1)S(1)}, bf16[160,896]{1,0:T(8,128)(2,1)}, u32[]{:S(2)}, u32[]{:S(2)}) collective-permute-start(bf16[160,896]{1,0:T(8,128)(2,1)S(1)} %pad_maximum_fusion.refs_0_), channel_id=1, source_target_pairs={{0,96},{32,0},{64,32},{96,64},{128,224},{160,128},{192,160},{224,1... | collective-permute-start | bytes 860168 | tf_op jit(solution)/shard_map/ppermute | solution.py:38
  43.9 2.9 %collective-permute-done.8.refs_6_ = bf16[40,1408]{1,0:T(8,128)(2,1)S(1)} collective-permute-done((bf16[40,1408]{1,0:T(8,128)(2,1)}, bf16[40,1408]{1,0:T(8,128)(2,1)S(1)}, u32[]{:S(2)}, u32[]{:S(2)}) %collective-permute-start.8) | collective-permute-done | bytes 112672 | tf_op jit(solution)/shard_map/ppermute | solution.py:55
  46.9 3.3 %collective-permute-start.13 = (bf16[160,896]{1,0:T(8,128)(2,1)S(1)}, bf16[160,896]{1,0:T(8,128)(2,1)S(1)}, u32[]{:S(2)}, u32[]{:S(2)}) collective-permute-start(bf16[160,896]{1,0:T(8,128)(2,1)S(1)} %pad_maximum_fusion.1.refs_1_), channel_id=1, source_target_pairs={{0,96},{32,0},{64,32},{96,64},{128,224},{160,128},{192,160},{224,1... | collective-permute-start | bytes 860168 | tf_op jit(solution)/shard_map/ppermute | solution.py:38
  50.2 1.6 %collective-permute-done.10.refs_2_ = bf16[160,896]{1,0:T(8,128)(2,1)} collective-permute-done((bf16[160,896]{1,0:T(8,128)(2,1)S(1)}, bf16[160,896]{1,0:T(8,128)(2,1)}, u32[]{:S(2)}, u32[]{:S(2)}) %collective-permute-start.10) | collective-permute-done | bytes 286752 | tf_op jit(solution)/shard_map/ppermute | solution.py:38
  51.8 3.2 %collective-permute-start.20 = (bf16[160,896]{1,0:T(8,128)(2,1)S(1)}, bf16[160,896]{1,0:T(8,128)(2,1)S(1)}, u32[]{:S(2)}, u32[]{:S(2)}) collective-permute-start(bf16[160,896]{1,0:T(8,128)(2,1)S(1)} %collective-permute-done.14.refs_6_), channel_id=1, source_target_pairs={{0,96},{32,0},{64,32},{96,64},{128,224},{160,128},{192,160},{224,1... | collective-permute-start | bytes 860168 | tf_op jit(solution)/shard_map/ppermute | solution.py:38
  55.0 1.5 collective-permute-start.15
  56.5 0.9 collective-permute-done.13.refs_5_
  57.4 3.7 %collective-permute-start.17 = (bf16[160,896]{1,0:T(8,128)(2,1)S(1)}, bf16[160,896]{1,0:T(8,128)(2,1)S(1)}, u32[]{:S(2)}, u32[]{:S(2)}) collective-permute-start(bf16[160,896]{1,0:T(8,128)(2,1)S(1)} %collective-permute-done.13.refs_5_), channel_id=1, source_target_pairs={{0,96},{32,0},{64,32},{96,64},{128,224},{160,128},{192,160},{224,1... | collective-permute-start | bytes 860168 | tf_op jit(solution)/shard_map/ppermute | solution.py:38
  61.1 1.4 collective-permute-done.16.refs_8_
  62.6 1.6 %collective-permute-start.22 = (bf16[160,896]{1,0:T(8,128)(2,1)S(1)}, bf16[160,896]{1,0:T(8,128)(2,1)S(1)}, u32[]{:S(2)}, u32[]{:S(2)}) collective-permute-start(bf16[160,896]{1,0:T(8,128)(2,1)S(1)} %collective-permute-done.16.refs_8_), channel_id=1, source_target_pairs={{0,128},{32,160},{64,192},{96,224},{128,0},{160,32},{192,64},{224,... | collective-permute-start | bytes 860168 | tf_op jit(solution)/shard_map/ppermute | solution.py:43
  64.1 0.7 collective-permute-start.11
  64.9 2.5 %collective-permute-start.21 = (bf16[160,896]{1,0:T(8,128)(2,1)S(1)}, bf16[160,896]{1,0:T(8,128)(2,1)S(1)}, u32[]{:S(2)}, u32[]{:S(2)}) collective-permute-start(bf16[160,896]{1,0:T(8,128)(2,1)S(1)} %collective-permute-done.15.refs_7_), channel_id=1, source_target_pairs={{0,96},{32,0},{64,32},{96,64},{128,224},{160,128},{192,160},{224,1... | collective-permute-start | bytes 860168 | tf_op jit(solution)/shard_map/ppermute | solution.py:38
  67.4 2.3 %collective-permute-done.17.refs_9_ = bf16[160,896]{1,0:T(8,128)(2,1)S(1)} collective-permute-done((bf16[160,896]{1,0:T(8,128)(2,1)S(1)}, bf16[160,896]{1,0:T(8,128)(2,1)S(1)}, u32[]{:S(2)}, u32[]{:S(2)}) %collective-permute-start.17) | collective-permute-done | bytes 286752 | tf_op jit(solution)/shard_map/ppermute | solution.py:38
  69.7 1.5 collective-permute-start.23
  71.2 3.9 %collective-permute-done.11.refs_3_ = bf16[160,896]{1,0:T(8,128)(2,1)S(1)} collective-permute-done((bf16[160,896]{1,0:T(8,128)(2,1)S(1)}, bf16[160,896]{1,0:T(8,128)(2,1)S(1)}, u32[]{:S(2)}, u32[]{:S(2)}) %collective-permute-start.11) | collective-permute-done | bytes 286752 | tf_op jit(solution)/shard_map/ppermute | solution.py:38
  75.1 3.1 %collective-permute-done.19.refs_11_ = bf16[160,896]{1,0:T(8,128)(2,1)S(1)} collective-permute-done((bf16[160,896]{1,0:T(8,128)(2,1)S(1)}, bf16[160,896]{1,0:T(8,128)(2,1)S(1)}, u32[]{:S(2)}, u32[]{:S(2)}) %collective-permute-start.19) | collective-permute-done | bytes 286752 | tf_op jit(solution)/shard_map/ppermute | solution.py:38
  78.3 0.7 copy-done.26
  79.1 5.9 %add_blocks.1 = bf16[8,320,128]{2,1,0:T(8,128)(2,1)} custom-call(s32[2]{0:T(128)} %pad_add_fusion.at_ref, bf16[160,896]{1,0:T(8,128)(2,1)} %copy-done.4, bf16[160,896]{1,0:T(8,128)(2,1)} %copy-done.5, bf16[160,896]{1,0:T(8,128)(2,1)} %collective-permute-done.10.refs_2_, bf16[160,896]{1,0:T(8,128)(2,1)} %copy-done.24, ...), custom_call_target="tpu_custom_call" | custom-call | flops 1174405120 | bytes 10485760 | tf_op jit(solution)/shard_map/add_blocks/pallas_call | solution.py:250
  85.0 3.6 %all-to-all-start.1 = ((bf16[8,320,128]{2,1,0:T(8,128)(2,1)}), bf16[8,320,128]{2,1,0:T(8,128)(2,1)S(1)}, u32[]{:S(2)}, u32[]{:S(2)}) async-start(bf16[8,320,128]{2,1,0:T(8,128)(2,1)} %add_blocks.1), calls=%async_computation.1 | async-start | bytes 1310720 | tf_op jit(solution)/shard_map/all_to_all | solution.py:67
  88.6 4.9 %copy.21 = bf16[256,8,576]{2,1,0:T(8,128)(2,1)} copy(bf16[256,8,576]{0,2,1:T(8,128)(2,1)} %param.10) | data formatting | bytes 4718592 | tf_op args[0]
  93.5 2.4 %select_units.1.refs_0_ = bf16[128,576]{1,0:T(8,128)(2,1)} custom-call(s32[1]{0:T(128)} %bitcast.e_ref.s_ref, s32[16]{0:T(128)} %ids_ref.1, bf16[40,1408]{1,0:T(8,128)(2,1)} %get-tuple-element.29.refs_0_, bf16[40,1408]{1,0:T(8,128)(2,1)} %copy-done.8, bf16[40,1408]{1,0:T(8,128)(2,1)} %copy-done.9, bf16[40,1408]{1,0:T(8,128)(2,1)} %copy-done.10, ...), custom_call_target="tpu_custom_call" | custom-call | flops 1000 | bytes 2097152 | tf_op jit(solution)/shard_map/select_units/pallas_call | solution.py:333
  95.9 1.5 %all-to-all-done.1.hid = bf16[8,320,128]{2,1,0:T(8,128)(2,1)S(1)} async-done(((bf16[8,320,128]{2,1,0:T(8,128)(2,1)}), bf16[8,320,128]{2,1,0:T(8,128)(2,1)S(1)}, u32[]{:S(2)}, u32[]{:S(2)}) %all-to-all-start.1) | async-done | bytes 655392 | tf_op jit(solution)/shard_map/all_to_all | solution.py:67
  97.4 0.9 copy-done.1
  98.3 3.6 %down.1 = bf16[8,40,896]{2,1,0:T(8,128)(2,1)} custom-call(s32[1]{0:T(128)} %bitcast.e_ref.s_ref, bf16[8,320,128]{2,1,0:T(8,128)(2,1)} %copy-done.1, bf16[8,128,896]{2,1,0:T(8,128)(2,1)} %copy-done), custom_call_target="tpu_custom_call" | custom-call | flops 587202560 | bytes 4194304 | tf_op jit(solution)/shard_map/down/pallas_call | solution.py:286
  101.9 9.4 %all-to-all-start.2 = ((bf16[8,40,896]{2,1,0:T(8,128)(2,1)}), bf16[8,40,896]{2,1,0:T(8,128)(2,1)S(1)}, u32[]{:S(2)}, u32[]{:S(2)}) async-start(bf16[8,40,896]{2,1,0:T(8,128)(2,1)} %down.1), calls=%async_computation.2 | async-start | bytes 1146880 | tf_op jit(solution)/shard_map/all_to_all | solution.py:61
  111.3 0.2 copy.22.own_ref
  111.5 1.9 %collective-permute-start.27 = (bf16[256,576]{1,0:T(8,128)(2,1)S(1)}, bf16[256,576]{1,0:T(8,128)(2,1)S(1)}, u32[]{:S(2)}, u32[]{:S(2)}) collective-permute-start(bf16[256,576]{1,0:T(8,128)(2,1)S(1)} %copy.22.own_ref), channel_id=1, source_target_pairs={{0,1},{1,2},{2,3},{3,4},{4,5},{5,6},{6,7},{7,8},{8,9},{9,10},{10,1... | collective-permute-start | bytes 884744 | tf_op jit(solution)/shard_map/ppermute | solution.py:474
  113.5 2.1 %collective-permute-start.26 = (bf16[128,576]{1,0:T(8,128)(2,1)S(1)}, bf16[128,576]{1,0:T(8,128)(2,1)S(1)}, u32[]{:S(2)}, u32[]{:S(2)}) collective-permute-start(bf16[128,576]{1,0:T(8,128)(2,1)S(1)} %copy-done.6), channel_id=1, source_target_pairs={{0,64},{32,96},{64,0},{96,32},{128,192},{160,224},{192,128},{224,1... | collective-permute-start | bytes 442376 | tf_op jit(solution)/shard_map/ppermute | solution.py:38
  115.6 1.2 collective-permute-start.25
  116.8 0.8 collective-permute-start.24
  117.6 6.3 %collective-permute-done.27.prev_ref = bf16[256,576]{1,0:T(8,128)(2,1)S(1)} collective-permute-done((bf16[256,576]{1,0:T(8,128)(2,1)S(1)}, bf16[256,576]{1,0:T(8,128)(2,1)S(1)}, u32[]{:S(2)}, u32[]{:S(2)}) %collective-permute-start.27) | collective-permute-done | bytes 294944 | tf_op jit(solution)/shard_map/ppermute | solution.py:474
  123.9 0.7 collective-permute-done.25.refs_2_
  124.6 1.0 collective-permute-done.24.refs_1_
  125.7 0.8 copy-done.2
  126.5 2.2 %mix.1 = (f32[32,896]{1,0:T(8,128)}, bf16[32,896]{1,0:T(8,128)(2,1)}, bf16[32,896]{1,0:T(8,128)(2,1)}, bf16[32,896]{1,0:T(8,128)(2,1)}) custom-call(s32[1]{0:T(128)} %bitcast.e_ref.s_ref, f32[8,128]{1,0:T(8,128)} %get-tuple-element.41.slot_ref, f32[8,128]{1,0:T(8,128)} %get-tuple-element.42.share_ref, bf16[320,896]{1,0:T(8,128)(2,1)} %bitcast.12), custom_call_target="tpu_custom_call" | custom-call | flops 146800640 | bytes 1146880 | tf_op jit(solution)/shard_map/mix/pallas_call | solution.py:372
  128.8 1.7 %collective-permute-start.29 = (bf16[32,896]{1,0:T(8,128)(2,1)}, bf16[32,896]{1,0:T(8,128)(2,1)S(1)}, u32[]{:S(2)}, u32[]{:S(2)}) collective-permute-start(bf16[32,896]{1,0:T(8,128)(2,1)} %get-tuple-element.47), channel_id=1, source_target_pairs={{0,2},{1,3},{2,0},{3,1},{4,6},{5,7},{6,4},{7,5},{8,10},{9,11},{10,... | collective-permute-start | bytes 172040 | tf_op jit(solution)/shard_map/ppermute | solution.py:51
  130.5 1.6 %collective-permute-start.30 = (bf16[32,896]{1,0:T(8,128)(2,1)}, bf16[32,896]{1,0:T(8,128)(2,1)S(1)}, u32[]{:S(2)}, u32[]{:S(2)}) collective-permute-start(bf16[32,896]{1,0:T(8,128)(2,1)} %get-tuple-element.48), channel_id=1, source_target_pairs={{0,3},{1,2},{2,1},{3,0},{4,7},{5,6},{6,5},{7,4},{8,11},{9,10},{10,... | collective-permute-start | bytes 172040 | tf_op jit(solution)/shard_map/ppermute | solution.py:51
  132.1 4.1 %attend.2.refs_4_ = bf16[2048,512]{1,0:T(8,128)(2,1)} custom-call(s32[1]{0:T(128)} %bitcast.e_ref.s_ref, bf16[2048,576]{1,0:T(8,128)(2,1)} %bitcast.10, bf16[256,576]{1,0:T(8,128)(2,1)} %copy-done.7, bf16[256,576]{1,0:T(8,128)(2,1)} %copy-done.3, bf16[128,576]{1,0:T(8,128)(2,1)} %select_units.1.refs_0_, bf16[128,576]{1,0:T(8,128)(2,1)} %copy-done.29, ...), custom_call_target="tpu_custom_call" | custom-call | flops 1000000000 | bytes 2097152 | tf_op jit(solution)/shard_map/attend/pallas_call | solution.py:433
  136.3 0.2 collective-permute-done.30
  136.5 0.8 broadcast_in_dim.2
  137.3 3.5 %all-to-all-start.3 = ((bf16[8,32,896]{2,1,0:T(8,128)(2,1)}), bf16[8,32,896]{2,1,0:T(8,128)(2,1)S(1)}, u32[]{:S(2)}, u32[]{:S(2)}) async-start(bf16[8,32,896]{2,1,0:T(8,128)(2,1)} %broadcast_in_dim.2), calls=%async_computation.3 | async-start | bytes 917504 | tf_op jit(solution)/shard_map/all_to_all | solution.py:67
  140.8 7.9 %attend.3 = bf16[2048,512]{1,0:T(8,128)(2,1)} custom-call(s32[1]{0:T(128)} %bitcast.e_ref.s_ref, bf16[2048,576]{1,0:T(8,128)(2,1)} %bitcast.11, bf16[256,576]{1,0:T(8,128)(2,1)} %copy-done.7, bf16[256,576]{1,0:T(8,128)(2,1)} %copy-done.3, bf16[128,576]{1,0:T(8,128)(2,1)} %select_units.1.refs_0_, ...), custom_call_target="tpu_custom_call", output_to_operand_aliasing={{}: (8, {})} | custom-call | flops 3000000000 | bytes 6291456 | tf_op jit(solution)/shard_map/attend/pallas_call | solution.py:433
  148.7 1.5 %all-to-all-done.3 = bf16[8,32,896]{2,1,0:T(8,128)(2,1)S(1)} async-done(((bf16[8,32,896]{2,1,0:T(8,128)(2,1)}), bf16[8,32,896]{2,1,0:T(8,128)(2,1)S(1)}, u32[]{:S(2)}, u32[]{:S(2)}) %all-to-all-start.3) | async-done | bytes 458784 | tf_op jit(solution)/shard_map/all_to_all | solution.py:67
  150.2 0.8 copy.26
  (99 shorter events, 0.5 us)
Async XLA Ops:
  3.7 6.5 %collective-permute-start.2 = (bf16[48,896]{1,0:T(8,128)(2,1)}, bf16[48,896]{1,0:T(8,128)(2,1)S(1)}, u32[]{:S(2)}, u32[]{:S(2)}) collective-permute-start(bf16[48,896]{1,0:T(8,128)(2,1)} %prep.1.m_ref), channel_id=1, source_target_pairs={{0,3},{1,2},{2,1},{3,0},{4,7},{5,6},{6,5},{7,4},{8,11},{9,10},{10,... | collective-permute-start | bytes 258056 | tf_op jit(solution)/shard_map/ppermute | solution.py:51
  6.2 6.8 %collective-permute-start.1 = (bf16[48,896]{1,0:T(8,128)(2,1)}, bf16[48,896]{1,0:T(8,128)(2,1)S(1)}, u32[]{:S(2)}, u32[]{:S(2)}) collective-permute-start(bf16[48,896]{1,0:T(8,128)(2,1)} %prep.1.m_ref), channel_id=1, source_target_pairs={{0,2},{1,3},{2,0},{3,1},{4,6},{5,7},{6,4},{7,5},{8,10},{9,11},{10,... | collective-permute-start | bytes 258056 | tf_op jit(solution)/shard_map/ppermute | solution.py:51
  6.8 6.2 %collective-permute-start = (bf16[48,896]{1,0:T(8,128)(2,1)}, bf16[48,896]{1,0:T(8,128)(2,1)S(1)}, u32[]{:S(2)}, u32[]{:S(2)}) collective-permute-start(bf16[48,896]{1,0:T(8,128)(2,1)} %prep.1.m_ref), channel_id=1, source_target_pairs={{0,1},{1,0},{2,3},{3,2},{4,5},{5,4},{6,7},{7,6},{8,9},{9,8},{10,11... | collective-permute-start | bytes 258056 | tf_op jit(solution)/shard_map/ppermute | solution.py:51
  10.2 2.8 %copy-start.31 = (bf16[48,896]{1,0:T(8,128)(2,1)}, bf16[48,896]{1,0:T(8,128)(2,1)S(1)}, u32[]{:S(2)}) copy-start(bf16[48,896]{1,0:T(8,128)(2,1)S(1)} %collective-permute-done.2.xc_ref) | copy-start | bytes 258052
  13.7 33.2 %all-to-all-start = ((bf16[8,128,896]{2,1,0:T(8,128)(2,1)}), bf16[8,128,896]{2,1,0:T(8,128)(2,1)S(1)}, u32[]{:S(2)}, u32[]{:S(2)}) async-start(bf16[8,128,896]{2,1,0:T(8,128)(2,1)} %cut_down.1), calls=%async_computation | async-start | bytes 3670016 | tf_op jit(solution)/shard_map/all_to_all | solution.py:67
  20.5 12.0 %collective-permute-start.3 = (bf16[40,1408]{1,0:T(8,128)(2,1)}, bf16[40,1408]{1,0:T(8,128)(2,1)S(1)}, u32[]{:S(2)}, u32[]{:S(2)}) collective-permute-start(bf16[40,1408]{1,0:T(8,128)(2,1)} %get-tuple-element.30), channel_id=1, source_target_pairs={{0,4},{1,5},{2,6},{3,7},{4,8},{5,9},{6,10},{7,11},{8,12},{9,13},{1... | collective-permute-start | bytes 337928 | tf_op jit(solution)/shard_map/ppermute | solution.py:55
  22.4 11.8 %collective-permute-start.4 = (bf16[40,1408]{1,0:T(8,128)(2,1)}, bf16[40,1408]{1,0:T(8,128)(2,1)S(1)}, u32[]{:S(2)}, u32[]{:S(2)}) collective-permute-start(bf16[40,1408]{1,0:T(8,128)(2,1)} %get-tuple-element.31), channel_id=1, source_target_pairs={{0,28},{1,29},{2,30},{3,31},{4,0},{5,1},{6,2},{7,3},{8,4},{9,5},{1... | collective-permute-start | bytes 337928 | tf_op jit(solution)/shard_map/ppermute | solution.py:55
  22.5 14.4 %collective-permute-start.5 = (bf16[40,1408]{1,0:T(8,128)(2,1)}, bf16[40,1408]{1,0:T(8,128)(2,1)S(1)}, u32[]{:S(2)}, u32[]{:S(2)}) collective-permute-start(bf16[40,1408]{1,0:T(8,128)(2,1)} %get-tuple-element.32), channel_id=1, source_target_pairs={{0,8},{1,9},{2,10},{3,11},{4,12},{5,13},{6,14},{7,15},{8,16},{9,17... | collective-permute-start | bytes 337928 | tf_op jit(solution)/shard_map/ppermute | solution.py:55
  29.1 11.9 %collective-permute-start.6 = (bf16[40,1408]{1,0:T(8,128)(2,1)}, bf16[40,1408]{1,0:T(8,128)(2,1)S(1)}, u32[]{:S(2)}, u32[]{:S(2)}) collective-permute-start(bf16[40,1408]{1,0:T(8,128)(2,1)} %get-tuple-element.33), channel_id=1, source_target_pairs={{0,24},{1,25},{2,26},{3,27},{4,28},{5,29},{6,30},{7,31},{8,0},{9,1... | collective-permute-start | bytes 337928 | tf_op jit(solution)/shard_map/ppermute | solution.py:55
  29.1 14.6 %collective-permute-start.7 = (bf16[40,1408]{1,0:T(8,128)(2,1)}, bf16[40,1408]{1,0:T(8,128)(2,1)S(1)}, u32[]{:S(2)}, u32[]{:S(2)}) collective-permute-start(bf16[40,1408]{1,0:T(8,128)(2,1)} %get-tuple-element.34), channel_id=1, source_target_pairs={{0,12},{1,13},{2,14},{3,15},{4,16},{5,17},{6,18},{7,19},{8,20},{9,... | collective-permute-start | bytes 337928 | tf_op jit(solution)/shard_map/ppermute | solution.py:55
  32.5 52.4 %copy-start.8 = (bf16[40,1408]{1,0:T(8,128)(2,1)}, bf16[40,1408]{1,0:T(8,128)(2,1)S(1)}, u32[]{:S(2)}) copy-start(bf16[40,1408]{1,0:T(8,128)(2,1)S(1)} %collective-permute-done.3.refs_1_) | copy-start | bytes 337924
  32.5 14.3 %collective-permute-start.8 = (bf16[40,1408]{1,0:T(8,128)(2,1)}, bf16[40,1408]{1,0:T(8,128)(2,1)S(1)}, u32[]{:S(2)}, u32[]{:S(2)}) collective-permute-start(bf16[40,1408]{1,0:T(8,128)(2,1)} %get-tuple-element.35), channel_id=1, source_target_pairs={{0,20},{1,21},{2,22},{3,23},{4,24},{5,25},{6,26},{7,27},{8,28},{9,... | collective-permute-start | bytes 337928 | tf_op jit(solution)/shard_map/ppermute | solution.py:55
  34.3 50.7 %copy-start.9 = (bf16[40,1408]{1,0:T(8,128)(2,1)}, bf16[40,1408]{1,0:T(8,128)(2,1)S(1)}, u32[]{:S(2)}) copy-start(bf16[40,1408]{1,0:T(8,128)(2,1)S(1)} %collective-permute-done.4.refs_2_) | copy-start | bytes 337924
  34.3 12.5 %collective-permute-start.9 = (bf16[40,1408]{1,0:T(8,128)(2,1)}, bf16[40,1408]{1,0:T(8,128)(2,1)S(1)}, u32[]{:S(2)}, u32[]{:S(2)}) collective-permute-start(bf16[40,1408]{1,0:T(8,128)(2,1)} %get-tuple-element.36), channel_id=1, source_target_pairs={{0,16},{1,17},{2,18},{3,19},{4,20},{5,21},{6,22},{7,23},{8,24},{9,... | collective-permute-start | bytes 337928 | tf_op jit(solution)/shard_map/ppermute | solution.py:55
  36.9 48.0 %copy-start.10 = (bf16[40,1408]{1,0:T(8,128)(2,1)}, bf16[40,1408]{1,0:T(8,128)(2,1)S(1)}, u32[]{:S(2)}) copy-start(bf16[40,1408]{1,0:T(8,128)(2,1)S(1)} %collective-permute-done.5.refs_3_) | copy-start | bytes 337924
  37.0 42.1 %copy-start.4 = (bf16[160,896]{1,0:T(8,128)(2,1)}, bf16[160,896]{1,0:T(8,128)(2,1)S(1)}, u32[]{:S(2)}) copy-start(bf16[160,896]{1,0:T(8,128)(2,1)S(1)} %pad_maximum_fusion.refs_0_) | copy-start | bytes 860164
  37.0 14.8 %collective-permute-start.14 = (bf16[160,896]{1,0:T(8,128)(2,1)S(1)}, bf16[160,896]{1,0:T(8,128)(2,1)S(1)}, u32[]{:S(2)}, u32[]{:S(2)}) collective-permute-start(bf16[160,896]{1,0:T(8,128)(2,1)S(1)} %pad_maximum_fusion.refs_0_), channel_id=1, source_target_pairs={{0,128},{32,160},{64,192},{96,224},{128,0},{160,32},{192,64},{224,... | collective-permute-start | bytes 860168 | tf_op jit(solution)/shard_map/ppermute | solution.py:43
  41.0 43.9 %copy-start.11 = (bf16[40,1408]{1,0:T(8,128)(2,1)}, bf16[40,1408]{1,0:T(8,128)(2,1)S(1)}, u32[]{:S(2)}) copy-start(bf16[40,1408]{1,0:T(8,128)(2,1)S(1)} %collective-permute-done.6.refs_4_) | copy-start | bytes 337924
  41.0 15.5 %collective-permute-start.12 = (bf16[160,896]{1,0:T(8,128)(2,1)S(1)}, bf16[160,896]{1,0:T(8,128)(2,1)}, u32[]{:S(2)}, u32[]{:S(2)}) collective-permute-start(bf16[160,896]{1,0:T(8,128)(2,1)S(1)} %pad_maximum_fusion.refs_0_), channel_id=1, source_target_pairs={{0,96},{32,0},{64,32},{96,64},{128,224},{160,128},{192,160},{224,1... | collective-permute-start | bytes 860168 | tf_op jit(solution)/shard_map/ppermute | solution.py:38
  43.7 41.2 %copy-start.12 = (bf16[40,1408]{1,0:T(8,128)(2,1)}, bf16[40,1408]{1,0:T(8,128)(2,1)S(1)}, u32[]{:S(2)}) copy-start(bf16[40,1408]{1,0:T(8,128)(2,1)S(1)} %collective-permute-done.7.refs_5_) | copy-start | bytes 337924
  43.8 8.0 %collective-permute-start.10 = (bf16[160,896]{1,0:T(8,128)(2,1)S(1)}, bf16[160,896]{1,0:T(8,128)(2,1)}, u32[]{:S(2)}, u32[]{:S(2)}) collective-permute-start(bf16[160,896]{1,0:T(8,128)(2,1)S(1)} %pad_maximum_fusion.refs_0_), channel_id=1, source_target_pairs={{0,32},{32,64},{64,96},{96,0},{128,160},{160,192},{192,224},{224,1... | collective-permute-start | bytes 860168 | tf_op jit(solution)/shard_map/ppermute | solution.py:38
  46.8 38.2 %copy-start.13 = (bf16[40,1408]{1,0:T(8,128)(2,1)}, bf16[40,1408]{1,0:T(8,128)(2,1)S(1)}, u32[]{:S(2)}) copy-start(bf16[40,1408]{1,0:T(8,128)(2,1)S(1)} %collective-permute-done.8.refs_6_) | copy-start | bytes 337924
  46.8 38.2 %copy-start.14 = (bf16[40,1408]{1,0:T(8,128)(2,1)}, bf16[40,1408]{1,0:T(8,128)(2,1)S(1)}, u32[]{:S(2)}) copy-start(bf16[40,1408]{1,0:T(8,128)(2,1)S(1)} %collective-permute-done.9.refs_7_) | copy-start | bytes 337924
  46.9 32.2 %copy-start.5 = (bf16[160,896]{1,0:T(8,128)(2,1)}, bf16[160,896]{1,0:T(8,128)(2,1)S(1)}, u32[]{:S(2)}) copy-start(bf16[160,896]{1,0:T(8,128)(2,1)S(1)} %pad_maximum_fusion.1.refs_1_) | copy-start | bytes 860164
  46.9 38.1 %copy-start = (bf16[8,128,896]{2,1,0:T(8,128)(2,1)}, bf16[8,128,896]{2,1,0:T(8,128)(2,1)S(1)}, u32[]{:S(2)}) copy-start(bf16[8,128,896]{2,1,0:T(8,128)(2,1)S(1)} %all-to-all-done.w_ref) | copy-start | bytes 5505028
  46.9 10.5 %collective-permute-start.13 = (bf16[160,896]{1,0:T(8,128)(2,1)S(1)}, bf16[160,896]{1,0:T(8,128)(2,1)S(1)}, u32[]{:S(2)}, u32[]{:S(2)}) collective-permute-start(bf16[160,896]{1,0:T(8,128)(2,1)S(1)} %pad_maximum_fusion.1.refs_1_), channel_id=1, source_target_pairs={{0,96},{32,0},{64,32},{96,64},{128,224},{160,128},{192,160},{224,1... | collective-permute-start | bytes 860168 | tf_op jit(solution)/shard_map/ppermute | solution.py:38
  51.8 10.8 %collective-permute-start.16 = (bf16[160,896]{1,0:T(8,128)(2,1)}, bf16[160,896]{1,0:T(8,128)(2,1)S(1)}, u32[]{:S(2)}, u32[]{:S(2)}) collective-permute-start(bf16[160,896]{1,0:T(8,128)(2,1)} %collective-permute-done.10.refs_2_), channel_id=1, source_target_pairs={{0,32},{32,64},{64,96},{96,0},{128,160},{160,192},{192,224},{224,1... | collective-permute-start | bytes 860168 | tf_op jit(solution)/shard_map/ppermute | solution.py:38
  51.8 27.2 %copy-start.16 = (bf16[160,896]{1,0:T(8,128)(2,1)}, bf16[160,896]{1,0:T(8,128)(2,1)S(1)}, u32[]{:S(2)}) copy-start(bf16[160,896]{1,0:T(8,128)(2,1)S(1)} %collective-permute-done.14.refs_6_) | copy-start | bytes 860164
  51.8 12.3 %collective-permute-start.20 = (bf16[160,896]{1,0:T(8,128)(2,1)S(1)}, bf16[160,896]{1,0:T(8,128)(2,1)S(1)}, u32[]{:S(2)}, u32[]{:S(2)}) collective-permute-start(bf16[160,896]{1,0:T(8,128)(2,1)S(1)} %collective-permute-done.14.refs_6_), channel_id=1, source_target_pairs={{0,96},{32,0},{64,32},{96,64},{128,224},{160,128},{192,160},{224,1... | collective-permute-start | bytes 860168 | tf_op jit(solution)/shard_map/ppermute | solution.py:38
  55.0 9.8 %collective-permute-start.15 = (bf16[160,896]{1,0:T(8,128)(2,1)S(1)}, bf16[160,896]{1,0:T(8,128)(2,1)S(1)}, u32[]{:S(2)}, u32[]{:S(2)}) collective-permute-start(bf16[160,896]{1,0:T(8,128)(2,1)S(1)} %pad_maximum_fusion.1.refs_1_), channel_id=1, source_target_pairs={{0,128},{32,160},{64,192},{96,224},{128,0},{160,32},{192,64},{224,... | collective-permute-start | bytes 860168 | tf_op jit(solution)/shard_map/ppermute | solution.py:43
  56.5 10.9 %collective-permute-start.18 = (bf16[160,896]{1,0:T(8,128)(2,1)S(1)}, bf16[160,896]{1,0:T(8,128)(2,1)S(1)}, u32[]{:S(2)}, u32[]{:S(2)}) collective-permute-start(bf16[160,896]{1,0:T(8,128)(2,1)S(1)} %collective-permute-done.14.refs_6_), channel_id=1, source_target_pairs={{0,32},{32,64},{64,96},{96,0},{128,160},{160,192},{192,224},{224,1... | collective-permute-start | bytes 860168 | tf_op jit(solution)/shard_map/ppermute | solution.py:38
  57.4 21.6 %copy-start.17 = (bf16[160,896]{1,0:T(8,128)(2,1)}, bf16[160,896]{1,0:T(8,128)(2,1)S(1)}, u32[]{:S(2)}) copy-start(bf16[160,896]{1,0:T(8,128)(2,1)S(1)} %collective-permute-done.13.refs_5_) | copy-start | bytes 860164
  57.4 12.3 %collective-permute-start.17 = (bf16[160,896]{1,0:T(8,128)(2,1)S(1)}, bf16[160,896]{1,0:T(8,128)(2,1)S(1)}, u32[]{:S(2)}, u32[]{:S(2)}) collective-permute-start(bf16[160,896]{1,0:T(8,128)(2,1)S(1)} %collective-permute-done.13.refs_5_), channel_id=1, source_target_pairs={{0,96},{32,0},{64,32},{96,64},{128,224},{160,128},{192,160},{224,1... | collective-permute-start | bytes 860168 | tf_op jit(solution)/shard_map/ppermute | solution.py:38
  62.6 16.5 %copy-start.18 = (bf16[160,896]{1,0:T(8,128)(2,1)}, bf16[160,896]{1,0:T(8,128)(2,1)S(1)}, u32[]{:S(2)}) copy-start(bf16[160,896]{1,0:T(8,128)(2,1)S(1)} %collective-permute-done.16.refs_8_) | copy-start | bytes 860164
  62.6 8.6 %collective-permute-start.22 = (bf16[160,896]{1,0:T(8,128)(2,1)S(1)}, bf16[160,896]{1,0:T(8,128)(2,1)S(1)}, u32[]{:S(2)}, u32[]{:S(2)}) collective-permute-start(bf16[160,896]{1,0:T(8,128)(2,1)S(1)} %collective-permute-done.16.refs_8_), channel_id=1, source_target_pairs={{0,128},{32,160},{64,192},{96,224},{128,0},{160,32},{192,64},{224,... | collective-permute-start | bytes 860168 | tf_op jit(solution)/shard_map/ppermute | solution.py:43
  64.1 11.0 %copy-start.19 = (bf16[160,896]{1,0:T(8,128)(2,1)}, bf16[160,896]{1,0:T(8,128)(2,1)S(1)}, u32[]{:S(2)}) copy-start(bf16[160,896]{1,0:T(8,128)(2,1)S(1)} %collective-permute-done.20.refs_12_) | copy-start | bytes 860164
  64.1 11.0 %collective-permute-start.11 = (bf16[160,896]{1,0:T(8,128)(2,1)S(1)}, bf16[160,896]{1,0:T(8,128)(2,1)S(1)}, u32[]{:S(2)}, u32[]{:S(2)}) collective-permute-start(bf16[160,896]{1,0:T(8,128)(2,1)S(1)} %pad_maximum_fusion.1.refs_1_), channel_id=1, source_target_pairs={{0,32},{32,64},{64,96},{96,0},{128,160},{160,192},{192,224},{224,1... | collective-permute-start | bytes 860168 | tf_op jit(solution)/shard_map/ppermute | solution.py:38
  64.9 10.3 %copy-start.20 = (bf16[160,896]{1,0:T(8,128)(2,1)}, bf16[160,896]{1,0:T(8,128)(2,1)S(1)}, u32[]{:S(2)}) copy-start(bf16[160,896]{1,0:T(8,128)(2,1)S(1)} %collective-permute-done.15.refs_7_) | copy-start | bytes 860164
  64.9 10.3 %collective-permute-start.21 = (bf16[160,896]{1,0:T(8,128)(2,1)S(1)}, bf16[160,896]{1,0:T(8,128)(2,1)S(1)}, u32[]{:S(2)}, u32[]{:S(2)}) collective-permute-start(bf16[160,896]{1,0:T(8,128)(2,1)S(1)} %collective-permute-done.15.refs_7_), channel_id=1, source_target_pairs={{0,96},{32,0},{64,32},{96,64},{128,224},{160,128},{192,160},{224,1... | collective-permute-start | bytes 860168 | tf_op jit(solution)/shard_map/ppermute | solution.py:38
  67.4 10.9 %copy-start.21 = (bf16[160,896]{1,0:T(8,128)(2,1)}, bf16[160,896]{1,0:T(8,128)(2,1)S(1)}, u32[]{:S(2)}) copy-start(bf16[160,896]{1,0:T(8,128)(2,1)S(1)} %collective-permute-done.18.refs_10_) | copy-start | bytes 860164
  67.4 10.9 %collective-permute-start.19 = (bf16[160,896]{1,0:T(8,128)(2,1)S(1)}, bf16[160,896]{1,0:T(8,128)(2,1)S(1)}, u32[]{:S(2)}, u32[]{:S(2)}) collective-permute-start(bf16[160,896]{1,0:T(8,128)(2,1)S(1)} %collective-permute-done.15.refs_7_), channel_id=1, source_target_pairs={{0,32},{32,64},{64,96},{96,0},{128,160},{160,192},{192,224},{224,1... | collective-permute-start | bytes 860168 | tf_op jit(solution)/shard_map/ppermute | solution.py:38
  69.7 8.6 %copy-start.22 = (bf16[160,896]{1,0:T(8,128)(2,1)}, bf16[160,896]{1,0:T(8,128)(2,1)S(1)}, u32[]{:S(2)}) copy-start(bf16[160,896]{1,0:T(8,128)(2,1)S(1)} %collective-permute-done.17.refs_9_) | copy-start | bytes 860164
  69.7 9.3 %collective-permute-start.23 = (bf16[160,896]{1,0:T(8,128)(2,1)S(1)}, bf16[160,896]{1,0:T(8,128)(2,1)}, u32[]{:S(2)}, u32[]{:S(2)}) collective-permute-start(bf16[160,896]{1,0:T(8,128)(2,1)S(1)} %collective-permute-done.17.refs_9_), channel_id=1, source_target_pairs={{0,128},{32,160},{64,192},{96,224},{128,0},{160,32},{192,64},{224,... | collective-permute-start | bytes 860168 | tf_op jit(solution)/shard_map/ppermute | solution.py:43
  71.2 7.1 %copy-start.23 = (bf16[160,896]{1,0:T(8,128)(2,1)}, bf16[160,896]{1,0:T(8,128)(2,1)S(1)}, u32[]{:S(2)}) copy-start(bf16[160,896]{1,0:T(8,128)(2,1)S(1)} %collective-permute-done.22.refs_14_) | copy-start | bytes 860164
  75.1 3.2 %copy-start.24 = (bf16[160,896]{1,0:T(8,128)(2,1)}, bf16[160,896]{1,0:T(8,128)(2,1)S(1)}, u32[]{:S(2)}) copy-start(bf16[160,896]{1,0:T(8,128)(2,1)S(1)} %collective-permute-done.11.refs_3_) | copy-start | bytes 860164
  75.1 3.2 %copy-start.25 = (bf16[160,896]{1,0:T(8,128)(2,1)}, bf16[160,896]{1,0:T(8,128)(2,1)S(1)}, u32[]{:S(2)}) copy-start(bf16[160,896]{1,0:T(8,128)(2,1)S(1)} %collective-permute-done.21.refs_13_) | copy-start | bytes 860164
  85.0 12.4 %all-to-all-start.1 = ((bf16[8,320,128]{2,1,0:T(8,128)(2,1)}), bf16[8,320,128]{2,1,0:T(8,128)(2,1)S(1)}, u32[]{:S(2)}, u32[]{:S(2)}) async-start(bf16[8,320,128]{2,1,0:T(8,128)(2,1)} %add_blocks.1), calls=%async_computation.1 | async-start | bytes 1310720 | tf_op jit(solution)/shard_map/all_to_all | solution.py:67
  98.3 13.1 %copy-start.15 = (bf16[256,576]{0,1:T(8,128)(2,1)S(1)}, bf16[256,576]{0,1:T(8,128)(2,1)}, u32[]{:S(2)}) copy-start(bf16[256,576]{0,1:T(8,128)(2,1)} %param.11) | copy-start | bytes 884740
  98.3 15.2 %copy-start.6 = (bf16[128,576]{1,0:T(8,128)(2,1)S(1)}, bf16[128,576]{1,0:T(8,128)(2,1)}, u32[]{:S(2)}) copy-start(bf16[128,576]{1,0:T(8,128)(2,1)} %select_units.1.refs_0_) | copy-start | bytes 442372
  101.9 23.8 %all-to-all-start.2 = ((bf16[8,40,896]{2,1,0:T(8,128)(2,1)}), bf16[8,40,896]{2,1,0:T(8,128)(2,1)S(1)}, u32[]{:S(2)}, u32[]{:S(2)}) async-start(bf16[8,40,896]{2,1,0:T(8,128)(2,1)} %down.1), calls=%async_computation.2 | async-start | bytes 1146880 | tf_op jit(solution)/shard_map/all_to_all | solution.py:61
  111.5 20.6 %copy-start.3 = (bf16[256,576]{1,0:T(8,128)(2,1)}, bf16[256,576]{1,0:T(8,128)(2,1)S(1)}, u32[]{:S(2)}) copy-start(bf16[256,576]{1,0:T(8,128)(2,1)S(1)} %copy.22.own_ref) | copy-start | bytes 884740
  111.5 12.4 %collective-permute-start.27 = (bf16[256,576]{1,0:T(8,128)(2,1)S(1)}, bf16[256,576]{1,0:T(8,128)(2,1)S(1)}, u32[]{:S(2)}, u32[]{:S(2)}) collective-permute-start(bf16[256,576]{1,0:T(8,128)(2,1)S(1)} %copy.22.own_ref), channel_id=1, source_target_pairs={{0,1},{1,2},{2,3},{3,4},{4,5},{5,6},{6,7},{7,8},{8,9},{9,10},{10,1... | collective-permute-start | bytes 884744 | tf_op jit(solution)/shard_map/ppermute | solution.py:474
  113.5 10.5 %collective-permute-start.26 = (bf16[128,576]{1,0:T(8,128)(2,1)S(1)}, bf16[128,576]{1,0:T(8,128)(2,1)S(1)}, u32[]{:S(2)}, u32[]{:S(2)}) collective-permute-start(bf16[128,576]{1,0:T(8,128)(2,1)S(1)} %copy-done.6), channel_id=1, source_target_pairs={{0,64},{32,96},{64,0},{96,32},{128,192},{160,224},{192,128},{224,1... | collective-permute-start | bytes 442376 | tf_op jit(solution)/shard_map/ppermute | solution.py:38
  115.6 9.1 %collective-permute-start.25 = (bf16[128,576]{1,0:T(8,128)(2,1)S(1)}, bf16[128,576]{1,0:T(8,128)(2,1)S(1)}, u32[]{:S(2)}, u32[]{:S(2)}) collective-permute-start(bf16[128,576]{1,0:T(8,128)(2,1)S(1)} %copy-done.6), channel_id=1, source_target_pairs={{0,96},{32,0},{64,32},{96,64},{128,224},{160,128},{192,160},{224,1... | collective-permute-start | bytes 442376 | tf_op jit(solution)/shard_map/ppermute | solution.py:38
  116.8 8.9 %collective-permute-start.24 = (bf16[128,576]{1,0:T(8,128)(2,1)S(1)}, bf16[128,576]{1,0:T(8,128)(2,1)S(1)}, u32[]{:S(2)}, u32[]{:S(2)}) collective-permute-start(bf16[128,576]{1,0:T(8,128)(2,1)S(1)} %copy-done.6), channel_id=1, source_target_pairs={{0,32},{32,64},{64,96},{96,0},{128,160},{160,192},{192,224},{224,1... | collective-permute-start | bytes 442376 | tf_op jit(solution)/shard_map/ppermute | solution.py:38
  123.9 8.2 %copy-start.7 = (bf16[256,576]{1,0:T(8,128)(2,1)}, bf16[256,576]{1,0:T(8,128)(2,1)S(1)}, u32[]{:S(2)}) copy-start(bf16[256,576]{1,0:T(8,128)(2,1)S(1)} %collective-permute-done.27.prev_ref) | copy-start | bytes 884740
  123.9 8.2 %copy-start.27 = (bf16[128,576]{1,0:T(8,128)(2,1)}, bf16[128,576]{1,0:T(8,128)(2,1)S(1)}, u32[]{:S(2)}) copy-start(bf16[128,576]{1,0:T(8,128)(2,1)S(1)} %collective-permute-done.26.refs_3_) | copy-start | bytes 442372
  124.6 7.5 %copy-start.28 = (bf16[128,576]{1,0:T(8,128)(2,1)}, bf16[128,576]{1,0:T(8,128)(2,1)S(1)}, u32[]{:S(2)}) copy-start(bf16[128,576]{1,0:T(8,128)(2,1)S(1)} %collective-permute-done.25.refs_2_) | copy-start | bytes 442372
  125.6 6.5 %copy-start.29 = (bf16[128,576]{1,0:T(8,128)(2,1)}, bf16[128,576]{1,0:T(8,128)(2,1)S(1)}, u32[]{:S(2)}) copy-start(bf16[128,576]{1,0:T(8,128)(2,1)S(1)} %collective-permute-done.24.refs_1_) | copy-start | bytes 442372
  128.7 7.5 %collective-permute-start.28 = (bf16[32,896]{1,0:T(8,128)(2,1)}, bf16[32,896]{1,0:T(8,128)(2,1)S(1)}, u32[]{:S(2)}, u32[]{:S(2)}) collective-permute-start(bf16[32,896]{1,0:T(8,128)(2,1)} %get-tuple-element.46), channel_id=1, source_target_pairs={{0,1},{1,0},{2,3},{3,2},{4,5},{5,4},{6,7},{7,6},{8,9},{9,8},{10,11... | collective-permute-start | bytes 172040 | tf_op jit(solution)/shard_map/ppermute | solution.py:51
  128.8 7.5 %collective-permute-start.29 = (bf16[32,896]{1,0:T(8,128)(2,1)}, bf16[32,896]{1,0:T(8,128)(2,1)S(1)}, u32[]{:S(2)}, u32[]{:S(2)}) collective-permute-start(bf16[32,896]{1,0:T(8,128)(2,1)} %get-tuple-element.47), channel_id=1, source_target_pairs={{0,2},{1,3},{2,0},{3,1},{4,6},{5,7},{6,4},{7,5},{8,10},{9,11},{10,... | collective-permute-start | bytes 172040 | tf_op jit(solution)/shard_map/ppermute | solution.py:51
  130.5 5.9 %copy-start.30 = (f32[32,896]{1,0:T(8,128)S(1)}, f32[32,896]{1,0:T(8,128)}, u32[]{:S(2)}) copy-start(f32[32,896]{1,0:T(8,128)} %get-tuple-element.55) | copy-start | bytes 344068
  130.5 5.9 %collective-permute-start.30 = (bf16[32,896]{1,0:T(8,128)(2,1)}, bf16[32,896]{1,0:T(8,128)(2,1)S(1)}, u32[]{:S(2)}, u32[]{:S(2)}) collective-permute-start(bf16[32,896]{1,0:T(8,128)(2,1)} %get-tuple-element.48), channel_id=1, source_target_pairs={{0,3},{1,2},{2,1},{3,0},{4,7},{5,6},{6,5},{7,4},{8,11},{9,10},{10,... | collective-permute-start | bytes 172040 | tf_op jit(solution)/shard_map/ppermute | solution.py:51
  137.3 13.0 %all-to-all-start.3 = ((bf16[8,32,896]{2,1,0:T(8,128)(2,1)}), bf16[8,32,896]{2,1,0:T(8,128)(2,1)S(1)}, u32[]{:S(2)}, u32[]{:S(2)}) async-start(bf16[8,32,896]{2,1,0:T(8,128)(2,1)} %broadcast_in_dim.2), calls=%async_computation.3 | async-start | bytes 917504 | tf_op jit(solution)/shard_map/all_to_all | solution.py:67
  (5 other events, 3.7 us)

commit v5 on v4

--- a/solution.py
+++ b/solution.py
@@ -519,7 +519,7 @@
 
     keys = (previous, group_latent, unit_rows)
     steps = group_latent.shape[0] // BLOCK
-    back, *_ = lax.optimization_barrier((back, unit_rows, previous))
+    back, *_ = lax.optimization_barrier((back, unit_rows))
     context = attend(at[1:], after(rows_q, back), *keys, 0, 1)
     kept, *passed = mix(own_e, slot, share, back)
     passed = [across_j(value, bit) for bit, value in enumerate(passed, 1)]

time: 154 us -> 155 us (level)
    ppermute x13, waiting for transfers between devices: 15.1 us -> 21.4 us  [along_y(): return lax.ppermute(value, 'section', pairs)]
    ppermute x1, waiting for transfers between devices: 6.32 us -> 0.01 us  [per_device(): lax.ppermute(group_latent, 'expert', [(i, i + 1) for i in range(N_EXPERT...]
  transfers between devices with their start and end apart: 35 -> 35, of which waited for: 16 -> 15; matrix products, arithmetic and copies ran while one was open for 4% -> 4% of each run, Pallas kernels for 13% -> 14%
where the time goes in v5:
time: 155 us; the launch traced here: 152 us
  starting transfers between devices  72.2 us (47%)
  Pallas kernels  33.7 us (22%)
  waiting for transfers between devices  32.5 us (21%)
  local copies, waits for them, and re-layouts  11.6 us (7%)
    ppermute x13, waiting for transfers between devices, along_y(): return lax.ppermute(value, 'section', pairs)  21.4 us
    ppermute x13, starting transfers between devices, along_y(): return lax.ppermute(value, 'section', pairs)  20.3 us
    ppermute x7, starting transfers between devices, along_z(): lax.ppermute(value, 'expert', [(e, (e + steps * N_J) % N_EXPERT) for e in...  15.5 us
    pallas_call x2, Pallas kernels, attend(): pl.pallas_call(functools.partial(attend_kernel, first_step), grid_spec=pl...  12 us
    all_to_all x3, starting transfers between devices, over_section(): lax.all_to_all(value, 'section', split_axis=0, concat_axis=0, tiled=True)  11.7 us
    all_to_all x1, starting transfers between devices, over_z(): lax.all_to_all(value, 'expert', split_axis=0, concat_axis=0, tiled=True,...  9.45 us
    unnamed x70, local copies, waits for them, and re-layouts  9.03 us
    ppermute x6, starting transfers between devices, across_j(): lax.ppermute(value, 'expert', [(e, e ^ bit) for e in range(N_EXPERT)])  6.73 us
  transfers between devices with their start and end apart: 35, of which 15 were waited for; matrix products, arithmetic and copies ran while one was open for 4% of the time, Pallas kernels for 14%

profile of v5, /device:TPU:64, one launch (start us, length us, event | category | flops | bytes accessed | tf_op | source)
XLA Modules:
  0.0 151.8 jit_solution(14529090332448816515)
XLA Ops:
  0.6 0.6 pad_add_fusion.at_ref
  1.3 2.4 %prep.1.m_ref = bf16[48,896]{1,0:T(8,128)(2,1)} custom-call(s32[2]{0:T(128)} %pad_add_fusion.at_ref, s32[16]{0:T(128)} %ids_ref.1, bf16[32,7168]{1,0:T(8,128)(2,1)} %tok_ref.1, s32[8,32]{1,0:T(8,128)} %bitcast.16, f32[8,32]{1,0:T(8,128)} %bitcast.17, bf16[4,32,576]{2,1,0:T(8,128)(2,1)} %cache_ref.1), custom_call_target="tpu_custom_call" | custom-call | flops 1000 | bytes 409600 | tf_op jit(solution)/shard_map/prep/pallas_call | solution.py:130
  3.7 2.5 %collective-permute-start.2 = (bf16[48,896]{1,0:T(8,128)(2,1)}, bf16[48,896]{1,0:T(8,128)(2,1)S(1)}, u32[]{:S(2)}, u32[]{:S(2)}) collective-permute-start(bf16[48,896]{1,0:T(8,128)(2,1)} %prep.1.m_ref), channel_id=1, source_target_pairs={{0,3},{1,2},{2,1},{3,0},{4,7},{5,6},{6,5},{7,4},{8,11},{9,10},{10,... | collective-permute-start | bytes 258056 | tf_op jit(solution)/shard_map/ppermute | solution.py:51
  6.2 0.6 collective-permute-start.1
  6.8 0.3 collective-permute-start
  7.1 2.9 %cut_down.1 = bf16[8,128,896]{2,1,0:T(8,128)(2,1)} custom-call(bf16[1,128,7168]{2,1,0:T(8,128)(2,1)} %in_ref), custom_call_target="tpu_custom_call" | custom-call | bytes 3670016 | tf_op jit(solution)/shard_map/cut_down/pallas_call | solution.py:211
  9.9 0.2 collective-permute-done.2.xc_ref
  10.2 2.8 %collective-permute-done.1.x_ref = bf16[48,896]{1,0:T(8,128)(2,1)S(1)} collective-permute-done((bf16[48,896]{1,0:T(8,128)(2,1)}, bf16[48,896]{1,0:T(8,128)(2,1)S(1)}, u32[]{:S(2)}, u32[]{:S(2)}) %collective-permute-start.1) | collective-permute-done | bytes 86048 | tf_op jit(solution)/shard_map/ppermute | solution.py:51
  13.0 0.6 copy-done.32
  13.7 4.5 %all-to-all-start = ((bf16[8,128,896]{2,1,0:T(8,128)(2,1)}), bf16[8,128,896]{2,1,0:T(8,128)(2,1)S(1)}, u32[]{:S(2)}, u32[]{:S(2)}) async-start(bf16[8,128,896]{2,1,0:T(8,128)(2,1)} %cut_down.1), calls=%async_computation | async-start | bytes 3670016 | tf_op jit(solution)/shard_map/all_to_all | solution.py:67
  18.2 2.3 %pack.1 = (f32[8,128]{1,0:T(8,128)}, f32[8,128]{1,0:T(8,128)}, bf16[40,1408]{1,0:T(8,128)(2,1)}, bf16[40,1408]{1,0:T(8,128)(2,1)}, bf16[40,1408]{1,0:T(8,128)(2,...) custom-call(s32[1]{0:T(128)} %bitcast.e_ref.s_ref, ...), custom_call_target="tpu_custom_call" | custom-call | flops 73400320 | bytes 1146880 | tf_op jit(solution)/shard_map/pack/pallas_call | solution.py:190
  20.5 1.9 %collective-permute-start.3 = (bf16[40,1408]{1,0:T(8,128)(2,1)}, bf16[40,1408]{1,0:T(8,128)(2,1)S(1)}, u32[]{:S(2)}, u32[]{:S(2)}) collective-permute-start(bf16[40,1408]{1,0:T(8,128)(2,1)} %get-tuple-element.30), channel_id=1, source_target_pairs={{0,4},{1,5},{2,6},{3,7},{4,8},{5,9},{6,10},{7,11},{8,12},{9,13},{1... | collective-permute-start | bytes 337928 | tf_op jit(solution)/shard_map/ppermute | solution.py:55
  22.4 0.1 collective-permute-start.4
  22.5 5.7 %collective-permute-start.5 = (bf16[40,1408]{1,0:T(8,128)(2,1)}, bf16[40,1408]{1,0:T(8,128)(2,1)S(1)}, u32[]{:S(2)}, u32[]{:S(2)}) collective-permute-start(bf16[40,1408]{1,0:T(8,128)(2,1)} %get-tuple-element.32), channel_id=1, source_target_pairs={{0,8},{1,9},{2,10},{3,11},{4,12},{5,13},{6,14},{7,15},{8,16},{9,17... | collective-permute-start | bytes 337928 | tf_op jit(solution)/shard_map/ppermute | solution.py:55
  28.2 0.9 slice.24
  29.1 3.4 %collective-permute-start.7 = (bf16[40,1408]{1,0:T(8,128)(2,1)}, bf16[40,1408]{1,0:T(8,128)(2,1)S(1)}, u32[]{:S(2)}, u32[]{:S(2)}) collective-permute-start(bf16[40,1408]{1,0:T(8,128)(2,1)} %get-tuple-element.34), channel_id=1, source_target_pairs={{0,12},{1,13},{2,14},{3,15},{4,16},{5,17},{6,18},{7,19},{8,20},{9,... | collective-permute-start | bytes 337928 | tf_op jit(solution)/shard_map/ppermute | solution.py:55
  32.5 1.7 %collective-permute-start.8 = (bf16[40,1408]{1,0:T(8,128)(2,1)}, bf16[40,1408]{1,0:T(8,128)(2,1)S(1)}, u32[]{:S(2)}, u32[]{:S(2)}) collective-permute-start(bf16[40,1408]{1,0:T(8,128)(2,1)} %get-tuple-element.35), channel_id=1, source_target_pairs={{0,20},{1,21},{2,22},{3,23},{4,24},{5,25},{6,26},{7,27},{8,28},{9,... | collective-permute-start | bytes 337928 | tf_op jit(solution)/shard_map/ppermute | solution.py:55
  34.3 2.6 %collective-permute-start.9 = (bf16[40,1408]{1,0:T(8,128)(2,1)}, bf16[40,1408]{1,0:T(8,128)(2,1)S(1)}, u32[]{:S(2)}, u32[]{:S(2)}) collective-permute-start(bf16[40,1408]{1,0:T(8,128)(2,1)} %get-tuple-element.36), channel_id=1, source_target_pairs={{0,16},{1,17},{2,18},{3,19},{4,20},{5,21},{6,22},{7,23},{8,24},{9,... | collective-permute-start | bytes 337928 | tf_op jit(solution)/shard_map/ppermute | solution.py:55
  37.0 2.1 %collective-permute-start.14 = (bf16[160,896]{1,0:T(8,128)(2,1)S(1)}, bf16[160,896]{1,0:T(8,128)(2,1)S(1)}, u32[]{:S(2)}, u32[]{:S(2)}) collective-permute-start(bf16[160,896]{1,0:T(8,128)(2,1)S(1)} %pad_maximum_fusion.refs_0_), channel_id=1, source_target_pairs={{0,128},{32,160},{64,192},{96,224},{128,0},{160,32},{192,64},{224,... | collective-permute-start | bytes 860168 | tf_op jit(solution)/shard_map/ppermute | solution.py:43
  39.1 1.9 %collective-permute-done.6.refs_4_ = bf16[40,1408]{1,0:T(8,128)(2,1)S(1)} collective-permute-done((bf16[40,1408]{1,0:T(8,128)(2,1)}, bf16[40,1408]{1,0:T(8,128)(2,1)S(1)}, u32[]{:S(2)}, u32[]{:S(2)}) %collective-permute-start.6) | collective-permute-done | bytes 112672 | tf_op jit(solution)/shard_map/ppermute | solution.py:55
  41.0 2.7 %collective-permute-start.12 = (bf16[160,896]{1,0:T(8,128)(2,1)S(1)}, bf16[160,896]{1,0:T(8,128)(2,1)}, u32[]{:S(2)}, u32[]{:S(2)}) collective-permute-start(bf16[160,896]{1,0:T(8,128)(2,1)S(1)} %pad_maximum_fusion.refs_0_), channel_id=1, source_target_pairs={{0,96},{32,0},{64,32},{96,64},{128,224},{160,128},{192,160},{224,1... | collective-permute-start | bytes 860168 | tf_op jit(solution)/shard_map/ppermute | solution.py:38
  43.9 2.9 %collective-permute-done.8.refs_6_ = bf16[40,1408]{1,0:T(8,128)(2,1)S(1)} collective-permute-done((bf16[40,1408]{1,0:T(8,128)(2,1)}, bf16[40,1408]{1,0:T(8,128)(2,1)S(1)}, u32[]{:S(2)}, u32[]{:S(2)}) %collective-permute-start.8) | collective-permute-done | bytes 112672 | tf_op jit(solution)/shard_map/ppermute | solution.py:55
  46.9 3.3 %collective-permute-start.13 = (bf16[160,896]{1,0:T(8,128)(2,1)S(1)}, bf16[160,896]{1,0:T(8,128)(2,1)S(1)}, u32[]{:S(2)}, u32[]{:S(2)}) collective-permute-start(bf16[160,896]{1,0:T(8,128)(2,1)S(1)} %pad_maximum_fusion.1.refs_1_), channel_id=1, source_target_pairs={{0,96},{32,0},{64,32},{96,64},{128,224},{160,128},{192,160},{224,1... | collective-permute-start | bytes 860168 | tf_op jit(solution)/shard_map/ppermute | solution.py:38
  50.2 1.6 %collective-permute-done.10.refs_2_ = bf16[160,896]{1,0:T(8,128)(2,1)} collective-permute-done((bf16[160,896]{1,0:T(8,128)(2,1)S(1)}, bf16[160,896]{1,0:T(8,128)(2,1)}, u32[]{:S(2)}, u32[]{:S(2)}) %collective-permute-start.10) | collective-permute-done | bytes 286752 | tf_op jit(solution)/shard_map/ppermute | solution.py:38
  51.8 3.2 %collective-permute-start.20 = (bf16[160,896]{1,0:T(8,128)(2,1)S(1)}, bf16[160,896]{1,0:T(8,128)(2,1)S(1)}, u32[]{:S(2)}, u32[]{:S(2)}) collective-permute-start(bf16[160,896]{1,0:T(8,128)(2,1)S(1)} %collective-permute-done.14.refs_6_), channel_id=1, source_target_pairs={{0,96},{32,0},{64,32},{96,64},{128,224},{160,128},{192,160},{224,1... | collective-permute-start | bytes 860168 | tf_op jit(solution)/shard_map/ppermute | solution.py:38
  55.0 1.5 collective-permute-start.15
  56.5 0.9 collective-permute-done.13.refs_5_
  57.4 3.7 %collective-permute-start.17 = (bf16[160,896]{1,0:T(8,128)(2,1)S(1)}, bf16[160,896]{1,0:T(8,128)(2,1)S(1)}, u32[]{:S(2)}, u32[]{:S(2)}) collective-permute-start(bf16[160,896]{1,0:T(8,128)(2,1)S(1)} %collective-permute-done.13.refs_5_), channel_id=1, source_target_pairs={{0,96},{32,0},{64,32},{96,64},{128,224},{160,128},{192,160},{224,1... | collective-permute-start | bytes 860168 | tf_op jit(solution)/shard_map/ppermute | solution.py:38
  61.1 1.4 collective-permute-done.16.refs_8_
  62.6 1.6 %collective-permute-start.22 = (bf16[160,896]{1,0:T(8,128)(2,1)S(1)}, bf16[160,896]{1,0:T(8,128)(2,1)S(1)}, u32[]{:S(2)}, u32[]{:S(2)}) collective-permute-start(bf16[160,896]{1,0:T(8,128)(2,1)S(1)} %collective-permute-done.16.refs_8_), channel_id=1, source_target_pairs={{0,128},{32,160},{64,192},{96,224},{128,0},{160,32},{192,64},{224,... | collective-permute-start | bytes 860168 | tf_op jit(solution)/shard_map/ppermute | solution.py:43
  64.1 0.7 collective-permute-start.11
  64.9 2.5 %collective-permute-start.21 = (bf16[160,896]{1,0:T(8,128)(2,1)S(1)}, bf16[160,896]{1,0:T(8,128)(2,1)S(1)}, u32[]{:S(2)}, u32[]{:S(2)}) collective-permute-start(bf16[160,896]{1,0:T(8,128)(2,1)S(1)} %collective-permute-done.15.refs_7_), channel_id=1, source_target_pairs={{0,96},{32,0},{64,32},{96,64},{128,224},{160,128},{192,160},{224,1... | collective-permute-start | bytes 860168 | tf_op jit(solution)/shard_map/ppermute | solution.py:38
  67.4 2.3 %collective-permute-done.17.refs_9_ = bf16[160,896]{1,0:T(8,128)(2,1)S(1)} collective-permute-done((bf16[160,896]{1,0:T(8,128)(2,1)S(1)}, bf16[160,896]{1,0:T(8,128)(2,1)S(1)}, u32[]{:S(2)}, u32[]{:S(2)}) %collective-permute-start.17) | collective-permute-done | bytes 286752 | tf_op jit(solution)/shard_map/ppermute | solution.py:38
  69.7 1.5 collective-permute-start.23
  71.2 3.9 %collective-permute-done.11.refs_3_ = bf16[160,896]{1,0:T(8,128)(2,1)S(1)} collective-permute-done((bf16[160,896]{1,0:T(8,128)(2,1)S(1)}, bf16[160,896]{1,0:T(8,128)(2,1)S(1)}, u32[]{:S(2)}, u32[]{:S(2)}) %collective-permute-start.11) | collective-permute-done | bytes 286752 | tf_op jit(solution)/shard_map/ppermute | solution.py:38
  75.1 3.1 %collective-permute-done.19.refs_11_ = bf16[160,896]{1,0:T(8,128)(2,1)S(1)} collective-permute-done((bf16[160,896]{1,0:T(8,128)(2,1)S(1)}, bf16[160,896]{1,0:T(8,128)(2,1)S(1)}, u32[]{:S(2)}, u32[]{:S(2)}) %collective-permute-start.19) | collective-permute-done | bytes 286752 | tf_op jit(solution)/shard_map/ppermute | solution.py:38
  78.3 0.7 copy-done.26
  79.1 5.9 %add_blocks.1 = bf16[8,320,128]{2,1,0:T(8,128)(2,1)} custom-call(s32[2]{0:T(128)} %pad_add_fusion.at_ref, bf16[160,896]{1,0:T(8,128)(2,1)} %copy-done.4, bf16[160,896]{1,0:T(8,128)(2,1)} %copy-done.5, bf16[160,896]{1,0:T(8,128)(2,1)} %collective-permute-done.10.refs_2_, bf16[160,896]{1,0:T(8,128)(2,1)} %copy-done.24, ...), custom_call_target="tpu_custom_call" | custom-call | flops 1174405120 | bytes 10485760 | tf_op jit(solution)/shard_map/add_blocks/pallas_call | solution.py:250
  85.0 3.6 %all-to-all-start.1 = ((bf16[8,320,128]{2,1,0:T(8,128)(2,1)}), bf16[8,320,128]{2,1,0:T(8,128)(2,1)S(1)}, u32[]{:S(2)}, u32[]{:S(2)}) async-start(bf16[8,320,128]{2,1,0:T(8,128)(2,1)} %add_blocks.1), calls=%async_computation.1 | async-start | bytes 1310720 | tf_op jit(solution)/shard_map/all_to_all | solution.py:67
  88.6 4.9 %copy.21 = bf16[256,8,576]{2,1,0:T(8,128)(2,1)} copy(bf16[256,8,576]{0,2,1:T(8,128)(2,1)} %param.10) | data formatting | bytes 4718592 | tf_op args[0]
  93.5 2.4 %select_units.1.refs_0_ = bf16[128,576]{1,0:T(8,128)(2,1)} custom-call(s32[1]{0:T(128)} %bitcast.e_ref.s_ref, s32[16]{0:T(128)} %ids_ref.1, bf16[40,1408]{1,0:T(8,128)(2,1)} %get-tuple-element.29.refs_0_, bf16[40,1408]{1,0:T(8,128)(2,1)} %copy-done.8, bf16[40,1408]{1,0:T(8,128)(2,1)} %copy-done.9, bf16[40,1408]{1,0:T(8,128)(2,1)} %copy-done.10, ...), custom_call_target="tpu_custom_call" | custom-call | flops 1000 | bytes 2097152 | tf_op jit(solution)/shard_map/select_units/pallas_call | solution.py:333
  95.9 1.5 %all-to-all-done.1.hid = bf16[8,320,128]{2,1,0:T(8,128)(2,1)S(1)} async-done(((bf16[8,320,128]{2,1,0:T(8,128)(2,1)}), bf16[8,320,128]{2,1,0:T(8,128)(2,1)S(1)}, u32[]{:S(2)}, u32[]{:S(2)}) %all-to-all-start.1) | async-done | bytes 655392 | tf_op jit(solution)/shard_map/all_to_all | solution.py:67
  97.4 0.9 copy-done.1
  98.3 3.6 %down.1 = bf16[8,40,896]{2,1,0:T(8,128)(2,1)} custom-call(s32[1]{0:T(128)} %bitcast.e_ref.s_ref, bf16[8,320,128]{2,1,0:T(8,128)(2,1)} %copy-done.1, bf16[8,128,896]{2,1,0:T(8,128)(2,1)} %copy-done), custom_call_target="tpu_custom_call" | custom-call | flops 587202560 | bytes 4194304 | tf_op jit(solution)/shard_map/down/pallas_call | solution.py:286
  101.9 9.4 %all-to-all-start.2 = ((bf16[8,40,896]{2,1,0:T(8,128)(2,1)}), bf16[8,40,896]{2,1,0:T(8,128)(2,1)S(1)}, u32[]{:S(2)}, u32[]{:S(2)}) async-start(bf16[8,40,896]{2,1,0:T(8,128)(2,1)} %down.1), calls=%async_computation.2 | async-start | bytes 1146880 | tf_op jit(solution)/shard_map/all_to_all | solution.py:61
  111.3 0.2 copy.22.own_ref
  111.5 1.9 %collective-permute-start.30 = (bf16[256,576]{1,0:T(8,128)(2,1)S(1)}, bf16[256,576]{1,0:T(8,128)(2,1)S(1)}, u32[]{:S(2)}, u32[]{:S(2)}) collective-permute-start(bf16[256,576]{1,0:T(8,128)(2,1)S(1)} %copy.22.own_ref), channel_id=1, source_target_pairs={{0,1},{1,2},{2,3},{3,4},{4,5},{5,6},{6,7},{7,8},{8,9},{9,10},{10,1... | collective-permute-start | bytes 884744 | tf_op jit(solution)/shard_map/ppermute | solution.py:474
  113.5 2.1 %collective-permute-start.26 = (bf16[128,576]{1,0:T(8,128)(2,1)S(1)}, bf16[128,576]{1,0:T(8,128)(2,1)S(1)}, u32[]{:S(2)}, u32[]{:S(2)}) collective-permute-start(bf16[128,576]{1,0:T(8,128)(2,1)S(1)} %copy-done.6), channel_id=1, source_target_pairs={{0,64},{32,96},{64,0},{96,32},{128,192},{160,224},{192,128},{224,1... | collective-permute-start | bytes 442376 | tf_op jit(solution)/shard_map/ppermute | solution.py:38
  115.6 1.2 collective-permute-start.25
  116.8 0.8 collective-permute-start.24
  117.6 4.5 %collective-permute-done.26.refs_3_ = bf16[128,576]{1,0:T(8,128)(2,1)S(1)} collective-permute-done((bf16[128,576]{1,0:T(8,128)(2,1)S(1)}, bf16[128,576]{1,0:T(8,128)(2,1)S(1)}, u32[]{:S(2)}, u32[]{:S(2)}) %collective-permute-start.26) | collective-permute-done | bytes 147488 | tf_op jit(solution)/shard_map/ppermute | solution.py:38
  122.0 2.6 %collective-permute-done.25.refs_2_ = bf16[128,576]{1,0:T(8,128)(2,1)S(1)} collective-permute-done((bf16[128,576]{1,0:T(8,128)(2,1)S(1)}, bf16[128,576]{1,0:T(8,128)(2,1)S(1)}, u32[]{:S(2)}, u32[]{:S(2)}) %collective-permute-start.25) | collective-permute-done | bytes 147488 | tf_op jit(solution)/shard_map/ppermute | solution.py:38
  124.6 1.0 collective-permute-done.24.refs_1_
  125.6 0.8 copy-done.2
  126.5 2.2 %mix.1 = (f32[32,896]{1,0:T(8,128)}, bf16[32,896]{1,0:T(8,128)(2,1)}, bf16[32,896]{1,0:T(8,128)(2,1)}, bf16[32,896]{1,0:T(8,128)(2,1)}) custom-call(s32[1]{0:T(128)} %bitcast.e_ref.s_ref, f32[8,128]{1,0:T(8,128)} %get-tuple-element.41.slot_ref, f32[8,128]{1,0:T(8,128)} %get-tuple-element.42.share_ref, bf16[320,896]{1,0:T(8,128)(2,1)} %bitcast.12), custom_call_target="tpu_custom_call" | custom-call | flops 146800640 | bytes 1146880 | tf_op jit(solution)/shard_map/mix/pallas_call | solution.py:372
  128.8 1.7 %collective-permute-start.28 = (bf16[32,896]{1,0:T(8,128)(2,1)}, bf16[32,896]{1,0:T(8,128)(2,1)S(1)}, u32[]{:S(2)}, u32[]{:S(2)}) collective-permute-start(bf16[32,896]{1,0:T(8,128)(2,1)} %get-tuple-element.47), channel_id=1, source_target_pairs={{0,2},{1,3},{2,0},{3,1},{4,6},{5,7},{6,4},{7,5},{8,10},{9,11},{10,... | collective-permute-start | bytes 172040 | tf_op jit(solution)/shard_map/ppermute | solution.py:51
  130.5 1.6 %collective-permute-start.29 = (bf16[32,896]{1,0:T(8,128)(2,1)}, bf16[32,896]{1,0:T(8,128)(2,1)S(1)}, u32[]{:S(2)}, u32[]{:S(2)}) collective-permute-start(bf16[32,896]{1,0:T(8,128)(2,1)} %get-tuple-element.48), channel_id=1, source_target_pairs={{0,3},{1,2},{2,1},{3,0},{4,7},{5,6},{6,5},{7,4},{8,11},{9,10},{10,... | collective-permute-start | bytes 172040 | tf_op jit(solution)/shard_map/ppermute | solution.py:51
  132.1 0.7 copy-done.7
  132.9 4.1 %attend.2.refs_4_ = bf16[2048,512]{1,0:T(8,128)(2,1)} custom-call(s32[1]{0:T(128)} %bitcast.e_ref.s_ref, bf16[2048,576]{1,0:T(8,128)(2,1)} %bitcast.10, bf16[256,576]{1,0:T(8,128)(2,1)} %copy-done.7, bf16[256,576]{1,0:T(8,128)(2,1)} %copy-done.3, bf16[128,576]{1,0:T(8,128)(2,1)} %select_units.1.refs_0_, bf16[128,576]{1,0:T(8,128)(2,1)} %copy-done.29, ...), custom_call_target="tpu_custom_call" | custom-call | flops 1000000000 | bytes 2097152 | tf_op jit(solution)/shard_map/attend/pallas_call | solution.py:433
  137.1 0.8 broadcast_in_dim.2
  137.9 3.7 %all-to-all-start.3 = ((bf16[8,32,896]{2,1,0:T(8,128)(2,1)}), bf16[8,32,896]{2,1,0:T(8,128)(2,1)S(1)}, u32[]{:S(2)}, u32[]{:S(2)}) async-start(bf16[8,32,896]{2,1,0:T(8,128)(2,1)} %broadcast_in_dim.2), calls=%async_computation.3 | async-start | bytes 917504 | tf_op jit(solution)/shard_map/all_to_all | solution.py:67
  141.6 7.9 %attend.3 = bf16[2048,512]{1,0:T(8,128)(2,1)} custom-call(s32[1]{0:T(128)} %bitcast.e_ref.s_ref, bf16[2048,576]{1,0:T(8,128)(2,1)} %bitcast.11, bf16[256,576]{1,0:T(8,128)(2,1)} %copy-done.7, bf16[256,576]{1,0:T(8,128)(2,1)} %copy-done.3, bf16[128,576]{1,0:T(8,128)(2,1)} %select_units.1.refs_0_, ...), custom_call_target="tpu_custom_call", output_to_operand_aliasing={{}: (8, {})} | custom-call | flops 3000000000 | bytes 6291456 | tf_op jit(solution)/shard_map/attend/pallas_call | solution.py:433
  149.4 1.5 %all-to-all-done.3 = bf16[8,32,896]{2,1,0:T(8,128)(2,1)S(1)} async-done(((bf16[8,32,896]{2,1,0:T(8,128)(2,1)}), bf16[8,32,896]{2,1,0:T(8,128)(2,1)S(1)}, u32[]{:S(2)}, u32[]{:S(2)}) %all-to-all-start.3) | async-done | bytes 458784 | tf_op jit(solution)/shard_map/all_to_all | solution.py:67
  151.0 0.8 copy.26
  (99 shorter events, 0.5 us)
Async XLA Ops:
  3.7 6.5 %collective-permute-start.2 = (bf16[48,896]{1,0:T(8,128)(2,1)}, bf16[48,896]{1,0:T(8,128)(2,1)S(1)}, u32[]{:S(2)}, u32[]{:S(2)}) collective-permute-start(bf16[48,896]{1,0:T(8,128)(2,1)} %prep.1.m_ref), channel_id=1, source_target_pairs={{0,3},{1,2},{2,1},{3,0},{4,7},{5,6},{6,5},{7,4},{8,11},{9,10},{10,... | collective-permute-start | bytes 258056 | tf_op jit(solution)/shard_map/ppermute | solution.py:51
  6.2 6.8 %collective-permute-start.1 = (bf16[48,896]{1,0:T(8,128)(2,1)}, bf16[48,896]{1,0:T(8,128)(2,1)S(1)}, u32[]{:S(2)}, u32[]{:S(2)}) collective-permute-start(bf16[48,896]{1,0:T(8,128)(2,1)} %prep.1.m_ref), channel_id=1, source_target_pairs={{0,2},{1,3},{2,0},{3,1},{4,6},{5,7},{6,4},{7,5},{8,10},{9,11},{10,... | collective-permute-start | bytes 258056 | tf_op jit(solution)/shard_map/ppermute | solution.py:51
  6.8 6.2 %collective-permute-start = (bf16[48,896]{1,0:T(8,128)(2,1)}, bf16[48,896]{1,0:T(8,128)(2,1)S(1)}, u32[]{:S(2)}, u32[]{:S(2)}) collective-permute-start(bf16[48,896]{1,0:T(8,128)(2,1)} %prep.1.m_ref), channel_id=1, source_target_pairs={{0,1},{1,0},{2,3},{3,2},{4,5},{5,4},{6,7},{7,6},{8,9},{9,8},{10,11... | collective-permute-start | bytes 258056 | tf_op jit(solution)/shard_map/ppermute | solution.py:51
  10.2 2.8 %copy-start.31 = (bf16[48,896]{1,0:T(8,128)(2,1)}, bf16[48,896]{1,0:T(8,128)(2,1)S(1)}, u32[]{:S(2)}) copy-start(bf16[48,896]{1,0:T(8,128)(2,1)S(1)} %collective-permute-done.2.xc_ref) | copy-start | bytes 258052
  13.7 33.2 %all-to-all-start = ((bf16[8,128,896]{2,1,0:T(8,128)(2,1)}), bf16[8,128,896]{2,1,0:T(8,128)(2,1)S(1)}, u32[]{:S(2)}, u32[]{:S(2)}) async-start(bf16[8,128,896]{2,1,0:T(8,128)(2,1)} %cut_down.1), calls=%async_computation | async-start | bytes 3670016 | tf_op jit(solution)/shard_map/all_to_all | solution.py:67
  20.5 12.0 %collective-permute-start.3 = (bf16[40,1408]{1,0:T(8,128)(2,1)}, bf16[40,1408]{1,0:T(8,128)(2,1)S(1)}, u32[]{:S(2)}, u32[]{:S(2)}) collective-permute-start(bf16[40,1408]{1,0:T(8,128)(2,1)} %get-tuple-element.30), channel_id=1, source_target_pairs={{0,4},{1,5},{2,6},{3,7},{4,8},{5,9},{6,10},{7,11},{8,12},{9,13},{1... | collective-permute-start | bytes 337928 | tf_op jit(solution)/shard_map/ppermute | solution.py:55
  22.4 11.8 %collective-permute-start.4 = (bf16[40,1408]{1,0:T(8,128)(2,1)}, bf16[40,1408]{1,0:T(8,128)(2,1)S(1)}, u32[]{:S(2)}, u32[]{:S(2)}) collective-permute-start(bf16[40,1408]{1,0:T(8,128)(2,1)} %get-tuple-element.31), channel_id=1, source_target_pairs={{0,28},{1,29},{2,30},{3,31},{4,0},{5,1},{6,2},{7,3},{8,4},{9,5},{1... | collective-permute-start | bytes 337928 | tf_op jit(solution)/shard_map/ppermute | solution.py:55
  22.5 14.4 %collective-permute-start.5 = (bf16[40,1408]{1,0:T(8,128)(2,1)}, bf16[40,1408]{1,0:T(8,128)(2,1)S(1)}, u32[]{:S(2)}, u32[]{:S(2)}) collective-permute-start(bf16[40,1408]{1,0:T(8,128)(2,1)} %get-tuple-element.32), channel_id=1, source_target_pairs={{0,8},{1,9},{2,10},{3,11},{4,12},{5,13},{6,14},{7,15},{8,16},{9,17... | collective-permute-start | bytes 337928 | tf_op jit(solution)/shard_map/ppermute | solution.py:55
  29.1 11.9 %collective-permute-start.6 = (bf16[40,1408]{1,0:T(8,128)(2,1)}, bf16[40,1408]{1,0:T(8,128)(2,1)S(1)}, u32[]{:S(2)}, u32[]{:S(2)}) collective-permute-start(bf16[40,1408]{1,0:T(8,128)(2,1)} %get-tuple-element.33), channel_id=1, source_target_pairs={{0,24},{1,25},{2,26},{3,27},{4,28},{5,29},{6,30},{7,31},{8,0},{9,1... | collective-permute-start | bytes 337928 | tf_op jit(solution)/shard_map/ppermute | solution.py:55
  29.1 14.6 %collective-permute-start.7 = (bf16[40,1408]{1,0:T(8,128)(2,1)}, bf16[40,1408]{1,0:T(8,128)(2,1)S(1)}, u32[]{:S(2)}, u32[]{:S(2)}) collective-permute-start(bf16[40,1408]{1,0:T(8,128)(2,1)} %get-tuple-element.34), channel_id=1, source_target_pairs={{0,12},{1,13},{2,14},{3,15},{4,16},{5,17},{6,18},{7,19},{8,20},{9,... | collective-permute-start | bytes 337928 | tf_op jit(solution)/shard_map/ppermute | solution.py:55
  32.5 52.4 %copy-start.8 = (bf16[40,1408]{1,0:T(8,128)(2,1)}, bf16[40,1408]{1,0:T(8,128)(2,1)S(1)}, u32[]{:S(2)}) copy-start(bf16[40,1408]{1,0:T(8,128)(2,1)S(1)} %collective-permute-done.3.refs_1_) | copy-start | bytes 337924
  32.5 14.3 %collective-permute-start.8 = (bf16[40,1408]{1,0:T(8,128)(2,1)}, bf16[40,1408]{1,0:T(8,128)(2,1)S(1)}, u32[]{:S(2)}, u32[]{:S(2)}) collective-permute-start(bf16[40,1408]{1,0:T(8,128)(2,1)} %get-tuple-element.35), channel_id=1, source_target_pairs={{0,20},{1,21},{2,22},{3,23},{4,24},{5,25},{6,26},{7,27},{8,28},{9,... | collective-permute-start | bytes 337928 | tf_op jit(solution)/shard_map/ppermute | solution.py:55
  34.3 50.7 %copy-start.9 = (bf16[40,1408]{1,0:T(8,128)(2,1)}, bf16[40,1408]{1,0:T(8,128)(2,1)S(1)}, u32[]{:S(2)}) copy-start(bf16[40,1408]{1,0:T(8,128)(2,1)S(1)} %collective-permute-done.4.refs_2_) | copy-start | bytes 337924
  34.3 12.5 %collective-permute-start.9 = (bf16[40,1408]{1,0:T(8,128)(2,1)}, bf16[40,1408]{1,0:T(8,128)(2,1)S(1)}, u32[]{:S(2)}, u32[]{:S(2)}) collective-permute-start(bf16[40,1408]{1,0:T(8,128)(2,1)} %get-tuple-element.36), channel_id=1, source_target_pairs={{0,16},{1,17},{2,18},{3,19},{4,20},{5,21},{6,22},{7,23},{8,24},{9,... | collective-permute-start | bytes 337928 | tf_op jit(solution)/shard_map/ppermute | solution.py:55
  36.9 48.0 %copy-start.10 = (bf16[40,1408]{1,0:T(8,128)(2,1)}, bf16[40,1408]{1,0:T(8,128)(2,1)S(1)}, u32[]{:S(2)}) copy-start(bf16[40,1408]{1,0:T(8,128)(2,1)S(1)} %collective-permute-done.5.refs_3_) | copy-start | bytes 337924
  37.0 42.1 %copy-start.4 = (bf16[160,896]{1,0:T(8,128)(2,1)}, bf16[160,896]{1,0:T(8,128)(2,1)S(1)}, u32[]{:S(2)}) copy-start(bf16[160,896]{1,0:T(8,128)(2,1)S(1)} %pad_maximum_fusion.refs_0_) | copy-start | bytes 860164
  37.0 14.8 %collective-permute-start.14 = (bf16[160,896]{1,0:T(8,128)(2,1)S(1)}, bf16[160,896]{1,0:T(8,128)(2,1)S(1)}, u32[]{:S(2)}, u32[]{:S(2)}) collective-permute-start(bf16[160,896]{1,0:T(8,128)(2,1)S(1)} %pad_maximum_fusion.refs_0_), channel_id=1, source_target_pairs={{0,128},{32,160},{64,192},{96,224},{128,0},{160,32},{192,64},{224,... | collective-permute-start | bytes 860168 | tf_op jit(solution)/shard_map/ppermute | solution.py:43
  41.0 43.9 %copy-start.11 = (bf16[40,1408]{1,0:T(8,128)(2,1)}, bf16[40,1408]{1,0:T(8,128)(2,1)S(1)}, u32[]{:S(2)}) copy-start(bf16[40,1408]{1,0:T(8,128)(2,1)S(1)} %collective-permute-done.6.refs_4_) | copy-start | bytes 337924
  41.0 15.5 %collective-permute-start.12 = (bf16[160,896]{1,0:T(8,128)(2,1)S(1)}, bf16[160,896]{1,0:T(8,128)(2,1)}, u32[]{:S(2)}, u32[]{:S(2)}) collective-permute-start(bf16[160,896]{1,0:T(8,128)(2,1)S(1)} %pad_maximum_fusion.refs_0_), channel_id=1, source_target_pairs={{0,96},{32,0},{64,32},{96,64},{128,224},{160,128},{192,160},{224,1... | collective-permute-start | bytes 860168 | tf_op jit(solution)/shard_map/ppermute | solution.py:38
  43.7 41.2 %copy-start.12 = (bf16[40,1408]{1,0:T(8,128)(2,1)}, bf16[40,1408]{1,0:T(8,128)(2,1)S(1)}, u32[]{:S(2)}) copy-start(bf16[40,1408]{1,0:T(8,128)(2,1)S(1)} %collective-permute-done.7.refs_5_) | copy-start | bytes 337924
  43.8 8.0 %collective-permute-start.10 = (bf16[160,896]{1,0:T(8,128)(2,1)S(1)}, bf16[160,896]{1,0:T(8,128)(2,1)}, u32[]{:S(2)}, u32[]{:S(2)}) collective-permute-start(bf16[160,896]{1,0:T(8,128)(2,1)S(1)} %pad_maximum_fusion.refs_0_), channel_id=1, source_target_pairs={{0,32},{32,64},{64,96},{96,0},{128,160},{160,192},{192,224},{224,1... | collective-permute-start | bytes 860168 | tf_op jit(solution)/shard_map/ppermute | solution.py:38
  46.8 38.2 %copy-start.13 = (bf16[40,1408]{1,0:T(8,128)(2,1)}, bf16[40,1408]{1,0:T(8,128)(2,1)S(1)}, u32[]{:S(2)}) copy-start(bf16[40,1408]{1,0:T(8,128)(2,1)S(1)} %collective-permute-done.8.refs_6_) | copy-start | bytes 337924
  46.8 38.2 %copy-start.14 = (bf16[40,1408]{1,0:T(8,128)(2,1)}, bf16[40,1408]{1,0:T(8,128)(2,1)S(1)}, u32[]{:S(2)}) copy-start(bf16[40,1408]{1,0:T(8,128)(2,1)S(1)} %collective-permute-done.9.refs_7_) | copy-start | bytes 337924
  46.9 32.2 %copy-start.5 = (bf16[160,896]{1,0:T(8,128)(2,1)}, bf16[160,896]{1,0:T(8,128)(2,1)S(1)}, u32[]{:S(2)}) copy-start(bf16[160,896]{1,0:T(8,128)(2,1)S(1)} %pad_maximum_fusion.1.refs_1_) | copy-start | bytes 860164
  46.9 38.1 %copy-start = (bf16[8,128,896]{2,1,0:T(8,128)(2,1)}, bf16[8,128,896]{2,1,0:T(8,128)(2,1)S(1)}, u32[]{:S(2)}) copy-start(bf16[8,128,896]{2,1,0:T(8,128)(2,1)S(1)} %all-to-all-done.w_ref) | copy-start | bytes 5505028
  46.9 10.5 %collective-permute-start.13 = (bf16[160,896]{1,0:T(8,128)(2,1)S(1)}, bf16[160,896]{1,0:T(8,128)(2,1)S(1)}, u32[]{:S(2)}, u32[]{:S(2)}) collective-permute-start(bf16[160,896]{1,0:T(8,128)(2,1)S(1)} %pad_maximum_fusion.1.refs_1_), channel_id=1, source_target_pairs={{0,96},{32,0},{64,32},{96,64},{128,224},{160,128},{192,160},{224,1... | collective-permute-start | bytes 860168 | tf_op jit(solution)/shard_map/ppermute | solution.py:38
  51.8 10.8 %collective-permute-start.16 = (bf16[160,896]{1,0:T(8,128)(2,1)}, bf16[160,896]{1,0:T(8,128)(2,1)S(1)}, u32[]{:S(2)}, u32[]{:S(2)}) collective-permute-start(bf16[160,896]{1,0:T(8,128)(2,1)} %collective-permute-done.10.refs_2_), channel_id=1, source_target_pairs={{0,32},{32,64},{64,96},{96,0},{128,160},{160,192},{192,224},{224,1... | collective-permute-start | bytes 860168 | tf_op jit(solution)/shard_map/ppermute | solution.py:38
  51.8 27.2 %copy-start.16 = (bf16[160,896]{1,0:T(8,128)(2,1)}, bf16[160,896]{1,0:T(8,128)(2,1)S(1)}, u32[]{:S(2)}) copy-start(bf16[160,896]{1,0:T(8,128)(2,1)S(1)} %collective-permute-done.14.refs_6_) | copy-start | bytes 860164
  51.8 12.3 %collective-permute-start.20 = (bf16[160,896]{1,0:T(8,128)(2,1)S(1)}, bf16[160,896]{1,0:T(8,128)(2,1)S(1)}, u32[]{:S(2)}, u32[]{:S(2)}) collective-permute-start(bf16[160,896]{1,0:T(8,128)(2,1)S(1)} %collective-permute-done.14.refs_6_), channel_id=1, source_target_pairs={{0,96},{32,0},{64,32},{96,64},{128,224},{160,128},{192,160},{224,1... | collective-permute-start | bytes 860168 | tf_op jit(solution)/shard_map/ppermute | solution.py:38
  55.0 9.8 %collective-permute-start.15 = (bf16[160,896]{1,0:T(8,128)(2,1)S(1)}, bf16[160,896]{1,0:T(8,128)(2,1)S(1)}, u32[]{:S(2)}, u32[]{:S(2)}) collective-permute-start(bf16[160,896]{1,0:T(8,128)(2,1)S(1)} %pad_maximum_fusion.1.refs_1_), channel_id=1, source_target_pairs={{0,128},{32,160},{64,192},{96,224},{128,0},{160,32},{192,64},{224,... | collective-permute-start | bytes 860168 | tf_op jit(solution)/shard_map/ppermute | solution.py:43
  56.5 10.9 %collective-permute-start.18 = (bf16[160,896]{1,0:T(8,128)(2,1)S(1)}, bf16[160,896]{1,0:T(8,128)(2,1)S(1)}, u32[]{:S(2)}, u32[]{:S(2)}) collective-permute-start(bf16[160,896]{1,0:T(8,128)(2,1)S(1)} %collective-permute-done.14.refs_6_), channel_id=1, source_target_pairs={{0,32},{32,64},{64,96},{96,0},{128,160},{160,192},{192,224},{224,1... | collective-permute-start | bytes 860168 | tf_op jit(solution)/shard_map/ppermute | solution.py:38
  57.4 21.6 %copy-start.17 = (bf16[160,896]{1,0:T(8,128)(2,1)}, bf16[160,896]{1,0:T(8,128)(2,1)S(1)}, u32[]{:S(2)}) copy-start(bf16[160,896]{1,0:T(8,128)(2,1)S(1)} %collective-permute-done.13.refs_5_) | copy-start | bytes 860164
  57.4 12.3 %collective-permute-start.17 = (bf16[160,896]{1,0:T(8,128)(2,1)S(1)}, bf16[160,896]{1,0:T(8,128)(2,1)S(1)}, u32[]{:S(2)}, u32[]{:S(2)}) collective-permute-start(bf16[160,896]{1,0:T(8,128)(2,1)S(1)} %collective-permute-done.13.refs_5_), channel_id=1, source_target_pairs={{0,96},{32,0},{64,32},{96,64},{128,224},{160,128},{192,160},{224,1... | collective-permute-start | bytes 860168 | tf_op jit(solution)/shard_map/ppermute | solution.py:38
  62.6 16.5 %copy-start.18 = (bf16[160,896]{1,0:T(8,128)(2,1)}, bf16[160,896]{1,0:T(8,128)(2,1)S(1)}, u32[]{:S(2)}) copy-start(bf16[160,896]{1,0:T(8,128)(2,1)S(1)} %collective-permute-done.16.refs_8_) | copy-start | bytes 860164
  62.6 8.6 %collective-permute-start.22 = (bf16[160,896]{1,0:T(8,128)(2,1)S(1)}, bf16[160,896]{1,0:T(8,128)(2,1)S(1)}, u32[]{:S(2)}, u32[]{:S(2)}) collective-permute-start(bf16[160,896]{1,0:T(8,128)(2,1)S(1)} %collective-permute-done.16.refs_8_), channel_id=1, source_target_pairs={{0,128},{32,160},{64,192},{96,224},{128,0},{160,32},{192,64},{224,... | collective-permute-start | bytes 860168 | tf_op jit(solution)/shard_map/ppermute | solution.py:43
  64.1 11.0 %copy-start.19 = (bf16[160,896]{1,0:T(8,128)(2,1)}, bf16[160,896]{1,0:T(8,128)(2,1)S(1)}, u32[]{:S(2)}) copy-start(bf16[160,896]{1,0:T(8,128)(2,1)S(1)} %collective-permute-done.20.refs_12_) | copy-start | bytes 860164
  64.1 11.0 %collective-permute-start.11 = (bf16[160,896]{1,0:T(8,128)(2,1)S(1)}, bf16[160,896]{1,0:T(8,128)(2,1)S(1)}, u32[]{:S(2)}, u32[]{:S(2)}) collective-permute-start(bf16[160,896]{1,0:T(8,128)(2,1)S(1)} %pad_maximum_fusion.1.refs_1_), channel_id=1, source_target_pairs={{0,32},{32,64},{64,96},{96,0},{128,160},{160,192},{192,224},{224,1... | collective-permute-start | bytes 860168 | tf_op jit(solution)/shard_map/ppermute | solution.py:38
  64.9 10.3 %copy-start.20 = (bf16[160,896]{1,0:T(8,128)(2,1)}, bf16[160,896]{1,0:T(8,128)(2,1)S(1)}, u32[]{:S(2)}) copy-start(bf16[160,896]{1,0:T(8,128)(2,1)S(1)} %collective-permute-done.15.refs_7_) | copy-start | bytes 860164
  64.9 10.3 %collective-permute-start.21 = (bf16[160,896]{1,0:T(8,128)(2,1)S(1)}, bf16[160,896]{1,0:T(8,128)(2,1)S(1)}, u32[]{:S(2)}, u32[]{:S(2)}) collective-permute-start(bf16[160,896]{1,0:T(8,128)(2,1)S(1)} %collective-permute-done.15.refs_7_), channel_id=1, source_target_pairs={{0,96},{32,0},{64,32},{96,64},{128,224},{160,128},{192,160},{224,1... | collective-permute-start | bytes 860168 | tf_op jit(solution)/shard_map/ppermute | solution.py:38
  67.4 10.9 %copy-start.21 = (bf16[160,896]{1,0:T(8,128)(2,1)}, bf16[160,896]{1,0:T(8,128)(2,1)S(1)}, u32[]{:S(2)}) copy-start(bf16[160,896]{1,0:T(8,128)(2,1)S(1)} %collective-permute-done.18.refs_10_) | copy-start | bytes 860164
  67.4 10.9 %collective-permute-start.19 = (bf16[160,896]{1,0:T(8,128)(2,1)S(1)}, bf16[160,896]{1,0:T(8,128)(2,1)S(1)}, u32[]{:S(2)}, u32[]{:S(2)}) collective-permute-start(bf16[160,896]{1,0:T(8,128)(2,1)S(1)} %collective-permute-done.15.refs_7_), channel_id=1, source_target_pairs={{0,32},{32,64},{64,96},{96,0},{128,160},{160,192},{192,224},{224,1... | collective-permute-start | bytes 860168 | tf_op jit(solution)/shard_map/ppermute | solution.py:38
  69.7 8.6 %copy-start.22 = (bf16[160,896]{1,0:T(8,128)(2,1)}, bf16[160,896]{1,0:T(8,128)(2,1)S(1)}, u32[]{:S(2)}) copy-start(bf16[160,896]{1,0:T(8,128)(2,1)S(1)} %collective-permute-done.17.refs_9_) | copy-start | bytes 860164
  69.7 9.3 %collective-permute-start.23 = (bf16[160,896]{1,0:T(8,128)(2,1)S(1)}, bf16[160,896]{1,0:T(8,128)(2,1)}, u32[]{:S(2)}, u32[]{:S(2)}) collective-permute-start(bf16[160,896]{1,0:T(8,128)(2,1)S(1)} %collective-permute-done.17.refs_9_), channel_id=1, source_target_pairs={{0,128},{32,160},{64,192},{96,224},{128,0},{160,32},{192,64},{224,... | collective-permute-start | bytes 860168 | tf_op jit(solution)/shard_map/ppermute | solution.py:43
  71.2 7.1 %copy-start.23 = (bf16[160,896]{1,0:T(8,128)(2,1)}, bf16[160,896]{1,0:T(8,128)(2,1)S(1)}, u32[]{:S(2)}) copy-start(bf16[160,896]{1,0:T(8,128)(2,1)S(1)} %collective-permute-done.22.refs_14_) | copy-start | bytes 860164
  75.1 3.2 %copy-start.24 = (bf16[160,896]{1,0:T(8,128)(2,1)}, bf16[160,896]{1,0:T(8,128)(2,1)S(1)}, u32[]{:S(2)}) copy-start(bf16[160,896]{1,0:T(8,128)(2,1)S(1)} %collective-permute-done.11.refs_3_) | copy-start | bytes 860164
  75.1 3.2 %copy-start.25 = (bf16[160,896]{1,0:T(8,128)(2,1)}, bf16[160,896]{1,0:T(8,128)(2,1)S(1)}, u32[]{:S(2)}) copy-start(bf16[160,896]{1,0:T(8,128)(2,1)S(1)} %collective-permute-done.21.refs_13_) | copy-start | bytes 860164
  85.0 12.4 %all-to-all-start.1 = ((bf16[8,320,128]{2,1,0:T(8,128)(2,1)}), bf16[8,320,128]{2,1,0:T(8,128)(2,1)S(1)}, u32[]{:S(2)}, u32[]{:S(2)}) async-start(bf16[8,320,128]{2,1,0:T(8,128)(2,1)} %add_blocks.1), calls=%async_computation.1 | async-start | bytes 1310720 | tf_op jit(solution)/shard_map/all_to_all | solution.py:67
  97.4 0.9 copy-start.1
  98.3 13.0 %copy-start.15 = (bf16[256,576]{0,1:T(8,128)(2,1)S(1)}, bf16[256,576]{0,1:T(8,128)(2,1)}, u32[]{:S(2)}) copy-start(bf16[256,576]{0,1:T(8,128)(2,1)} %param.11) | copy-start | bytes 884740
  98.3 15.2 %copy-start.6 = (bf16[128,576]{1,0:T(8,128)(2,1)S(1)}, bf16[128,576]{1,0:T(8,128)(2,1)}, u32[]{:S(2)}) copy-start(bf16[128,576]{1,0:T(8,128)(2,1)} %select_units.1.refs_0_) | copy-start | bytes 442372
  101.9 23.8 %all-to-all-start.2 = ((bf16[8,40,896]{2,1,0:T(8,128)(2,1)}), bf16[8,40,896]{2,1,0:T(8,128)(2,1)S(1)}, u32[]{:S(2)}, u32[]{:S(2)}) async-start(bf16[8,40,896]{2,1,0:T(8,128)(2,1)} %down.1), calls=%async_computation.2 | async-start | bytes 1146880 | tf_op jit(solution)/shard_map/all_to_all | solution.py:61
  111.5 20.6 %copy-start.3 = (bf16[256,576]{1,0:T(8,128)(2,1)}, bf16[256,576]{1,0:T(8,128)(2,1)S(1)}, u32[]{:S(2)}) copy-start(bf16[256,576]{1,0:T(8,128)(2,1)S(1)} %copy.22.own_ref) | copy-start | bytes 884740
  111.5 20.6 %collective-permute-start.30 = (bf16[256,576]{1,0:T(8,128)(2,1)S(1)}, bf16[256,576]{1,0:T(8,128)(2,1)S(1)}, u32[]{:S(2)}, u32[]{:S(2)}) collective-permute-start(bf16[256,576]{1,0:T(8,128)(2,1)S(1)} %copy.22.own_ref), channel_id=1, source_target_pairs={{0,1},{1,2},{2,3},{3,4},{4,5},{5,6},{6,7},{7,8},{8,9},{9,10},{10,1... | collective-permute-start | bytes 884744 | tf_op jit(solution)/shard_map/ppermute | solution.py:474
  113.5 8.6 %collective-permute-start.26 = (bf16[128,576]{1,0:T(8,128)(2,1)S(1)}, bf16[128,576]{1,0:T(8,128)(2,1)S(1)}, u32[]{:S(2)}, u32[]{:S(2)}) collective-permute-start(bf16[128,576]{1,0:T(8,128)(2,1)S(1)} %copy-done.6), channel_id=1, source_target_pairs={{0,64},{32,96},{64,0},{96,32},{128,192},{160,224},{192,128},{224,1... | collective-permute-start | bytes 442376 | tf_op jit(solution)/shard_map/ppermute | solution.py:38
  115.6 9.1 %collective-permute-start.25 = (bf16[128,576]{1,0:T(8,128)(2,1)S(1)}, bf16[128,576]{1,0:T(8,128)(2,1)S(1)}, u32[]{:S(2)}, u32[]{:S(2)}) collective-permute-start(bf16[128,576]{1,0:T(8,128)(2,1)S(1)} %copy-done.6), channel_id=1, source_target_pairs={{0,96},{32,0},{64,32},{96,64},{128,224},{160,128},{192,160},{224,1... | collective-permute-start | bytes 442376 | tf_op jit(solution)/shard_map/ppermute | solution.py:38
  116.8 8.9 %collective-permute-start.24 = (bf16[128,576]{1,0:T(8,128)(2,1)S(1)}, bf16[128,576]{1,0:T(8,128)(2,1)S(1)}, u32[]{:S(2)}, u32[]{:S(2)}) collective-permute-start(bf16[128,576]{1,0:T(8,128)(2,1)S(1)} %copy-done.6), channel_id=1, source_target_pairs={{0,32},{32,64},{64,96},{96,0},{128,160},{160,192},{192,224},{224,1... | collective-permute-start | bytes 442376 | tf_op jit(solution)/shard_map/ppermute | solution.py:38
  122.0 10.1 %copy-start.27 = (bf16[128,576]{1,0:T(8,128)(2,1)}, bf16[128,576]{1,0:T(8,128)(2,1)S(1)}, u32[]{:S(2)}) copy-start(bf16[128,576]{1,0:T(8,128)(2,1)S(1)} %collective-permute-done.26.refs_3_) | copy-start | bytes 442372
  124.6 7.5 %copy-start.28 = (bf16[128,576]{1,0:T(8,128)(2,1)}, bf16[128,576]{1,0:T(8,128)(2,1)S(1)}, u32[]{:S(2)}) copy-start(bf16[128,576]{1,0:T(8,128)(2,1)S(1)} %collective-permute-done.25.refs_2_) | copy-start | bytes 442372
  125.6 6.5 %copy-start.29 = (bf16[128,576]{1,0:T(8,128)(2,1)}, bf16[128,576]{1,0:T(8,128)(2,1)S(1)}, u32[]{:S(2)}) copy-start(bf16[128,576]{1,0:T(8,128)(2,1)S(1)} %collective-permute-done.24.refs_1_) | copy-start | bytes 442372
  128.7 8.3 %collective-permute-start.27 = (bf16[32,896]{1,0:T(8,128)(2,1)}, bf16[32,896]{1,0:T(8,128)(2,1)S(1)}, u32[]{:S(2)}, u32[]{:S(2)}) collective-permute-start(bf16[32,896]{1,0:T(8,128)(2,1)} %get-tuple-element.46), channel_id=1, source_target_pairs={{0,1},{1,0},{2,3},{3,2},{4,5},{5,4},{6,7},{7,6},{8,9},{9,8},{10,11... | collective-permute-start | bytes 172040 | tf_op jit(solution)/shard_map/ppermute | solution.py:51
  128.8 8.2 %collective-permute-start.28 = (bf16[32,896]{1,0:T(8,128)(2,1)}, bf16[32,896]{1,0:T(8,128)(2,1)S(1)}, u32[]{:S(2)}, u32[]{:S(2)}) collective-permute-start(bf16[32,896]{1,0:T(8,128)(2,1)} %get-tuple-element.47), channel_id=1, source_target_pairs={{0,2},{1,3},{2,0},{3,1},{4,6},{5,7},{6,4},{7,5},{8,10},{9,11},{10,... | collective-permute-start | bytes 172040 | tf_op jit(solution)/shard_map/ppermute | solution.py:51
  130.5 6.5 %copy-start.30 = (f32[32,896]{1,0:T(8,128)S(1)}, f32[32,896]{1,0:T(8,128)}, u32[]{:S(2)}) copy-start(f32[32,896]{1,0:T(8,128)} %get-tuple-element.55) | copy-start | bytes 344068
  130.5 6.5 %collective-permute-start.29 = (bf16[32,896]{1,0:T(8,128)(2,1)}, bf16[32,896]{1,0:T(8,128)(2,1)S(1)}, u32[]{:S(2)}, u32[]{:S(2)}) collective-permute-start(bf16[32,896]{1,0:T(8,128)(2,1)} %get-tuple-element.48), channel_id=1, source_target_pairs={{0,3},{1,2},{2,1},{3,0},{4,7},{5,6},{6,5},{7,4},{8,11},{9,10},{10,... | collective-permute-start | bytes 172040 | tf_op jit(solution)/shard_map/ppermute | solution.py:51
  137.9 13.1 %all-to-all-start.3 = ((bf16[8,32,896]{2,1,0:T(8,128)(2,1)}), bf16[8,32,896]{2,1,0:T(8,128)(2,1)S(1)}, u32[]{:S(2)}, u32[]{:S(2)}) async-start(bf16[8,32,896]{2,1,0:T(8,128)(2,1)} %broadcast_in_dim.2), calls=%async_computation.3 | async-start | bytes 917504 | tf_op jit(solution)/shard_map/all_to_all | solution.py:67
  (5 other events, 3.6 us)
